TPU v7x, 128 devices: a whole 4x4x4 slice. The times are simulated.
128 devices in a mesh: freq: 16 (over z, x_hi, core), src: 8 (over y, x_lo).
Axes of the slice: x: 4 (x_hi: 2, x_lo: 2; x = x_hi * 2 + x_lo), y: 4, z: 4, core: 2. Of those that a mesh axis runs over, the one named last changes fastest.
Arguments:
- reflection: bfloat16 [2, 16, 5120, 5120], P(None, 'freq', None, 'src'), may hold values from -0.15625 to 0.15625
- focus_start: bfloat16 [256, 5120, 128], P('freq', 'src'), may hold values from -6 to 6
- onsets: int32 [5120, 128], P('src'), may hold values from 16 to 127
Outputs:
- focus_minus: bfloat16 [256, 5120, 128], P('freq', 'src')
- focus_plus: bfloat16 [256, 5120, 128], P('freq', 'src')
All inputs are finite; a program needn't handle non-finite values.
Results may differ from a plain program's by a relative error of at most 0.033.
Values may be sent and summed in bfloat16 or wider, within the bound.
No kernel may reach another device: no remote copies, remote signals or barrier semaphores. Data moves between devices by JAX's collectives and lax.ppermute only.
A program may use at most 128 MiB of HBM per device.

v0:
```python
import math

import jax
import jax.numpy as jnp
from jax import lax
from jax.sharding import PartitionSpec as P

NT = 256


TWO_PI = 2.0 * math.pi


def phase_tables(freq_rows, time_rows, time_count):
    phases = (freq_rows[:, None] + 1) * time_rows[None, :] % time_count
    angles = phases.astype(jnp.float32) * (TWO_PI / time_count)
    return (jnp.cos(angles).astype(jnp.bfloat16), jnp.sin(angles).astype(jnp.bfloat16))


def to_freq(signal, freq_rows, time_rows, time_count):
    cosines, sines = phase_tables(freq_rows, time_rows, time_count)
    flattened = signal.reshape(signal.shape[0], -1)
    real_part = jnp.dot(cosines, flattened, preferred_element_type=jnp.float32)
    imag_part = -jnp.dot(sines, flattened, preferred_element_type=jnp.float32)
    stacked = jnp.stack([real_part, imag_part], axis=1)
    return stacked.reshape(freq_rows.shape[0], 2, signal.shape[1], signal.shape[2])


def to_time(spectra, freq_rows, time_rows, time_count):
    cosines, sines = phase_tables(freq_rows, time_rows, time_count)
    real_part = jnp.einsum(
        "ft,rfc->trc", cosines, spectra[:, :, 0], preferred_element_type=jnp.float32
    )
    imag_part = jnp.einsum(
        "ft,rfc->trc", sines, spectra[:, :, 1], preferred_element_type=jnp.float32
    )
    return 2.0 / time_count * (real_part - imag_part)


def windowed(signal, time_rows, onset_rows, time_count):
    distance = jnp.minimum(time_rows, time_count - time_rows)
    kept_mask = distance[:, None, None] < onset_rows[None]
    return jnp.where(kept_mask, signal, jnp.zeros_like(signal))


def local(reflection, focus_start, onsets):
    freq_size = lax.axis_size("freq")
    freq_dev = reflection.shape[1]
    time_count = NT

    def source_sum(spectra, conj_sign):
        products = jnp.einsum(
            "pjrs,jqsc->rjpqc", reflection, spectra, preferred_element_type=jnp.float32
        )
        real_part = products[:, :, 0, 0] - conj_sign * products[:, :, 1, 1]
        imag_part = products[:, :, 0, 1] + conj_sign * products[:, :, 1, 0]
        return lax.psum_scatter(
            jnp.stack([real_part, imag_part], axis=2).astype(jnp.bfloat16),
            "src",
            scatter_dimension=0,
            tiled=True,
        )

    time_dev = time_count // freq_size
    own_times = lax.axis_index("freq") * time_dev + jnp.arange(time_dev, dtype=jnp.int32)

    def spectra_of(signal):
        freq_rows = jnp.arange(lax.axis_size("freq") * freq_dev, dtype=jnp.int32)
        return lax.psum_scatter(
            to_freq(signal, freq_rows, own_times, time_count).astype(jnp.bfloat16),
            "freq",
            scatter_dimension=0,
            tiled=True,
        )

    def field_of(spectra):
        shard_piece = lax.all_gather(spectra, "freq", axis=1, tiled=True)
        freq_rows = jnp.arange(shard_piece.shape[1], dtype=jnp.int32)
        return to_time(shard_piece, freq_rows, own_times, time_count)

    minus_field = windowed(
        field_of(source_sum(spectra_of(focus_start), 1.0)), own_times, onsets, time_count
    ).astype(jnp.bfloat16)
    update = windowed(
        field_of(source_sum(spectra_of(minus_field), -1.0)), own_times, onsets, time_count
    )
    plus_field = (focus_start.astype(jnp.float32) + update).astype(jnp.bfloat16)
    return (minus_field, plus_field)


def solution(mesh):
    placed = (P(None, "freq", None, "src"), P("freq", "src", None), P("src", None))
    return jax.shard_map(
        local,
        mesh=mesh,
        in_specs=placed,
        out_specs=(P("freq", "src", None), P("freq", "src", None)),
        check_vma=False,
    )
```

profile of v0, /device:TPU:1, one launch (start us, length us, event | category | flops | bytes accessed | tf_op | source)
XLA Modules:
  0.0 530.2 jit_solution(11250732527100863458)
XLA Ops:
  7.2 3.8 convert_bitcast_fusion.1
  11.0 5.8 %fusion.44 = bf16[2,8,640,128]{3,1,2,0:T(8,128)(2,1)S(1)} fusion(bf16[2,8,640,128]{3,2,1,0:T(8,128)(2,1)S(1)} %bitcast.166, s32[16]{0:T(128)S(1)} %get-tuple-element.13, s32[16]{0:T(128)S(1)} %get-tuple-element.12), kind=kOutput, calls=%fused_computation.56 | convolution fusion | flops 44568320 | bytes 5243008 | tf_op jit(solution)/shard_map/dot_general | solution.py:24
  17.3 1.7 copy.44
  19.5 3.7 copy.45
  23.7 86.7 %reduce-scatter.9.cloned.1.call-done = bf16[1,2,640,128]{3,2,1,0:T(8,128)(2,1)} async-done(((bf16[16,2,640,128]{3,2,1,0:T(8,128)(2,1)}), bf16[1,2,640,128]{3,2,1,0:T(8,128)(2,1)}) %reduce-scatter.9.cloned.1.call-update) | async-done | bytes 327696 | tf_op jit(solution)/shard_map/reduce_scatter | solution.py:69
  110.4 13.1 %fusion.6 = f32[5120,1,2,2,128]{0,4,2,3,1:T(8,128)} fusion(bf16[2,1,5120,640]{3,2,1,0:T(8,128)(2,1)} %param.3, bf16[1,2,640,128]{3,2,1,0:T(8,128)(2,1)} %reduce-scatter.9.cloned.1.call-done), kind=kOutput, calls=%fused_computation.8 | convolution fusion | flops 3355443200 | bytes 23920640 | tf_op jit(solution)/shard_map/pjrs,jqsc->rjpqc/dot_general | solution.py:52
  123.6 2.8 fusion.48
  126.4 2.8 fusion.47
  129.4 2.6 copy.81
  132.1 62.1 %reduce-scatter.13.cloned.1.call-done = bf16[640,256]{1,0:T(8,128)(2,1)} async-done(((bf16[5120,256]{1,0:T(8,128)(2,1)}), bf16[640,256]{1,0:T(8,128)(2,1)}) %reduce-scatter.13.cloned.1.call-update) | async-done | bytes 327696
  194.2 1.2 copy.82
  196.5 60.7 %all-gather.3.cloned.1.call-done = bf16[640,16,2,128]{3,0,2,1:T(8,128)(2,1)} async-done(((bf16[640,1,2,128]{3,0,2,1:T(8,128)(2,1)}), bf16[640,16,2,128]{3,0,2,1:T(8,128)(2,1)}) %all-gather.3.cloned.1.call-update) | async-done | bytes 5242896 | tf_op jit(solution)/shard_map/all_gather | solution.py:77
  257.3 3.1 fusion.96
  260.4 1.7 fusion.33
  262.2 2.3 fusion.12
  264.5 1.3 convert_bitcast_fusion
  265.8 1.3 fusion.41
  267.6 1.7 copy.56
  269.8 3.7 copy.57
  273.8 81.0 %reduce-scatter.11.cloned.1.call-done = bf16[1,2,640,128]{3,2,1,0:T(8,128)(2,1)} async-done(((bf16[16,2,640,128]{3,2,1,0:T(8,128)(2,1)}), bf16[1,2,640,128]{3,2,1,0:T(8,128)(2,1)}) %reduce-scatter.11.cloned.1.call-update) | async-done | bytes 327696 | tf_op jit(solution)/shard_map/reduce_scatter | solution.py:69
  354.8 13.1 %fusion.9 = f32[5120,1,2,2,128]{0,4,2,3,1:T(8,128)} fusion(bf16[2,1,5120,640]{3,2,1,0:T(8,128)(2,1)} %param.3, bf16[1,2,640,128]{3,2,1,0:T(8,128)(2,1)} %reduce-scatter.11.cloned.1.call-done), kind=kOutput, calls=%fused_computation.9 | convolution fusion | flops 3355443200 | bytes 23920640 | tf_op jit(solution)/shard_map/pjrs,jqsc->rjpqc/dot_general | solution.py:52
  367.9 2.8 fusion.50
  370.7 2.8 fusion.49
  373.5 1.7 pad_maximum_fusion.3
  375.2 4.4 copy.83
  379.7 62.1 %reduce-scatter.15.cloned.1.call-done = bf16[640,256]{1,0:T(8,128)(2,1)} async-done(((bf16[5120,256]{1,0:T(8,128)(2,1)}), bf16[640,256]{1,0:T(8,128)(2,1)}) %reduce-scatter.15.cloned.1.call-update) | async-done | bytes 327696
  443.9 2.2 copy.65
  446.1 58.6 %all-gather.5.cloned.1.call-done = bf16[640,16,2,128]{3,0,2,1:T(8,128)(2,1)} async-done(((bf16[640,1,2,128]{3,0,2,1:T(8,128)(2,1)}), bf16[640,16,2,128]{3,0,2,1:T(8,128)(2,1)}) %all-gather.5.cloned.1.call-update) | async-done | bytes 5242896 | tf_op jit(solution)/shard_map/all_gather | solution.py:77
  504.7 3.1 fusion.95
  507.8 1.7 fusion.31
  509.6 11.4 %fusion.14 = bf16[16,640,128]{2,0,1:T(8,128)(2,1)S(1)} fusion(f32[16,640,128]{2,0,1:T(8,128)S(1)} %fusion.31, bf16[16,640,128]{2,1,0:T(8,128)(2,1)S(1)} %copy-done.1, s32[640,128]{1,0:T(8,128)S(1)} %copy-done.2, s32[16]{0:T(128)S(1)} %subtract_minimum_fusion, bf16[640,16,1,128]{3,0,2,1:T(8,128)(2,1)S(1)} %get-tuple-element.8, s32[16]{0:T(128)S(1)} %get-tuple-element.13, ...), kind=kOutput, calls=%fused_computation.14 | convolution fusion | flops 51121920 | bytes 13435072 | tf_op jit(solution)/shard_map/ft,rfc->trc/dot_general | solution.py:31
  521.0 2.2 copy.66
  (28 shorter events, 6.4 us)
Async XLA Ops:
  7.2 103.3 %reduce-scatter.9.cloned.1.call-start = ((), (), s32[]{:S(2)}) async-start(), calls=%async_computation.4 | async-start | bytes 5570560 | tf_op jit(solution)/shard_map/reduce_scatter | solution.py:69
  7.2 3.8 copy-start
  23.2 171.0 %reduce-scatter.13.cloned.1.call-start = ((), (), s32[]{:S(2)}) async-start(), calls=%async_computation.8 | async-start | bytes 2949120
  132.0 125.3 %all-gather.3.cloned.1.call-start = ((), (), s32[]{:S(2)}) async-start(), calls=%async_computation.5 | async-start | bytes 5570560 | tf_op jit(solution)/shard_map/all_gather | solution.py:77
  196.3 158.4 %reduce-scatter.11.cloned.1.call-start = ((), (), s32[]{:S(2)}) async-start(), calls=%async_computation.6 | async-start | bytes 5570560 | tf_op jit(solution)/shard_map/reduce_scatter | solution.py:69
  260.4 1.8 copy-start.2
  273.5 168.3 %reduce-scatter.15.cloned.1.call-start = ((), (), s32[]{:S(2)}) async-start(), calls=%async_computation.9 | async-start | bytes 2949120
  379.6 125.1 %all-gather.5.cloned.1.call-start = ((), (), s32[]{:S(2)}) async-start(), calls=%async_computation.7 | async-start | bytes 5570560 | tf_op jit(solution)/shard_map/all_gather | solution.py:77
  507.8 1.8 copy-start.1
Sparse Core Ops, SparseCore 0:
  23.3 87.0 reduce-scatter.8
  132.1 62.0 reduce-scatter.12
  197.2 59.9 all-gather.2
  273.6 81.0 reduce-scatter.10
  379.7 62.0 reduce-scatter.14
  444.7 59.9 all-gather.4
where the time goes:
time: 537 us; the launch traced here: 530 us
  waiting for transfers between devices  411 us (77%)
  matrix products  55.7 us (10%)
  local copies, waits for them, and re-layouts  33.3 us (6%)
  between operations  14.6 us (3%)
  other arithmetic  14.1 us (3%)
    reduce_scatter x2, waiting for transfers between devices, spectra_of(): lax.psum_scatter(to_freq(signal, freq_rows, own_times, time_count).astype...  168 us
    unnamed x8, waiting for transfers between devices  124 us
    all_gather x2, waiting for transfers between devices, field_of(): shard_piece = lax.all_gather(spectra, 'freq', axis=1, tiled=True)  119 us
    dot_general x2, matrix products, source_sum(): jnp.einsum('pjrs,jqsc->rjpqc', reflection, spectra, preferred_element_typ...  26.2 us
    unnamed x14, local copies, waits for them, and re-layouts  14.6 us
    dot_general x2, matrix products, to_time(): jnp.einsum('ft,rfc->trc', cosines, spectra[:, :, 0], preferred_element_ty...  13.7 us
    another operation x6, other arithmetic, source_sum(): jnp.stack([real_part, imag_part], axis=2).astype(jnp.bfloat16)  13.2 us
  transfers between devices with their start and end apart: 6, of which 6 were waited for; matrix products, arithmetic and copies ran while one was open for 0% of the time, Pallas kernels for 0%

commit v1 on v0

v1 whole, which is shorter than its diff:
```python
import functools
import math

import jax
import jax.numpy as jnp
import ml_dtypes
import numpy as np
from jax import lax
from jax.experimental import pallas as pl
from jax.experimental.pallas import tpu as pltpu
from jax.sharding import Mesh
from jax.sharding import PartitionSpec as P

NT = 256
NF = 16
FREQ = ("z", "xh", "core")
SRC = ("y", "xl")
MIB = 1 << 20


def angle_tables():
    phases = ((np.arange(NF)[:, None] + 1) * np.arange(NT)[None, :]) % NT
    angles = phases.astype(np.float32) * np.float32(2.0 * math.pi / NT)
    return np.cos(angles), np.sin(angles)


def forward_table():
    cosines, sines = angle_tables()
    return np.stack([cosines, -sines], axis=1)


def inverse_table():
    cosines, sines = angle_tables()
    return (2.0 / NT) * np.stack([cosines, -sines], axis=1).reshape(2 * NF, NT).T


def spread(table, rows):
    return np.kron(table, np.eye(rows, dtype=np.float32)).astype(ml_dtypes.bfloat16)


def first_weights():
    table = forward_table()
    blocks = []
    for dev in range(16):
        own = np.arange(dev * 16, dev * 16 + 16)
        other = np.arange((dev ^ 1) * 16, (dev ^ 1) * 16 + 16)
        freqs = np.arange(8) * 2 + dev % 2
        part = table[freqs].reshape(16, NT)
        blocks.append(np.stack([spread(part[:, own], 16), spread(part[:, other], 16)]))
    return np.stack(blocks)


def inverse_weights(chunk):
    table = inverse_table()
    return np.stack([spread(table[i : i + chunk], 8) for i in range(0, NT, chunk)])


def forward_weights(chunk):
    table = forward_table().reshape(2 * NF, NT)
    return np.stack([spread(table[:, i : i + chunk], 8) for i in range(0, NT, chunk)])


def dot(a, b):
    return jnp.dot(a, b, preferred_element_type=jnp.float32)


def params(mib=48):
    return pltpu.CompilerParams(vmem_limit_bytes=mib * MIB)


def first_kernel(dev_ref, x_ref, xo_ref, w_ref, out_ref):
    rows = x_ref.shape[1]
    for at in range(0, rows, 16):
        own = x_ref[:, at : at + 16, :].reshape(256, 128)
        other = xo_ref[:, at : at + 16, :].reshape(256, 128)
        part = dot(w_ref[0, 0], own) + dot(w_ref[0, 1], other)
        out_ref[:, :, at : at + 16, :] = part.astype(jnp.bfloat16).reshape(8, 2, 16, 128)


def first_transform(dev, x, xo):
    rows = x.shape[1]
    step = 128
    weights = jnp.asarray(first_weights())
    spec = pl.BlockSpec((16, step, 128), lambda i, d: (0, i, 0))
    return pl.pallas_call(
        first_kernel,
        out_shape=jax.ShapeDtypeStruct((8, 2, rows, 128), jnp.bfloat16),
        grid_spec=pltpu.PrefetchScalarGridSpec(
            num_scalar_prefetch=1,
            grid=(rows // step,),
            in_specs=[spec, spec, pl.BlockSpec((1, 2, 256, 256), lambda i, d: (d[0], 0, 0, 0))],
            out_specs=pl.BlockSpec((8, 2, step, 128), lambda i, d: (0, 0, i, 0)),
        ),
        compiler_params=params(),
        name="first_transform",
    )(dev, x, xo, weights)


def product_kernel(sign, summed, s_ref, r_ref, out_ref, held):
    @pl.when(pl.program_id(0) == 0)
    def _():
        if summed:
            total = s_ref[0].astype(jnp.float32)
            for i in range(1, s_ref.shape[0]):
                total = total + s_ref[i].astype(jnp.float32)
            real, imag = total[0], total[1]
        else:
            real = jnp.concatenate([s_ref[i, 0].astype(jnp.float32) for i in range(16)], axis=0)
            imag = jnp.concatenate([s_ref[i, 1].astype(jnp.float32) for i in range(16)], axis=0)
        depth = real.shape[0]
        held[:depth, :128] = real.astype(jnp.bfloat16)
        held[:depth, 128:] = imag.astype(jnp.bfloat16)
        held[depth:, :128] = (-sign * imag).astype(jnp.bfloat16)
        held[depth:, 128:] = (sign * real).astype(jnp.bfloat16)

    both = jnp.concatenate([r_ref[0, 0], r_ref[1, 0]], axis=1)
    part = dot(both, held[...])
    for g in range(16):
        out_ref[g, 0] = part[g * 40 : g * 40 + 40, :128].astype(jnp.bfloat16)
        out_ref[g, 1] = part[g * 40 : g * 40 + 40, 128:].astype(jnp.bfloat16)


def product(spectra, reflection, sign, summed):
    depth = reflection.shape[3]
    zeros = (0,) * spectra.ndim
    return pl.pallas_call(
        functools.partial(product_kernel, sign, summed),
        out_shape=jax.ShapeDtypeStruct((128, 2, 40, 128), jnp.bfloat16),
        grid=(8,),
        in_specs=[
            pl.BlockSpec(spectra.shape, lambda i: zeros),
            pl.BlockSpec((2, 1, 640, depth), lambda i: (0, 0, i, 0)),
        ],
        out_specs=pl.BlockSpec((16, 2, 40, 128), lambda i: (i, 0, 0, 0)),
        scratch_shapes=[pltpu.VMEM((2 * depth, 256), jnp.bfloat16)],
        compiler_params=params(),
        name="product",
    )(spectra, reflection)


def lanes(rows):
    return jnp.concatenate([rows[:, i : i + 8, :].reshape(-1, 128) for i in range(0, 40, 8)], axis=1)


def unlanes(flat):
    parts = [flat[:, i * 128 : i * 128 + 128].reshape(-1, 8, 128) for i in range(5)]
    return jnp.concatenate(parts, axis=1)


def kept(field, first, onsets):
    chunk = field.shape[0] // 8
    times = first + lax.broadcasted_iota(jnp.int32, (chunk, 8, 128), 0)
    distance = jnp.minimum(times, NT - times)
    parts = []
    for i in range(5):
        piece = field[:, i * 128 : i * 128 + 128].reshape(chunk, 8, 128)
        parts.append(jnp.where(distance < onsets[i * 8 : i * 8 + 8][None], piece, 0.0).reshape(-1, 128))
    return jnp.concatenate(parts, axis=1)


def summed_product(p_ref):
    total = p_ref[0].astype(jnp.float32)
    for i in range(1, 8):
        total = total + p_ref[i].astype(jnp.float32)
    return total.reshape(2 * NF, 40, 128)


def middle_kernel(p_ref, onset_ref, wi_ref, wf_ref, sum_ref, out_ref, acc):
    total = summed_product(p_ref)
    sum_ref[...] = total.astype(jnp.bfloat16)
    flat = lanes(total).astype(jnp.bfloat16)
    onsets = onset_ref[0]
    acc[...] = jnp.zeros_like(acc)

    def body(i, carry):
        field = dot(wi_ref[i], flat)
        minus = kept(field, i * 32, onsets).astype(jnp.bfloat16)
        acc[...] += dot(wf_ref[i], minus)
        return carry

    lax.fori_loop(0, 8, body, 0)
    out_ref[...] = unlanes(acc[...]).astype(jnp.bfloat16).reshape(NF, 2, 40, 128)


def onset_spec():
    return pl.BlockSpec((1, 40, 128), lambda i, d: (d[0], 0, 0))


def whole(shape):
    zeros = (0,) * len(shape)
    return pl.BlockSpec(shape, lambda i, d: zeros)


def middle(dev, parts, onsets):
    wi = jnp.asarray(inverse_weights(32))
    wf = jnp.asarray(forward_weights(32))
    return pl.pallas_call(
        lambda d, *refs: middle_kernel(*refs),
        out_shape=(
            jax.ShapeDtypeStruct((2 * NF, 40, 128), jnp.bfloat16),
            jax.ShapeDtypeStruct((NF, 2, 40, 128), jnp.bfloat16),
        ),
        grid_spec=pltpu.PrefetchScalarGridSpec(
            num_scalar_prefetch=1,
            grid=(1,),
            in_specs=[whole(parts.shape), onset_spec(), whole(wi.shape), whole(wf.shape)],
            out_specs=(whole((2 * NF, 40, 128)), whole((NF, 2, 40, 128))),
            scratch_shapes=[pltpu.VMEM((256, 640), jnp.float32)],
        ),
        compiler_params=params(),
        name="middle",
    )(dev, parts, onsets, wi, wf)


def update_kernel(p_ref, onset_ref, wi_ref, out_ref):
    flat = lanes(summed_product(p_ref)).astype(jnp.bfloat16)
    onsets = onset_ref[0]

    def body(i, carry):
        field = kept(dot(wi_ref[i], flat), i * 32, onsets)
        out_ref[pl.ds(i * 32, 32)] = unlanes(field).astype(jnp.bfloat16)
        return carry

    lax.fori_loop(0, 8, body, 0)


def update_of(dev, parts, onsets):
    wi = jnp.asarray(inverse_weights(32))
    return pl.pallas_call(
        lambda d, *refs: update_kernel(*refs),
        out_shape=jax.ShapeDtypeStruct((NT, 40, 128), jnp.bfloat16),
        grid_spec=pltpu.PrefetchScalarGridSpec(
            num_scalar_prefetch=1,
            grid=(1,),
            in_specs=[whole(parts.shape), onset_spec(), whole(wi.shape)],
            out_specs=whole((NT, 40, 128)),
        ),
        compiler_params=params(),
        name="update_of",
    )(dev, parts, onsets, wi)


def minus_kernel(dev_ref, p_ref, onset_ref, w_ref, out_ref):
    first = dev_ref[0] * 16
    pieces = []
    for g in range(2):
        flat = lanes(p_ref[g].astype(jnp.float32)).astype(jnp.bfloat16)
        pieces.append(unlanes(kept(dot(w_ref[0], flat), first, onset_ref[g])))
    out_ref[...] = jnp.concatenate(pieces, axis=1).astype(jnp.bfloat16)


def minus_output(dev, gathered, onsets):
    weights = jnp.asarray(inverse_weights(16))
    return pl.pallas_call(
        minus_kernel,
        out_shape=jax.ShapeDtypeStruct((16, 640, 128), jnp.bfloat16),
        grid_spec=pltpu.PrefetchScalarGridSpec(
            num_scalar_prefetch=1,
            grid=(8,),
            in_specs=[
                pl.BlockSpec((2, 2 * NF, 40, 128), lambda i, d: (i, 0, 0, 0)),
                pl.BlockSpec((2, 40, 128), lambda i, d: (i, 0, 0)),
                pl.BlockSpec((1, 128, 256), lambda i, d: (d[0], 0, 0)),
            ],
            out_specs=pl.BlockSpec((16, 80, 128), lambda i, d: (0, i, 0)),
        ),
        compiler_params=params(),
        name="minus_output",
    )(dev, gathered, onsets, weights)


def plus_kernel(u_ref, x_ref, out_ref):
    update = jnp.concatenate([u_ref[g].astype(jnp.float32) for g in range(16)], axis=1)
    out_ref[...] = (x_ref[...].astype(jnp.float32) + update).astype(jnp.bfloat16)


def plus_output(update, x):
    step = 4
    return pl.pallas_call(
        plus_kernel,
        out_shape=jax.ShapeDtypeStruct(x.shape, jnp.bfloat16),
        grid=(16 // step,),
        in_specs=[
            pl.BlockSpec((16, step, 40, 128), lambda i: (0, i, 0, 0)),
            pl.BlockSpec((step, 640, 128), lambda i: (i, 0, 0)),
        ],
        out_specs=pl.BlockSpec((step, 640, 128), lambda i: (i, 0, 0)),
        compiler_params=params(),
        name="plus_output",
    )(update, x)


def exchange(x, axes):
    return lax.all_to_all(x, axes, 0, 0, tiled=True)


def local(reflection, focus_start, onsets):
    dev = lax.axis_index(FREQ).astype(jnp.int32).reshape(1)
    onsets = onsets.reshape(16, 40, 128)
    other = lax.ppermute(focus_start, "core", [(0, 1), (1, 0)])
    partial = first_transform(dev, focus_start, other)
    partial = exchange(partial, ("z", "xh"))
    start_parts = exchange(product(partial, reflection, 1.0, True), SRC + FREQ)
    product_start, spectra = middle(dev, start_parts.reshape(8, NF, 2, 40, 128), onsets)
    gathered = lax.all_gather(product_start, FREQ)
    spectra = exchange(spectra, FREQ)
    minus_parts = exchange(product(spectra, reflection, -1.0, False), SRC + FREQ)
    update = update_of(dev, minus_parts.reshape(8, NF, 2, 40, 128), onsets)
    update = exchange(update.reshape(16, 16, 40, 128), FREQ)
    minus_field = minus_output(dev, gathered, onsets)
    return minus_field, plus_output(update, focus_start)


def solution(mesh):
    cut = Mesh(mesh.devices.reshape(4, 2, 2, 4, 2), FREQ + SRC)
    return jax.shard_map(
        local,
        mesh=cut,
        in_specs=(P(None, FREQ, None, SRC), P(FREQ, SRC, None), P(SRC, None)),
        out_specs=(P(FREQ, SRC, None), P(FREQ, SRC, None)),
        check_vma=False,
    )
```

time: 537 us -> 257 us (0.48); the launches traced: 530 us -> 256 us
  waiting for transfers between devices: 411 us -> 4.76 us
  blocking collectives: 0 us -> 189 us
  matrix products: 55.7 us -> 0 us
  Pallas kernels: 0 us -> 43.1 us
  local copies, waits for them, and re-layouts: 33.3 us -> 3.26 us
  other arithmetic: 14.1 us -> 0 us
    all_to_all x0 -> x5, blocking collectives: none -> 189 us  [exchange(): return lax.all_to_all(x, axes, 0, 0, tiled=True)]
    reduce_scatter x2 -> x0, waiting for transfers between devices: 168 us -> none  [spectra_of(): lax.psum_scatter(to_freq(signal, freq_rows, own_times, time_count).astype...]
    unnamed x8 -> x1, waiting for transfers between devices: 124 us -> 0.02 us
    all_gather x2 -> x1, waiting for transfers between devices: 119 us -> 0.01 us  [local(): gathered = lax.all_gather(product_start, FREQ)]
    dot_general x10 -> x0, matrix products: 55.7 us -> none  [the longest x2 26.2 us: source_sum(): jnp.einsum('pjrs,jqsc->rjpqc', reflection, spectra, preferred_element_typ...]
    pallas_call x0 -> x7, Pallas kernels: none -> 43.1 us  [the longest x2 18.8 us: product(): pl.pallas_call(functools.partial(product_kernel, sign, summed), out_shape...]
    another operation x8 -> x0, other arithmetic: 14.1 us -> none  [the longest x6 13.2 us: source_sum(): jnp.stack([real_part, imag_part], axis=2).astype(jnp.bfloat16)]
    unnamed x14, local copies, waits for them, and re-layouts: 14.6 us -> 3.26 us
  transfers between devices with their start and end apart: 6 -> 2, of which waited for: 6 -> 1; matrix products, arithmetic and copies ran while one was open for 0% -> 0% of each run, Pallas kernels for 0% -> 6%
where the time goes in v1:
time: 257 us; the launch traced here: 256 us
  blocking collectives  189 us (74%)
  Pallas kernels  43.1 us (17%)
  between operations  14.1 us (5%)
  waiting for transfers between devices  4.76 us (2%)
  local copies, waits for them, and re-layouts  3.26 us (1%)
    all_to_all x5, blocking collectives, exchange(): return lax.all_to_all(x, axes, 0, 0, tiled=True)  189 us
    pallas_call x2, Pallas kernels, product(): pl.pallas_call(functools.partial(product_kernel, sign, summed), out_shape...  18.8 us
    pallas_call x1, Pallas kernels, minus_output(): pl.pallas_call(minus_kernel, out_shape=jax.ShapeDtypeStruct((16, 640, 128...  7.3 us
    pallas_call x1, Pallas kernels, first_transform(): pl.pallas_call(first_kernel, out_shape=jax.ShapeDtypeStruct((8, 2, rows,...  5.51 us
  transfers between devices with their start and end apart: 2, of which 1 were waited for; matrix products, arithmetic and copies ran while one was open for 0% of the time, Pallas kernels for 6%

profile of v1, /device:TPU:1, one launch (start us, length us, event | category | flops | bytes accessed | tf_op | source)
XLA Modules:
  0.0 256.1 jit_solution(14283529205329854953)
XLA Ops:
  7.2 0.0 all-gather.3.cloned.1.call-start
  7.2 1.5 collective-permute-start
  8.7 4.7 %collective-permute-done.xo_ref = bf16[16,640,128]{2,1,0:T(8,128)(2,1)S(1)} collective-permute-done((bf16[16,640,128]{2,1,0:T(8,128)(2,1)}, bf16[16,640,128]{2,1,0:T(8,128)(2,1)S(1)}, u32[]{:S(2)}, u32[]{:S(2)}) %collective-permute-start) | collective-permute-done | bytes 2621472 | tf_op jit(solution)/shard_map/ppermute | solution.py:300
  13.5 0.0 copy-start.6
  13.5 1.5 copy-done.6
  14.9 0.0 copy-start
  15.0 1.7 copy-done
  16.7 5.5 %first_transform.1 = bf16[8,2,640,128]{3,2,1,0:T(8,128)(2,1)S(1)} custom-call(s32[1]{0:T(128)} %bitcast.dev_ref.d, bf16[16,640,128]{2,1,0:T(8,128)(2,1)S(1)} %copy-done, bf16[16,640,128]{2,1,0:T(8,128)(2,1)} %copy-done.6, bf16[16,2,256,256]{3,2,1,0:T(8,128)(2,1)} %constant.27.clone.w_ref), custom_call_target="tpu_custom_call" | custom-call | tf_op jit(solution)/shard_map/first_transform/pallas_call | solution.py:85
  22.2 40.6 %all_to_all.25.s_ref = bf16[8,2,640,128]{3,2,1,0:T(8,128)(2,1)S(1)} all-to-all(bf16[8,2,640,128]{3,2,1,0:T(8,128)(2,1)S(1)} %first_transform.1), channel_id=1, replica_groups=mesh['z'=4,'xh'=2,'core'=2,'y'=4,'xl'=2] {'z','xh'}, dimensions={0} | all-to-all | bytes 5242880 | tf_op jit(solution)/shard_map/all_to_all | solution.py:294
  62.8 9.5 %product.2 = bf16[128,2,40,128]{3,2,1,0:T(8,128)(2,1)S(1)} custom-call(bf16[8,2,640,128]{3,2,1,0:T(8,128)(2,1)S(1)} %all_to_all.25.s_ref, bf16[2,1,5120,640]{3,2,1,0:T(8,128)(2,1)} %r_ref.3), custom_call_target="tpu_custom_call" | custom-call | tf_op jit(solution)/shard_map/product/pallas_call | solution.py:126
  72.3 0.0 copy-start.2
  72.3 0.0 copy-start.3
  72.3 0.0 copy-start.5
  72.3 42.1 %all_to_all.26 = bf16[128,2,40,128]{3,2,1,0:T(8,128)(2,1)S(1)} all-to-all(bf16[128,2,40,128]{3,2,1,0:T(8,128)(2,1)S(1)} %product.2), channel_id=1, replica_groups=mesh['z'=4,'xh'=2,'core'=2,'y'=4,'xl'=2] {'y','xl','z','xh','core'}, dimensions={0} | all-to-all | bytes 5242880 | tf_op jit(solution)/shard_map/all_to_all | solution.py:294
  114.5 0.0 copy-done.2
  114.5 0.0 copy-done.3
  114.5 0.0 copy-done.5
  114.5 4.6 %middle.1 = (bf16[32,40,128]{2,1,0:T(8,128)(2,1)}, bf16[16,2,40,128]{3,2,1,0:T(8,128)(2,1)S(1)}) custom-call(s32[1]{0:T(128)} %bitcast.dev_ref.d, bf16[8,16,2,40,128]{4,3,2,1,0:T(8,128)(2,1)S(1)} %bitcast.6, s32[16,40,128]{2,1,0:T(8,128)S(1)} %bitcast.8, bf16[8,256,256]{2,1,0:T(8,128)(2,1)S(1)} %copy-done.2, bf16[8,256,256]{2,1,0:T(8,128)(2,1)S(1)} %copy-done.5), custom_call_target="tpu_custom_call" | custom-call | tf_op jit(solution)/shard_map/middle/pallas_call | solution.py:197
  119.1 0.0 all-gather.3.cloned.1.call-update
  119.1 13.3 %all_to_all.27.s_ref = bf16[16,2,40,128]{3,2,1,0:T(8,128)(2,1)S(1)} all-to-all(bf16[16,2,40,128]{3,2,1,0:T(8,128)(2,1)S(1)} %get-tuple-element.5), channel_id=1, replica_groups=mesh['z'=4,'xh'=2,'core'=2,'y'=4,'xl'=2] {'z','xh','core'}, dimensions={0} | all-to-all | bytes 655360 | tf_op jit(solution)/shard_map/all_to_all | solution.py:294
  132.4 9.2 %product.3 = bf16[128,2,40,128]{3,2,1,0:T(8,128)(2,1)S(1)} custom-call(bf16[16,2,40,128]{3,2,1,0:T(8,128)(2,1)S(1)} %all_to_all.27.s_ref, bf16[2,1,5120,640]{3,2,1,0:T(8,128)(2,1)} %r_ref.3), custom_call_target="tpu_custom_call" | custom-call | tf_op jit(solution)/shard_map/product/pallas_call | solution.py:126
  141.7 55.2 %all_to_all.28 = bf16[128,2,40,128]{3,2,1,0:T(8,128)(2,1)} all-to-all(bf16[128,2,40,128]{3,2,1,0:T(8,128)(2,1)S(1)} %product.3), channel_id=1, replica_groups=mesh['z'=4,'xh'=2,'core'=2,'y'=4,'xl'=2] {'y','xl','z','xh','core'}, dimensions={0} | all-to-all | bytes 5242880 | tf_op jit(solution)/shard_map/all_to_all | solution.py:294
  196.9 4.6 %update_of.1 = bf16[256,40,128]{2,1,0:T(8,128)(2,1)S(1)} custom-call(s32[1]{0:T(128)} %bitcast.dev_ref.d, bf16[8,16,2,40,128]{4,3,2,1,0:T(8,128)(2,1)} %bitcast.11, s32[16,40,128]{2,1,0:T(8,128)S(1)} %bitcast.9, bf16[8,256,256]{2,1,0:T(8,128)(2,1)S(1)} %copy-done.2), custom_call_target="tpu_custom_call" | custom-call | tf_op jit(solution)/shard_map/update_of/pallas_call | solution.py:229
  201.5 0.0 copy-start.1
  201.5 38.1 %all_to_all.29.u_ref = bf16[16,16,40,128]{3,2,1,0:T(8,128)(2,1)S(1)} all-to-all(bf16[16,16,40,128]{3,2,1,0:T(8,128)(2,1)S(1)} %bitcast.7), channel_id=1, replica_groups=mesh['z'=4,'xh'=2,'core'=2,'y'=4,'xl'=2] {'z','xh','core'}, dimensions={0} | all-to-all | bytes 5242880 | tf_op jit(solution)/shard_map/all_to_all | solution.py:294
  239.6 0.0 copy-done.1
  239.6 0.0 copy-start.4
  239.6 2.4 plus_output.1
  242.0 0.0 all-gather.3.cloned.1.call-done
  242.0 0.0 copy-done.4
  242.0 7.3 %minus_output.1 = bf16[16,640,128]{2,1,0:T(8,128)(2,1)} custom-call(s32[1]{0:T(128)} %bitcast.dev_ref.d, bf16[16,32,40,128]{3,2,1,0:T(8,128)(2,1)} %bitcast.12, s32[16,40,128]{2,1,0:T(8,128)S(1)} %bitcast.10, bf16[16,128,256]{2,1,0:T(8,128)(2,1)S(1)} %copy-done.4), custom_call_target="tpu_custom_call" | custom-call | tf_op jit(solution)/shard_map/minus_output/pallas_call | solution.py:254
Async XLA Ops:
  7.2 234.8 %all-gather.3.cloned.1.call-start = ((), (), s32[]{:S(2)}) async-start(), calls=%async_computation.5 | async-start | bytes 5570560 | tf_op jit(solution)/shard_map/all_gather | solution.py:305
  7.2 6.2 %collective-permute-start = (bf16[16,640,128]{2,1,0:T(8,128)(2,1)}, bf16[16,640,128]{2,1,0:T(8,128)(2,1)S(1)}, u32[]{:S(2)}, u32[]{:S(2)}) collective-permute-start(bf16[16,640,128]{2,1,0:T(8,128)(2,1)} %x_ref.3), channel_id=1, source_target_pairs={{0,8},{8,0},{1,9},{9,1},{2,10},{10,2},{3,11},{11,3},{4,12},{12,4},... | collective-permute-start | bytes 7864328 | tf_op jit(solution)/shard_map/ppermute | solution.py:300
  13.5 1.5 copy-start.6
  14.9 1.7 copy-start
  72.3 42.2 %copy-start.2 = (bf16[8,256,256]{2,1,0:T(8,128)(2,1)S(1)}, bf16[8,256,256]{2,1,0:T(8,128)(2,1)}, u32[]{:S(2)}) copy-start(bf16[8,256,256]{2,1,0:T(8,128)(2,1)} %constant.28.clone.refs_2_) | copy-start | bytes 3145732
  72.3 42.2 %copy-start.3 = (s32[640,128]{1,0:T(8,128)S(1)}, s32[640,128]{1,0:T(8,128)}, u32[]{:S(2)}) copy-start(s32[640,128]{1,0:T(8,128)} %param.10) | copy-start | bytes 983044
  72.3 42.2 %copy-start.5 = (bf16[8,256,256]{2,1,0:T(8,128)(2,1)S(1)}, bf16[8,256,256]{2,1,0:T(8,128)(2,1)}, u32[]{:S(2)}) copy-start(bf16[8,256,256]{2,1,0:T(8,128)(2,1)} %constant.29.clone.refs_3_) | copy-start | bytes 3145732
  201.5 38.1 %copy-start.1 = (bf16[16,640,128]{2,1,0:T(8,128)(2,1)S(1)}, bf16[16,640,128]{2,1,0:T(8,128)(2,1)}, u32[]{:S(2)}) copy-start(bf16[16,640,128]{2,1,0:T(8,128)(2,1)} %x_ref.3) | copy-start | bytes 7864324
  239.6 2.4 copy-start.4
Sparse Core Ops, SparseCore 0:
  119.3 80.0 all-gather.2

commit v2 on v1

v2 whole, which is shorter than its diff:
```python
import functools
import math

import jax
import jax.numpy as jnp
import ml_dtypes
import numpy as np
from jax import lax
from jax.experimental import pallas as pl
from jax.experimental.pallas import tpu as pltpu
from jax.sharding import Mesh
from jax.sharding import PartitionSpec as P

NT = 256
NF = 16
FREQ = ("z", "xh", "core")
SRC = ("y", "xl")
MIB = 1 << 20


def angle_tables():
    phases = ((np.arange(NF)[:, None] + 1) * np.arange(NT)[None, :]) % NT
    angles = phases.astype(np.float32) * np.float32(2.0 * math.pi / NT)
    return np.cos(angles), np.sin(angles)


def forward_table():
    cosines, sines = angle_tables()
    return np.stack([cosines, -sines], axis=1)


def inverse_table():
    cosines, sines = angle_tables()
    return (2.0 / NT) * np.stack([cosines, -sines], axis=1).reshape(2 * NF, NT).T


def spread(table, rows):
    return np.kron(table, np.eye(rows, dtype=np.float32)).astype(ml_dtypes.bfloat16)


def place(dev):
    return dev // 4, dev // 2 % 2, dev % 2


def frequency(z, xh, core):
    return (z % 4 * 2 + xh % 2) * 2 + core % 2


def first_weights():
    table = forward_table()
    blocks = []
    for dev in range(16):
        z, xh, core = place(dev)
        own = np.arange(dev * 16, dev * 16 + 16)
        other = np.arange((dev ^ 1) * 16, (dev ^ 1) * 16 + 16)
        freqs = [frequency(z + dz, xh + e, core) for dz in range(4) for e in range(2)]
        part = table[freqs].reshape(16, NT)
        blocks.append(np.stack([spread(part[:, own], 16), spread(part[:, other], 16)]))
    return np.stack(blocks)


def last_weights():
    table = inverse_table().reshape(NT, NF, 2)
    blocks = []
    for dev in range(16):
        z, xh, core = place(dev)
        own = np.arange(dev * 16, dev * 16 + 16)
        freqs = [frequency(z - k, xh + e, core + c) for c in range(2) for e in range(2) for k in range(4)]
        blocks.append(spread(table[own][:, freqs].reshape(16, 2 * NF), 16))
    return np.stack(blocks)


def inverse_weights(chunk):
    table = inverse_table()
    return np.stack([spread(table[i : i + chunk], 8) for i in range(0, NT, chunk)])


def forward_weights(chunk):
    table = forward_table().reshape(2 * NF, NT)
    return np.stack([spread(table[:, i : i + chunk], 8) for i in range(0, NT, chunk)])


def dot(a, b):
    return jnp.dot(a, b, preferred_element_type=jnp.float32)


def params(mib=24):
    return pltpu.CompilerParams(vmem_limit_bytes=mib * MIB)


def cost(flops, moved):
    return pl.CostEstimate(flops=flops, bytes_accessed=moved, transcendentals=0)


HALF = 320


def first_kernel(by_z, dev_ref, x_ref, xo_ref, w_ref, *out_refs):
    rows = x_ref.shape[1]
    for at in range(0, rows, 16):
        own = x_ref[:, at : at + 16, :].reshape(256, 128)
        other = xo_ref[:, at : at + 16, :].reshape(256, 128)
        part = dot(w_ref[0, 0], own) + dot(w_ref[0, 1], other)
        part = part.astype(jnp.bfloat16).reshape(4, 2, 2, 16, 128)
        for i, out_ref in enumerate(out_refs):
            out_ref[:, :, at : at + 16, :] = part[i] if by_z else part[:, i]


def first_transform(dev, x, xo, by_z):
    step = 160
    spec = pl.BlockSpec((16, step, 128), lambda i, d: (0, i, 0))
    count, lead = (4, 2) if by_z else (2, 4)
    return pl.pallas_call(
        functools.partial(first_kernel, by_z),
        out_shape=[jax.ShapeDtypeStruct((lead, 2, HALF, 128), jnp.bfloat16)] * count,
        grid_spec=pltpu.PrefetchScalarGridSpec(
            num_scalar_prefetch=1,
            grid=(HALF // step,),
            in_specs=[spec, spec, pl.BlockSpec((1, 2, 256, 256), lambda i, d: (d[0], 0, 0, 0))],
            out_specs=[pl.BlockSpec((lead, 2, step, 128), lambda i, d: (0, 0, i, 0))] * count,
        ),
        compiler_params=params(),
        cost_estimate=cost(700 << 20, 6 << 20),
        name="first_transform",
    )(dev, x, xo, jnp.asarray(first_weights()))


def total_of(refs):
    total = refs[0][...].astype(jnp.float32)
    for ref in refs[1:]:
        total = total + ref[...].astype(jnp.float32)
    return total


def hold(held, real, imag, sign):
    depth = real.shape[0]
    held[:depth, :128] = real.astype(jnp.bfloat16)
    held[:depth, 128:] = imag.astype(jnp.bfloat16)
    held[depth:, :128] = (-sign * imag).astype(jnp.bfloat16)
    held[depth:, 128:] = (sign * real).astype(jnp.bfloat16)


def start_product_kernel(counts, *refs):
    s_refs, (r_ref, out_ref, held) = refs[: sum(counts)], refs[sum(counts) :]

    @pl.when(pl.program_id(0) == 0)
    def _():
        halves = [total_of(s_refs[: counts[0]]), total_of(s_refs[counts[0] :])]
        real, imag = [jnp.concatenate([h[i] for h in halves], axis=0) for i in range(2)]
        hold(held, real, imag, 1.0)

    both = jnp.concatenate([r_ref[0, 0], r_ref[1, 0]], axis=1)
    part = dot(both, held[...])
    for g in range(out_ref.shape[0]):
        out_ref[g, 0] = part[g * 40 : g * 40 + 40, :128].astype(jnp.bfloat16)
        out_ref[g, 1] = part[g * 40 : g * 40 + 40, 128:].astype(jnp.bfloat16)


def start_product(spectra, counts, reflection):
    depth = reflection.shape[3]
    rows = 1280
    return pl.pallas_call(
        functools.partial(start_product_kernel, counts),
        out_shape=jax.ShapeDtypeStruct((128, 2, 40, 128), jnp.bfloat16),
        grid=(5120 // rows,),
        in_specs=[pl.BlockSpec(s.shape, lambda i, n=s.ndim: (0,) * n) for s in spectra]
        + [pl.BlockSpec((2, 1, rows, depth), lambda i: (0, 0, i, 0))],
        out_specs=pl.BlockSpec((rows // 40, 2, 40, 128), lambda i: (i, 0, 0, 0)),
        scratch_shapes=[pltpu.VMEM((2 * depth, 256), jnp.bfloat16)],
        compiler_params=params(),
        cost_estimate=cost(4 << 30, 18 << 20),
        name="start_product",
    )(*spectra, reflection)


def minus_product_kernel(s_ref, r_ref, out_ref, held):
    @pl.when(pl.program_id(0) == 0)
    def _():
        real, imag = [
            jnp.concatenate([s_ref[i, part].astype(jnp.float32) for i in range(16)], axis=0) for part in range(2)
        ]
        hold(held, real, imag, -1.0)

    both = jnp.concatenate([r_ref[0, 0], r_ref[1, 0]], axis=1)
    part = dot(both, held[...]).astype(jnp.bfloat16)
    for g in range(out_ref.shape[0]):
        for i in range(2):
            out_ref[g, i] = part[g * 640 : g * 640 + 640, i * 128 : i * 128 + 128]


def minus_product(spectra, reflection):
    depth = reflection.shape[3]
    rows = 1280
    return pl.pallas_call(
        minus_product_kernel,
        out_shape=jax.ShapeDtypeStruct((8, 2, 640, 128), jnp.bfloat16),
        grid=(5120 // rows,),
        in_specs=[
            pl.BlockSpec(spectra.shape, lambda i: (0, 0, 0, 0)),
            pl.BlockSpec((2, 1, rows, depth), lambda i: (0, 0, i, 0)),
        ],
        out_specs=pl.BlockSpec((rows // 640, 2, 640, 128), lambda i: (i, 0, 0, 0)),
        scratch_shapes=[pltpu.VMEM((2 * depth, 256), jnp.bfloat16)],
        compiler_params=params(),
        cost_estimate=cost(4 << 30, 18 << 20),
        name="minus_product",
    )(spectra, reflection)


def lanes(rows):
    return jnp.concatenate([rows[:, i : i + 8, :].reshape(-1, 128) for i in range(0, 40, 8)], axis=1)


def unlanes(flat):
    parts = [flat[:, i * 128 : i * 128 + 128].reshape(-1, 8, 128) for i in range(5)]
    return jnp.concatenate(parts, axis=1)


def kept(field, first, onsets):
    chunk = field.shape[0] // 8
    times = first + lax.broadcasted_iota(jnp.int32, (chunk, 8, 128), 0)
    distance = jnp.minimum(times, NT - times)
    parts = []
    for i in range(5):
        piece = field[:, i * 128 : i * 128 + 128].reshape(chunk, 8, 128)
        parts.append(jnp.where(distance < onsets[i * 8 : i * 8 + 8][None], piece, 0.0).reshape(-1, 128))
    return jnp.concatenate(parts, axis=1)


def summed_product(p_ref):
    total = p_ref[0].astype(jnp.float32)
    for i in range(1, 8):
        total = total + p_ref[i].astype(jnp.float32)
    return total.reshape(2 * NF, 40, 128)


def middle_kernel(p_ref, onset_ref, wi_ref, wf_ref, sum_ref, out_ref, acc):
    total = summed_product(p_ref)
    sum_ref[...] = total.astype(jnp.bfloat16)
    flat = lanes(total).astype(jnp.bfloat16)
    onsets = onset_ref[0]
    acc[...] = jnp.zeros_like(acc)

    def body(i, carry):
        field = dot(wi_ref[i], flat)
        minus = kept(field, i * 32, onsets).astype(jnp.bfloat16)
        acc[...] += dot(wf_ref[i], minus)
        return carry

    lax.fori_loop(0, 8, body, 0)
    out_ref[...] = unlanes(acc[...]).astype(jnp.bfloat16).reshape(NF, 2, 40, 128)


def onset_spec():
    return pl.BlockSpec((1, 40, 128), lambda i, d: (d[0], 0, 0))


def whole(shape):
    zeros = (0,) * len(shape)
    return pl.BlockSpec(shape, lambda i, d: zeros)


def middle(dev, parts, onsets):
    wi = jnp.asarray(inverse_weights(32))
    wf = jnp.asarray(forward_weights(32))
    return pl.pallas_call(
        lambda d, *refs: middle_kernel(*refs),
        out_shape=(
            jax.ShapeDtypeStruct((2 * NF, 40, 128), jnp.bfloat16),
            jax.ShapeDtypeStruct((NF, 2, 40, 128), jnp.bfloat16),
        ),
        grid_spec=pltpu.PrefetchScalarGridSpec(
            num_scalar_prefetch=1,
            grid=(1,),
            in_specs=[whole(parts.shape), onset_spec(), whole(wi.shape), whole(wf.shape)],
            out_specs=(whole((2 * NF, 40, 128)), whole((NF, 2, 40, 128))),
            scratch_shapes=[pltpu.VMEM((256, 640), jnp.float32)],
        ),
        compiler_params=params(),
        cost_estimate=cost(2 << 30, 8 << 20),
        name="middle",
    )(dev, parts, onsets, wi, wf)


def minus_kernel(dev_ref, *refs):
    mine, others, onset_ref, w_ref, out_ref = refs[:4], refs[4:8], refs[8], refs[9], refs[10]
    dev = dev_ref[0]
    z, xh, core = lax.div(dev, 4), lax.rem(lax.div(dev, 2), 2), lax.rem(dev, 2)
    for k in range(4):
        for e in range(2):
            chip = lax.rem(z + 4 - k, 4) * 2 + lax.rem(xh + e, 2)
            pieces = []
            for ref, at in ((mine[k], core), (others[k], 1 - core)):
                flat = lanes(ref[e].astype(jnp.float32)).astype(jnp.bfloat16)
                pieces.append(unlanes(kept(dot(w_ref[0], flat), dev * 16, onset_ref[chip * 2 + at])))
            swap = core == 1
            both = [jnp.where(swap, pieces[1], pieces[0]), jnp.where(swap, pieces[0], pieces[1])]
            rows = pl.ds(pl.multiple_of(chip * 80, 16), 80)
            out_ref[:, rows, :] = jnp.concatenate(both, axis=1).astype(jnp.bfloat16)


def minus_output(dev, mine, others, onsets):
    weights = jnp.asarray(inverse_weights(16))
    return pl.pallas_call(
        minus_kernel,
        out_shape=jax.ShapeDtypeStruct((16, 640, 128), jnp.bfloat16),
        grid_spec=pltpu.PrefetchScalarGridSpec(
            num_scalar_prefetch=1,
            grid=(1,),
            in_specs=[whole((2, 2 * NF, 40, 128))] * 8
            + [whole((16, 40, 128)), pl.BlockSpec((1, 128, 256), lambda i, d: (d[0], 0, 0))],
            out_specs=whole((16, 640, 128)),
        ),
        compiler_params=params(),
        cost_estimate=cost(700 << 20, 8 << 20),
        name="minus_output",
    )(dev, *mine, *others, onsets, weights)


def plus_kernel(half, dev_ref, *refs):
    *p_refs, onset_ref, x_ref, w_ref = refs[:-2] if half else refs[:-1]
    out_ref = refs[-1]
    first = dev_ref[0] * 16
    rows = x_ref.shape[1]
    times = first + lax.broadcasted_iota(jnp.int32, (16, 16, 128), 0)
    distance = jnp.minimum(times, NT - times)
    for at in range(0, rows, 32):
        sides = []
        for here in (slice(at, at + 16), slice(at + 16, at + 32)):
            if half:
                flat = [p_refs[c * 4 + k][e, :, here, :] for c in range(2) for e in range(2) for k in range(4)]
            else:
                flat = [p_refs[c * 2 + e][k, :, here, :] for c in range(2) for e in range(2) for k in range(4)]
            sides.append(jnp.concatenate([piece.reshape(32, 128) for piece in flat], axis=0))
        field = dot(w_ref[0], jnp.concatenate(sides, axis=1))
        for i in range(2):
            here = slice(at + i * 16, at + i * 16 + 16)
            side = field[:, i * 128 : i * 128 + 128].reshape(16, 16, 128)
            update = jnp.where(distance < onset_ref[here][None], side, 0.0)
            out_ref[:, here, :] = (x_ref[:, here, :].astype(jnp.float32) + update).astype(jnp.bfloat16)


def plus_output(dev, half, parts, onsets, x, held):
    step = 64
    start = half * HALF // step
    weights = jnp.asarray(last_weights())
    lead = 2 if half else 4
    time_spec = pl.BlockSpec((16, step, 128), lambda i, d: (0, i + start, 0))
    operands = [dev, *parts, onsets, x, weights] + ([held] if half else [])
    return pl.pallas_call(
        functools.partial(plus_kernel, half),
        out_shape=jax.ShapeDtypeStruct(x.shape, jnp.bfloat16),
        grid_spec=pltpu.PrefetchScalarGridSpec(
            num_scalar_prefetch=1,
            grid=(HALF // step,),
            in_specs=[pl.BlockSpec((lead, 2, step, 128), lambda i, d: (0, 0, i, 0))] * len(parts)
            + [
                pl.BlockSpec((step, 128), lambda i, d: (i + start, 0)),
                time_spec,
                pl.BlockSpec((1, 256, 512), lambda i, d: (d[0], 0, 0)),
            ]
            + ([pl.BlockSpec(memory_space=pl.ANY)] if half else []),
            out_specs=time_spec,
        ),
        input_output_aliases={len(operands) - 1: 0} if half else {},
        compiler_params=params(),
        cost_estimate=cost(700 << 20, 6 << 20),
        name="plus_output",
    )(*operands)


def exchange(x, axes):
    return lax.all_to_all(x, axes, 0, 0, tiled=True)


def along(x, axis, step):
    size = lax.axis_size(axis)
    return lax.ppermute(x, axis, [(i, (i + step) % size) for i in range(size)])


def add(*arrays):
    total = arrays[0].astype(jnp.float32)
    for array in arrays[1:]:
        total = total + array.astype(jnp.float32)
    return total.astype(jnp.bfloat16)


STEPS = (2, 1, 3)


def start_spectra(dev, x):
    xa, xb = x[:, :HALF], x[:, HALF:]
    xoa, xob = along(xa, "core", 1), along(xb, "core", 1)
    a_got = around(first_transform(dev, xa, xoa, True), "z")
    b_own, b_send = first_transform(dev, xb, xob, False)
    b_got = along(b_send, "xh", 1)
    a_got, b_got = together(a_got, b_got)
    a_keep, a_pass = [add(*[got[e] for got in a_got]) for e in range(2)]
    b_parts = around([add(b_own[k], b_got[k]) for k in range(4)], "z")
    return [a_keep, along(a_pass, "xh", 1)] + b_parts


def around(parts, axis):
    got = {k: along(parts[k], axis, k) for k in STEPS}
    return [parts[0], got[1], got[2], got[3]]


def together(*groups):
    return lax.optimization_barrier(groups)


def local(reflection, focus_start, onsets):
    dev = lax.axis_index(FREQ).astype(jnp.int32).reshape(1)
    blocks = onsets.reshape(16, 40, 128)
    spectra = start_spectra(dev, focus_start)
    start_parts = exchange(start_product(spectra, (2, 4), reflection), SRC + FREQ)
    summed, spectra = middle(dev, start_parts.reshape(8, NF, 2, 40, 128), blocks)
    spectra, far = together(exchange(spectra, FREQ), along(summed, "xh", 1))
    parts, near = together(minus_product(spectra, reflection), jnp.stack([summed, far]))
    parts, mine = together(exchange(parts, SRC), around([near] * 4, "z"))

    total = parts.astype(jnp.float32).sum(0).astype(jnp.bfloat16)
    a, b = total[:, :HALF], total[:, HALF:]
    b_far, a_near = along(b, "xh", 1), around([a] * 4, "z")
    others = [along(v, "core", 1) for v in mine]
    b_far, a_near = together(b_far, a_near)
    a_near, b_near = jnp.stack(a_near), jnp.stack([b, b_far])
    a_far, b_all = together(along(a_near, "xh", 1), around([b_near] * 4, "z"))
    minus_field = minus_output(dev, mine, others, blocks)
    a_all, b_all = [a_near, a_far], list(b_all)
    a_all = a_all + [along(v, "core", 1) for v in a_all]
    b_all = b_all + [along(v, "core", 1) for v in b_all]
    plus_field = plus_output(dev, 0, a_all, onsets, focus_start, None)
    plus_field = plus_output(dev, 1, b_all, onsets, focus_start, plus_field)
    return minus_field, plus_field


def solution(mesh):
    cut = Mesh(mesh.devices.reshape(4, 2, 2, 4, 2), FREQ + SRC)
    return jax.shard_map(
        local,
        mesh=cut,
        in_specs=(P(None, FREQ, None, SRC), P(FREQ, SRC, None), P(SRC, None)),
        out_specs=(P(FREQ, SRC, None), P(FREQ, SRC, None)),
        check_vma=False,
    )
```

time: 257 us -> 217 us (0.84)
  blocking collectives: 189 us -> 55.4 us
  waiting for transfers between devices: 4.76 us -> 81.1 us
  starting transfers between devices: 1.54 us -> 36.1 us
  between operations: 14.1 us -> 0.8 us
  Pallas kernels: 43.1 us -> 32.3 us
  local copies, waits for them, and re-layouts: 3.26 us -> 7.36 us
  other arithmetic: 0 us -> 3.45 us
    all_to_all x5 -> x2, blocking collectives: 189 us -> 55.4 us  [exchange(): return lax.all_to_all(x, axes, 0, 0, tiled=True)]
    ppermute x1 -> x32, waiting for transfers between devices: 4.75 us -> 81.1 us  [along(): return lax.ppermute(x, axis, [(i, (i + step) % size) for i in range(size)])]
    ppermute x1 -> x32, starting transfers between devices: 1.5 us -> 31.7 us  [along(): return lax.ppermute(x, axis, [(i, (i + step) % size) for i in range(size)])]
    pallas_call x5 -> x6, Pallas kernels: 31.2 us -> 24.2 us  [the longest x2 6.57 us: plus_output(): pl.pallas_call(functools.partial(plus_kernel, half), out_shape=jax.ShapeD...]
    all_to_all x0 -> x1, starting transfers between devices: none -> 4.4 us  [exchange(): return lax.all_to_all(x, axes, 0, 0, tiled=True)]
    pallas_call x1, Pallas kernels: 7.3 us -> 3.69 us  [minus_output(): pl.pallas_call(minus_kernel, out_shape=jax.ShapeDtypeStruct((16, 640, 128...]
    reduce_sum x0 -> x1, other arithmetic: none -> 2.91 us  [local(): total = parts.astype(jnp.float32).sum(0).astype(jnp.bfloat16)]
  transfers between devices with their start and end apart: 2 -> 33, of which waited for: 1 -> 16; matrix products, arithmetic and copies ran while one was open for 0% -> 0% of each run, Pallas kernels for 6% -> 6%
where the time goes in v2:
time: 217 us
  waiting for transfers between devices  81.1 us (37%)
  blocking collectives  55.4 us (26%)
  starting transfers between devices  36.1 us (17%)
  Pallas kernels  32.3 us (15%)
  local copies, waits for them, and re-layouts  7.36 us (3%)
  other arithmetic  3.45 us (2%)
    ppermute x32, waiting for transfers between devices, along(): return lax.ppermute(x, axis, [(i, (i + step) % size) for i in range(size)])  81.1 us
    all_to_all x2, blocking collectives, exchange(): return lax.all_to_all(x, axes, 0, 0, tiled=True)  55.4 us
    ppermute x32, starting transfers between devices, along(): return lax.ppermute(x, axis, [(i, (i + step) % size) for i in range(size)])  31.7 us
    pallas_call x2, Pallas kernels, plus_output(): pl.pallas_call(functools.partial(plus_kernel, half), out_shape=jax.ShapeD...  6.57 us
    pallas_call x1, Pallas kernels, minus_product(): pl.pallas_call(minus_product_kernel, out_shape=jax.ShapeDtypeStruct((8, 2...  6.22 us
    pallas_call x2, Pallas kernels, first_transform(): pl.pallas_call(functools.partial(first_kernel, by_z), out_shape=[jax.Shap...  5.95 us
    pallas_call x1, Pallas kernels, start_product(): pl.pallas_call(functools.partial(start_product_kernel, counts), out_shape...  5.43 us
    pallas_call x1, Pallas kernels, middle(): pl.pallas_call(lambda d, *refs: middle_kernel(*refs), out_shape=(jax.Shap...  4.43 us
  transfers between devices with their start and end apart: 33, of which 16 were waited for; matrix products, arithmetic and copies ran while one was open for 0% of the time, Pallas kernels for 6%

profile of v2, /device:TPU:1, one launch (start us, length us, event | category | flops | bytes accessed | tf_op | source)
XLA Modules:
  0.0 216.5 jit_solution(8998554893685737277)
XLA Ops:
  0.6 1.9 fusion.6
  4.1 2.7 %collective-permute-done.4.xo_ref = bf16[16,320,128]{2,1,0:T(8,128)(2,1)} collective-permute-done((bf16[16,320,128]{2,1,0:T(8,128)(2,1)S(1)}, bf16[16,320,128]{2,1,0:T(8,128)(2,1)}, u32[]{:S(2)}, u32[]{:S(2)}) %collective-permute-start.4) | collective-permute-done | bytes 1310752 | tf_op jit(solution)/shard_map/ppermute | solution.py:378
  6.8 2.2 %copy-done.3 = bf16[16,2,256,256]{3,2,1,0:T(8,128)(2,1)S(1)} copy-done((bf16[16,2,256,256]{3,2,1,0:T(8,128)(2,1)S(1)}, bf16[16,2,256,256]{3,2,1,0:T(8,128)(2,1)}, u32[]{:S(2)}) %copy-start.3) | copy-done | bytes 4194328
  9.0 3.0 %first_transform.3 = (bf16[4,2,320,128]{3,2,1,0:T(8,128)(2,1)S(1)}, bf16[4,2,320,128]{3,2,1,0:T(8,128)(2,1)S(1)}) custom-call(s32[1]{0:T(128)} %bitcast.dev_ref.d, bf16[16,320,128]{2,1,0:T(8,128)(2,1)S(1)} %get-tuple-element.66.x_ref, bf16[16,320,128]{2,1,0:T(8,128)(2,1)} %collective-permute-done.4.xo_ref, bf16[16,2,256,256]{3,2,1,0:T(8,128)(2,1)S(1)} %copy-done.3), custom_call_target="tpu_custom_call" | custom-call | flops 734003200 | bytes 6291456 | tf_op jit(solution)/shard_map/first_transform/pallas_call | solution.py:113
  12.1 2.9 %collective-permute-start.5 = (bf16[4,2,320,128]{3,2,1,0:T(8,128)(2,1)S(1)}, bf16[4,2,320,128]{3,2,1,0:T(8,128)(2,1)S(1)}, u32[]{:S(2)}, u32[]{:S(2)}) collective-permute-start(bf16[4,2,320,128]{3,2,1,0:T(8,128)(2,1)S(1)} %get-tuple-element.38), channel_id=1, source_target_pairs={{0,16},{16,0},{1,17},{17,1},{2,18},{18,2},{3,19},{19,3},{4,20},{20... | collective-permute-start | bytes 1966088 | tf_op jit(solution)/shard_map/ppermute | solution.py:378
  15.0 2.2 %copy-done.4 = bf16[16,2,256,256]{3,2,1,0:T(8,128)(2,1)S(1)} copy-done((bf16[16,2,256,256]{3,2,1,0:T(8,128)(2,1)S(1)}, bf16[16,2,256,256]{3,2,1,0:T(8,128)(2,1)}, u32[]{:S(2)}) %copy-start.4) | copy-done | bytes 4194328
  17.2 2.9 %first_transform.2 = (bf16[2,2,320,128]{3,2,1,0:T(8,128)(2,1)S(1)}, bf16[2,2,320,128]{3,2,1,0:T(8,128)(2,1)S(1)}, bf16[2,2,320,128]{3,2,1,0:T(8,128)(2,1)S(1)}, bf16[2,2,320,128]{3,2,1,0:T(8,128)(2,1)S(1)}) custom-call(s32[1]{0:T(128)} %bitcast.dev_ref.d, bf16[16,320,128]{2,1,0:T(8,128)(2,1)S(1)} %get-tuple-element.67.x_ref, ...), custom_call_target="tpu_custom_call" | custom-call | flops 734003200 | bytes 6291456 | tf_op jit(solution)/shard_map/first_transform/pallas_call | solution.py:113
  21.8 3.3 %collective-permute-start.2 = (bf16[2,2,320,128]{3,2,1,0:T(8,128)(2,1)S(1)}, bf16[2,2,320,128]{3,2,1,0:T(8,128)(2,1)S(1)}, u32[]{:S(2)}, u32[]{:S(2)}) collective-permute-start(bf16[2,2,320,128]{3,2,1,0:T(8,128)(2,1)S(1)} %get-tuple-element.36), channel_id=1, source_target_pairs={{0,64},{32,96},{64,0},{96,32},{1,65},{33,97},{65,1},{97,33},{2,66}... | collective-permute-start | bytes 983048 | tf_op jit(solution)/shard_map/ppermute | solution.py:378
  25.8 5.5 %collective-permute-done.1 = bf16[2,2,320,128]{3,2,1,0:T(8,128)(2,1)S(1)} collective-permute-done((bf16[2,2,320,128]{3,2,1,0:T(8,128)(2,1)S(1)}, bf16[2,2,320,128]{3,2,1,0:T(8,128)(2,1)S(1)}, u32[]{:S(2)}, u32[]{:S(2)}) %collective-permute-start.1) | collective-permute-done | bytes 327712 | tf_op jit(solution)/shard_map/ppermute | solution.py:378
  31.4 7.9 %collective-permute-done.2 = bf16[2,2,320,128]{3,2,1,0:T(8,128)(2,1)S(1)} collective-permute-done((bf16[2,2,320,128]{3,2,1,0:T(8,128)(2,1)S(1)}, bf16[2,2,320,128]{3,2,1,0:T(8,128)(2,1)S(1)}, u32[]{:S(2)}, u32[]{:S(2)}) %collective-permute-start.2) | collective-permute-done | bytes 327712 | tf_op jit(solution)/shard_map/ppermute | solution.py:378
  39.4 3.0 %collective-permute-start.9 = (bf16[2,320,128]{2,1,0:T(8,128)(2,1)S(1)}, bf16[2,320,128]{2,1,0:T(8,128)(2,1)S(1)}, u32[]{:S(2)}, u32[]{:S(2)}) collective-permute-start(bf16[2,320,128]{2,1,0:T(8,128)(2,1)S(1)} %get-tuple-element.68), channel_id=1, source_target_pairs={{0,96},{32,0},{64,32},{96,64},{1,97},{33,1},{65,33},{97,65},{2,98}... | collective-permute-start | bytes 491528 | tf_op jit(solution)/shard_map/ppermute | solution.py:378
  44.3 4.8 %collective-permute-done.9.refs_5_ = bf16[2,320,128]{2,1,0:T(8,128)(2,1)S(1)} collective-permute-done((bf16[2,320,128]{2,1,0:T(8,128)(2,1)S(1)}, bf16[2,320,128]{2,1,0:T(8,128)(2,1)S(1)}, u32[]{:S(2)}, u32[]{:S(2)}) %collective-permute-start.9) | collective-permute-done | bytes 163872 | tf_op jit(solution)/shard_map/ppermute | solution.py:378
  49.1 4.4 %collective-permute-done.7.refs_3_ = bf16[2,320,128]{2,1,0:T(8,128)(2,1)S(1)} collective-permute-done((bf16[2,320,128]{2,1,0:T(8,128)(2,1)S(1)}, bf16[2,320,128]{2,1,0:T(8,128)(2,1)S(1)}, u32[]{:S(2)}, u32[]{:S(2)}) %collective-permute-start.7) | collective-permute-done | bytes 163872 | tf_op jit(solution)/shard_map/ppermute | solution.py:378
  53.6 5.4 %start_product.1 = bf16[128,2,40,128]{3,2,1,0:T(8,128)(2,1)S(1)} custom-call(bf16[2,320,128]{2,1,0:T(8,128)(2,1)S(1)} %get-tuple-element.73.refs_0_, bf16[2,320,128]{2,1,0:T(8,128)(2,1)S(1)} %collective-permute-done.6.refs_1_, bf16[2,320,128]{2,1,0:T(8,128)(2,1)S(1)} %get-tuple-element.71.refs_2_, bf16[2,320,128]{2,1,0:T(8,128)(2,1)S(1)} %collective-permute-done.7.refs_3_, ...), custom_call_target="tpu_custom_call" | custom-call | flops 4294967296 | bytes 18874368 | tf_op jit(solution)/shard_map/start_product/pallas_call | solution.py:162
  59.0 40.8 %all_to_all.15 = bf16[128,2,40,128]{3,2,1,0:T(8,128)(2,1)S(1)} all-to-all(bf16[128,2,40,128]{3,2,1,0:T(8,128)(2,1)S(1)} %start_product.1), channel_id=1, replica_groups=mesh['z'=4,'xh'=2,'core'=2,'y'=4,'xl'=2] {'y','xl','z','xh','core'}, dimensions={0} | all-to-all | bytes 5242880 | tf_op jit(solution)/shard_map/all_to_all | solution.py:373
  99.9 4.4 %middle.1 = (bf16[32,40,128]{2,1,0:T(8,128)(2,1)S(1)}, bf16[16,2,40,128]{3,2,1,0:T(8,128)(2,1)S(1)}) custom-call(s32[1]{0:T(128)} %bitcast.dev_ref.d, bf16[8,16,2,40,128]{4,3,2,1,0:T(8,128)(2,1)S(1)} %bitcast.26, s32[16,40,128]{2,1,0:T(8,128)S(1)} %bitcast.24, bf16[8,256,256]{2,1,0:T(8,128)(2,1)S(1)} %copy-done.8, bf16[8,256,256]{2,1,0:T(8,128)(2,1)S(1)} %copy-done.7), custom_call_target="tpu_custom_call" | custom-call | flops 2147483648 | bytes 8388608 | tf_op jit(solution)/shard_map/middle/pallas_call | solution.py:266
  105.9 14.6 %all_to_all.16.s_ref = bf16[16,2,40,128]{3,2,1,0:T(8,128)(2,1)S(1)} all-to-all(bf16[16,2,40,128]{3,2,1,0:T(8,128)(2,1)S(1)} %get-tuple-element.45), channel_id=1, replica_groups=mesh['z'=4,'xh'=2,'core'=2,'y'=4,'xl'=2] {'z','xh','core'}, dimensions={0} | all-to-all | bytes 655360 | tf_op jit(solution)/shard_map/all_to_all | solution.py:373
  120.5 6.2 %minus_product.1 = bf16[8,2,640,128]{3,2,1,0:T(8,128)(2,1)} custom-call(bf16[16,2,40,128]{3,2,1,0:T(8,128)(2,1)S(1)} %all_to_all.16.s_ref, bf16[2,1,5120,640]{3,2,1,0:T(8,128)(2,1)S(1)} %copy-done), custom_call_target="tpu_custom_call" | custom-call | flops 4294967296 | bytes 18874368 | tf_op jit(solution)/shard_map/minus_product/pallas_call | solution.py:194
  126.8 4.4 %all-to-all-start.2 = ((bf16[8,2,640,128]{3,2,1,0:T(8,128)(2,1)}), bf16[8,2,640,128]{3,2,1,0:T(8,128)(2,1)}, u32[]{:S(2)}, u32[]{:S(2)}) async-start(bf16[8,2,640,128]{3,2,1,0:T(8,128)(2,1)} %minus_product.1), calls=%async_computation.2 | async-start | bytes 5242880 | tf_op jit(solution)/shard_map/all_to_all | solution.py:373
  133.5 12.9 %collective-permute-done.13.refs_3_ = bf16[2,32,40,128]{3,2,1,0:T(8,128)(2,1)S(1)} collective-permute-done((bf16[2,32,40,128]{3,2,1,0:T(8,128)(2,1)S(1)}, bf16[2,32,40,128]{3,2,1,0:T(8,128)(2,1)S(1)}, u32[]{:S(2)}, u32[]{:S(2)}) %collective-permute-start.13) | collective-permute-done | bytes 655392 | tf_op jit(solution)/shard_map/ppermute | solution.py:378
  146.5 2.3 %collective-permute-done.12.refs_2_ = bf16[2,32,40,128]{3,2,1,0:T(8,128)(2,1)S(1)} collective-permute-done((bf16[2,32,40,128]{3,2,1,0:T(8,128)(2,1)S(1)}, bf16[2,32,40,128]{3,2,1,0:T(8,128)(2,1)S(1)}, u32[]{:S(2)}, u32[]{:S(2)}) %collective-permute-start.12) | collective-permute-done | bytes 655392 | tf_op jit(solution)/shard_map/ppermute | solution.py:378
  148.8 15.6 %collective-permute-done.11.refs_1_ = bf16[2,32,40,128]{3,2,1,0:T(8,128)(2,1)} collective-permute-done((bf16[2,32,40,128]{3,2,1,0:T(8,128)(2,1)S(1)}, bf16[2,32,40,128]{3,2,1,0:T(8,128)(2,1)}, u32[]{:S(2)}, u32[]{:S(2)}) %collective-permute-start.11) | collective-permute-done | bytes 655392 | tf_op jit(solution)/shard_map/ppermute | solution.py:378
  164.4 2.9 %reduce_sum.12 = bf16[2,640,128]{2,1,0:T(8,128)(2,1)} reduce(bf16[8,2,640,128]{3,2,1,0:T(8,128)(2,1)} %all-to-all-done.2, bf16[]{:T(256)} %constant.31.clone.1), dimensions={0}, to_apply=%region_0.0 | reduce | flops 1146880 | bytes 2949122 | tf_op jit(solution)/shard_map/reduce_sum | solution.py:422
  171.3 4.0 %collective-permute-done.18 = bf16[2,320,128]{2,1,0:T(8,128)(2,1)S(1)} collective-permute-done((bf16[2,320,128]{2,1,0:T(8,128)(2,1)S(1)}, bf16[2,320,128]{2,1,0:T(8,128)(2,1)S(1)}, u32[]{:S(2)}, u32[]{:S(2)}) %collective-permute-start.18) | collective-permute-done | bytes 163872 | tf_op jit(solution)/shard_map/ppermute | solution.py:378
  176.2 5.0 %collective-permute-done.19 = bf16[2,320,128]{2,1,0:T(8,128)(2,1)S(1)} collective-permute-done((bf16[2,320,128]{2,1,0:T(8,128)(2,1)S(1)}, bf16[2,320,128]{2,1,0:T(8,128)(2,1)S(1)}, u32[]{:S(2)}, u32[]{:S(2)}) %collective-permute-start.19) | collective-permute-done | bytes 163872 | tf_op jit(solution)/shard_map/ppermute | solution.py:378
  181.8 1.8 collective-permute-start.14
  186.0 7.0 %collective-permute-done.25.refs_3_ = bf16[2,2,320,128]{3,2,1,0:T(8,128)(2,1)S(1)} collective-permute-done((bf16[2,2,320,128]{3,2,1,0:T(8,128)(2,1)S(1)}, bf16[2,2,320,128]{3,2,1,0:T(8,128)(2,1)S(1)}, u32[]{:S(2)}, u32[]{:S(2)}) %collective-permute-start.25) | collective-permute-done | bytes 327712 | tf_op jit(solution)/shard_map/ppermute | solution.py:378
  195.1 1.8 collective-permute-start.16
  196.9 5.8 %collective-permute-done.23.refs_1_ = bf16[2,2,320,128]{3,2,1,0:T(8,128)(2,1)S(1)} collective-permute-done((bf16[2,2,320,128]{3,2,1,0:T(8,128)(2,1)S(1)}, bf16[2,2,320,128]{3,2,1,0:T(8,128)(2,1)S(1)}, u32[]{:S(2)}, u32[]{:S(2)}) %collective-permute-start.23) | collective-permute-done | bytes 327712 | tf_op jit(solution)/shard_map/ppermute | solution.py:378
  206.2 3.7 %minus_output.1 = bf16[16,640,128]{2,1,0:T(8,128)(2,1)} custom-call(s32[1]{0:T(128)} %bitcast.dev_ref.d, bf16[2,32,40,128]{3,2,1,0:T(8,128)(2,1)S(1)} %pad_maximum_fusion.refs_0_, bf16[2,32,40,128]{3,2,1,0:T(8,128)(2,1)} %collective-permute-done.11.refs_1_, bf16[2,32,40,128]{3,2,1,0:T(8,128)(2,1)S(1)} %collective-permute-done.12.refs_2_, ...), custom_call_target="tpu_custom_call" | custom-call | flops 734003200 | bytes 8388608 | tf_op jit(solution)/shard_map/minus_output/pallas_call | solution.py:304
  209.9 3.3 %plus_output.2.refs_11_ = bf16[16,640,128]{2,1,0:T(8,128)(2,1)} custom-call(s32[1]{0:T(128)} %bitcast.dev_ref.d, bf16[4,2,320,128]{3,2,1,0:T(8,128)(2,1)S(1)} %pad_maximum_fusion.1.refs_0_, bf16[4,2,320,128]{3,2,1,0:T(8,128)(2,1)S(1)} %collective-permute-done.22.refs_1_, bf16[4,2,320,128]{3,2,1,0:T(8,128)(2,1)S(1)} %collective-permute-done.30.refs_2_, ...), custom_call_target="tpu_custom_call" | custom-call | flops 734003200 | bytes 6291456 | tf_op jit(solution)/shard_map/plus_output/pallas_call | solution.py:350
  213.2 3.3 %plus_output.3 = bf16[16,640,128]{2,1,0:T(8,128)(2,1)} custom-call(s32[1]{0:T(128)} %bitcast.dev_ref.d, bf16[2,2,320,128]{3,2,1,0:T(8,128)(2,1)S(1)} %pad_maximum_fusion.2.refs_0_, bf16[2,2,320,128]{3,2,1,0:T(8,128)(2,1)S(1)} %collective-permute-done.23.refs_1_, ...), custom_call_target="tpu_custom_call", output_to_operand_aliasing={{}: (12, {})} | custom-call | flops 734003200 | bytes 6291456 | tf_op jit(solution)/shard_map/plus_output/pallas_call | solution.py:350
  (70 shorter events, 23.7 us)
Async XLA Ops:
  2.5 4.3 %collective-permute-start.4 = (bf16[16,320,128]{2,1,0:T(8,128)(2,1)S(1)}, bf16[16,320,128]{2,1,0:T(8,128)(2,1)}, u32[]{:S(2)}, u32[]{:S(2)}) collective-permute-start(bf16[16,320,128]{2,1,0:T(8,128)(2,1)S(1)} %get-tuple-element.66.x_ref), channel_id=1, source_target_pairs={{0,8},{8,0},{1,9},{9,1},{2,10},{10,2},{3,11},{11,3},{4,12},{12,4},... | collective-permute-start | bytes 3932168 | tf_op jit(solution)/shard_map/ppermute | solution.py:378
  4.0 10.9 %collective-permute-start = (bf16[16,320,128]{2,1,0:T(8,128)(2,1)S(1)}, bf16[16,320,128]{2,1,0:T(8,128)(2,1)}, u32[]{:S(2)}, u32[]{:S(2)}) collective-permute-start(bf16[16,320,128]{2,1,0:T(8,128)(2,1)S(1)} %get-tuple-element.67.x_ref), channel_id=1, source_target_pairs={{0,8},{8,0},{1,9},{9,1},{2,10},{10,2},{3,11},{11,3},{4,12},{12,4},... | collective-permute-start | bytes 3932168 | tf_op jit(solution)/shard_map/ppermute | solution.py:378
  12.1 27.2 %collective-permute-start.5 = (bf16[4,2,320,128]{3,2,1,0:T(8,128)(2,1)S(1)}, bf16[4,2,320,128]{3,2,1,0:T(8,128)(2,1)S(1)}, u32[]{:S(2)}, u32[]{:S(2)}) collective-permute-start(bf16[4,2,320,128]{3,2,1,0:T(8,128)(2,1)S(1)} %get-tuple-element.38), channel_id=1, source_target_pairs={{0,16},{16,0},{1,17},{17,1},{2,18},{18,2},{3,19},{19,3},{4,20},{20... | collective-permute-start | bytes 1966088 | tf_op jit(solution)/shard_map/ppermute | solution.py:378
  20.1 11.3 %collective-permute-start.1 = (bf16[2,2,320,128]{3,2,1,0:T(8,128)(2,1)S(1)}, bf16[2,2,320,128]{3,2,1,0:T(8,128)(2,1)S(1)}, u32[]{:S(2)}, u32[]{:S(2)}) collective-permute-start(bf16[2,2,320,128]{3,2,1,0:T(8,128)(2,1)S(1)} %get-tuple-element.35), channel_id=1, source_target_pairs={{0,32},{32,64},{64,96},{96,0},{1,33},{33,65},{65,97},{97,1},{2,34}... | collective-permute-start | bytes 983048 | tf_op jit(solution)/shard_map/ppermute | solution.py:378
  21.8 17.5 %collective-permute-start.2 = (bf16[2,2,320,128]{3,2,1,0:T(8,128)(2,1)S(1)}, bf16[2,2,320,128]{3,2,1,0:T(8,128)(2,1)S(1)}, u32[]{:S(2)}, u32[]{:S(2)}) collective-permute-start(bf16[2,2,320,128]{3,2,1,0:T(8,128)(2,1)S(1)} %get-tuple-element.36), channel_id=1, source_target_pairs={{0,64},{32,96},{64,0},{96,32},{1,65},{33,97},{65,1},{97,33},{2,66}... | collective-permute-start | bytes 983048 | tf_op jit(solution)/shard_map/ppermute | solution.py:378
  25.1 14.2 %collective-permute-start.3 = (bf16[2,2,320,128]{3,2,1,0:T(8,128)(2,1)S(1)}, bf16[2,2,320,128]{3,2,1,0:T(8,128)(2,1)S(1)}, u32[]{:S(2)}, u32[]{:S(2)}) collective-permute-start(bf16[2,2,320,128]{3,2,1,0:T(8,128)(2,1)S(1)} %get-tuple-element.37), channel_id=1, source_target_pairs={{0,96},{32,0},{64,32},{96,64},{1,97},{33,1},{65,33},{97,65},{2,98}... | collective-permute-start | bytes 983048 | tf_op jit(solution)/shard_map/ppermute | solution.py:378
  39.4 9.7 %collective-permute-start.9 = (bf16[2,320,128]{2,1,0:T(8,128)(2,1)S(1)}, bf16[2,320,128]{2,1,0:T(8,128)(2,1)S(1)}, u32[]{:S(2)}, u32[]{:S(2)}) collective-permute-start(bf16[2,320,128]{2,1,0:T(8,128)(2,1)S(1)} %get-tuple-element.68), channel_id=1, source_target_pairs={{0,96},{32,0},{64,32},{96,64},{1,97},{33,1},{65,33},{97,65},{2,98}... | collective-permute-start | bytes 491528 | tf_op jit(solution)/shard_map/ppermute | solution.py:378
  42.4 6.7 %collective-permute-start.8 = (bf16[2,320,128]{2,1,0:T(8,128)(2,1)S(1)}, bf16[2,320,128]{2,1,0:T(8,128)(2,1)S(1)}, u32[]{:S(2)}, u32[]{:S(2)}) collective-permute-start(bf16[2,320,128]{2,1,0:T(8,128)(2,1)S(1)} %get-tuple-element.69), channel_id=1, source_target_pairs={{0,64},{32,96},{64,0},{96,32},{1,65},{33,97},{65,1},{97,33},{2,66}... | collective-permute-start | bytes 491528 | tf_op jit(solution)/shard_map/ppermute | solution.py:378
  42.9 10.7 %collective-permute-start.7 = (bf16[2,320,128]{2,1,0:T(8,128)(2,1)S(1)}, bf16[2,320,128]{2,1,0:T(8,128)(2,1)S(1)}, u32[]{:S(2)}, u32[]{:S(2)}) collective-permute-start(bf16[2,320,128]{2,1,0:T(8,128)(2,1)S(1)} %get-tuple-element.70), channel_id=1, source_target_pairs={{0,32},{32,64},{64,96},{96,0},{1,33},{33,65},{65,97},{97,1},{2,34}... | collective-permute-start | bytes 491528 | tf_op jit(solution)/shard_map/ppermute | solution.py:378
  43.3 10.3 %collective-permute-start.6 = (bf16[2,320,128]{2,1,0:T(8,128)(2,1)S(1)}, bf16[2,320,128]{2,1,0:T(8,128)(2,1)S(1)}, u32[]{:S(2)}, u32[]{:S(2)}) collective-permute-start(bf16[2,320,128]{2,1,0:T(8,128)(2,1)S(1)} %get-tuple-element.72), channel_id=1, source_target_pairs={{0,16},{16,0},{1,17},{17,1},{2,18},{18,2},{3,19},{19,3},{4,20},{20... | collective-permute-start | bytes 491528 | tf_op jit(solution)/shard_map/ppermute | solution.py:378
  104.3 16.2 %collective-permute-start.10 = (bf16[32,40,128]{2,1,0:T(8,128)(2,1)S(1)}, bf16[32,40,128]{2,1,0:T(8,128)(2,1)S(1)}, u32[]{:S(2)}, u32[]{:S(2)}) collective-permute-start(bf16[32,40,128]{2,1,0:T(8,128)(2,1)S(1)} %get-tuple-element.46), channel_id=1, source_target_pairs={{0,16},{16,0},{1,17},{17,1},{2,18},{18,2},{3,19},{19,3},{4,20},{20... | collective-permute-start | bytes 983048 | tf_op jit(solution)/shard_map/ppermute | solution.py:378
  126.8 37.6 %all-to-all-start.2 = ((bf16[8,2,640,128]{3,2,1,0:T(8,128)(2,1)}), bf16[8,2,640,128]{3,2,1,0:T(8,128)(2,1)}, u32[]{:S(2)}, u32[]{:S(2)}) async-start(bf16[8,2,640,128]{3,2,1,0:T(8,128)(2,1)} %minus_product.1), calls=%async_computation.2 | async-start | bytes 5242880 | tf_op jit(solution)/shard_map/all_to_all | solution.py:373
  131.2 15.2 %collective-permute-start.13 = (bf16[2,32,40,128]{3,2,1,0:T(8,128)(2,1)S(1)}, bf16[2,32,40,128]{3,2,1,0:T(8,128)(2,1)S(1)}, u32[]{:S(2)}, u32[]{:S(2)}) collective-permute-start(bf16[2,32,40,128]{3,2,1,0:T(8,128)(2,1)S(1)} %pad_maximum_fusion.refs_0_), channel_id=1, source_target_pairs={{0,96},{32,0},{64,32},{96,64},{1,97},{33,1},{65,33},{97,65},{2,98}... | collective-permute-start | bytes 1966088 | tf_op jit(solution)/shard_map/ppermute | solution.py:378
  132.1 16.7 %collective-permute-start.12 = (bf16[2,32,40,128]{3,2,1,0:T(8,128)(2,1)S(1)}, bf16[2,32,40,128]{3,2,1,0:T(8,128)(2,1)S(1)}, u32[]{:S(2)}, u32[]{:S(2)}) collective-permute-start(bf16[2,32,40,128]{3,2,1,0:T(8,128)(2,1)S(1)} %pad_maximum_fusion.refs_0_), channel_id=1, source_target_pairs={{0,64},{32,96},{64,0},{96,32},{1,65},{33,97},{65,1},{97,33},{2,66}... | collective-permute-start | bytes 1966088 | tf_op jit(solution)/shard_map/ppermute | solution.py:378
  133.3 31.1 %collective-permute-start.11 = (bf16[2,32,40,128]{3,2,1,0:T(8,128)(2,1)S(1)}, bf16[2,32,40,128]{3,2,1,0:T(8,128)(2,1)}, u32[]{:S(2)}, u32[]{:S(2)}) collective-permute-start(bf16[2,32,40,128]{3,2,1,0:T(8,128)(2,1)S(1)} %pad_maximum_fusion.refs_0_), channel_id=1, source_target_pairs={{0,32},{32,64},{64,96},{96,0},{1,33},{33,65},{65,97},{97,1},{2,34}... | collective-permute-start | bytes 1966088 | tf_op jit(solution)/shard_map/ppermute | solution.py:378
  168.4 6.9 %collective-permute-start.18 = (bf16[2,320,128]{2,1,0:T(8,128)(2,1)S(1)}, bf16[2,320,128]{2,1,0:T(8,128)(2,1)S(1)}, u32[]{:S(2)}, u32[]{:S(2)}) collective-permute-start(bf16[2,320,128]{2,1,0:T(8,128)(2,1)S(1)} %get-tuple-element.76), channel_id=1, source_target_pairs={{0,16},{16,0},{1,17},{17,1},{2,18},{18,2},{3,19},{19,3},{4,20},{20... | collective-permute-start | bytes 491528 | tf_op jit(solution)/shard_map/ppermute | solution.py:378
  169.7 5.6 %collective-permute-start.21 = (bf16[2,320,128]{2,1,0:T(8,128)(2,1)S(1)}, bf16[2,320,128]{2,1,0:T(8,128)(2,1)S(1)}, u32[]{:S(2)}, u32[]{:S(2)}) collective-permute-start(bf16[2,320,128]{2,1,0:T(8,128)(2,1)S(1)} %get-tuple-element.56), channel_id=1, source_target_pairs={{0,96},{32,0},{64,32},{96,64},{1,97},{33,1},{65,33},{97,65},{2,98}... | collective-permute-start | bytes 491528 | tf_op jit(solution)/shard_map/ppermute | solution.py:378
  170.2 6.0 %collective-permute-start.20 = (bf16[2,320,128]{2,1,0:T(8,128)(2,1)S(1)}, bf16[2,320,128]{2,1,0:T(8,128)(2,1)S(1)}, u32[]{:S(2)}, u32[]{:S(2)}) collective-permute-start(bf16[2,320,128]{2,1,0:T(8,128)(2,1)S(1)} %get-tuple-element.56), channel_id=1, source_target_pairs={{0,64},{32,96},{64,0},{96,32},{1,65},{33,97},{65,1},{97,33},{2,66}... | collective-permute-start | bytes 491528 | tf_op jit(solution)/shard_map/ppermute | solution.py:378
  171.0 10.1 %collective-permute-start.19 = (bf16[2,320,128]{2,1,0:T(8,128)(2,1)S(1)}, bf16[2,320,128]{2,1,0:T(8,128)(2,1)S(1)}, u32[]{:S(2)}, u32[]{:S(2)}) collective-permute-start(bf16[2,320,128]{2,1,0:T(8,128)(2,1)S(1)} %get-tuple-element.56), channel_id=1, source_target_pairs={{0,32},{32,64},{64,96},{96,0},{1,33},{33,65},{65,97},{97,1},{2,34}... | collective-permute-start | bytes 491528 | tf_op jit(solution)/shard_map/ppermute | solution.py:378
  181.2 22.0 %collective-permute-start.22 = (bf16[4,2,320,128]{3,2,1,0:T(8,128)(2,1)S(1)}, bf16[4,2,320,128]{3,2,1,0:T(8,128)(2,1)S(1)}, u32[]{:S(2)}, u32[]{:S(2)}) collective-permute-start(bf16[4,2,320,128]{3,2,1,0:T(8,128)(2,1)S(1)} %pad_maximum_fusion.1.refs_0_), channel_id=1, source_target_pairs={{0,16},{16,0},{1,17},{17,1},{2,18},{18,2},{3,19},{19,3},{4,20},{20... | collective-permute-start | bytes 1966088 | tf_op jit(solution)/shard_map/ppermute | solution.py:378
  181.8 21.5 %collective-permute-start.14 = (bf16[2,32,40,128]{3,2,1,0:T(8,128)(2,1)S(1)}, bf16[2,32,40,128]{3,2,1,0:T(8,128)(2,1)S(1)}, u32[]{:S(2)}, u32[]{:S(2)}) collective-permute-start(bf16[2,32,40,128]{3,2,1,0:T(8,128)(2,1)S(1)} %pad_maximum_fusion.refs_0_), channel_id=1, source_target_pairs={{0,8},{8,0},{1,9},{9,1},{2,10},{10,2},{3,11},{11,3},{4,12},{12,4},... | collective-permute-start | bytes 1966088 | tf_op jit(solution)/shard_map/ppermute | solution.py:378
  183.6 9.4 %collective-permute-start.25 = (bf16[2,2,320,128]{3,2,1,0:T(8,128)(2,1)S(1)}, bf16[2,2,320,128]{3,2,1,0:T(8,128)(2,1)S(1)}, u32[]{:S(2)}, u32[]{:S(2)}) collective-permute-start(bf16[2,2,320,128]{3,2,1,0:T(8,128)(2,1)S(1)} %pad_maximum_fusion.2.refs_0_), channel_id=1, source_target_pairs={{0,96},{32,0},{64,32},{96,64},{1,97},{33,1},{65,33},{97,65},{2,98}... | collective-permute-start | bytes 983048 | tf_op jit(solution)/shard_map/ppermute | solution.py:378
  184.6 10.6 %collective-permute-start.24 = (bf16[2,2,320,128]{3,2,1,0:T(8,128)(2,1)S(1)}, bf16[2,2,320,128]{3,2,1,0:T(8,128)(2,1)S(1)}, u32[]{:S(2)}, u32[]{:S(2)}) collective-permute-start(bf16[2,2,320,128]{3,2,1,0:T(8,128)(2,1)S(1)} %pad_maximum_fusion.2.refs_0_), channel_id=1, source_target_pairs={{0,64},{32,96},{64,0},{96,32},{1,65},{33,97},{65,1},{97,33},{2,66}... | collective-permute-start | bytes 983048 | tf_op jit(solution)/shard_map/ppermute | solution.py:378
  185.5 17.2 %collective-permute-start.23 = (bf16[2,2,320,128]{3,2,1,0:T(8,128)(2,1)S(1)}, bf16[2,2,320,128]{3,2,1,0:T(8,128)(2,1)S(1)}, u32[]{:S(2)}, u32[]{:S(2)}) collective-permute-start(bf16[2,2,320,128]{3,2,1,0:T(8,128)(2,1)S(1)} %pad_maximum_fusion.2.refs_0_), channel_id=1, source_target_pairs={{0,32},{32,64},{64,96},{96,0},{1,33},{33,65},{65,97},{97,1},{2,34}... | collective-permute-start | bytes 983048 | tf_op jit(solution)/shard_map/ppermute | solution.py:378
  193.0 10.7 %collective-permute-start.15 = (bf16[2,32,40,128]{3,2,1,0:T(8,128)(2,1)}, bf16[2,32,40,128]{3,2,1,0:T(8,128)(2,1)S(1)}, u32[]{:S(2)}, u32[]{:S(2)}) collective-permute-start(bf16[2,32,40,128]{3,2,1,0:T(8,128)(2,1)} %collective-permute-done.11.refs_1_), channel_id=1, source_target_pairs={{0,8},{8,0},{1,9},{9,1},{2,10},{10,2},{3,11},{11,3},{4,12},{12,4},... | collective-permute-start | bytes 1966088 | tf_op jit(solution)/shard_map/ppermute | solution.py:378
  195.1 8.7 %collective-permute-start.16 = (bf16[2,32,40,128]{3,2,1,0:T(8,128)(2,1)S(1)}, bf16[2,32,40,128]{3,2,1,0:T(8,128)(2,1)S(1)}, u32[]{:S(2)}, u32[]{:S(2)}) collective-permute-start(bf16[2,32,40,128]{3,2,1,0:T(8,128)(2,1)S(1)} %collective-permute-done.12.refs_2_), channel_id=1, source_target_pairs={{0,8},{8,0},{1,9},{9,1},{2,10},{10,2},{3,11},{11,3},{4,12},{12,4},... | collective-permute-start | bytes 1966088 | tf_op jit(solution)/shard_map/ppermute | solution.py:378
  203.2 2.7 %collective-permute-start.30 = (bf16[4,2,320,128]{3,2,1,0:T(8,128)(2,1)S(1)}, bf16[4,2,320,128]{3,2,1,0:T(8,128)(2,1)S(1)}, u32[]{:S(2)}, u32[]{:S(2)}) collective-permute-start(bf16[4,2,320,128]{3,2,1,0:T(8,128)(2,1)S(1)} %pad_maximum_fusion.1.refs_0_), channel_id=1, source_target_pairs={{0,8},{8,0},{1,9},{9,1},{2,10},{10,2},{3,11},{11,3},{4,12},{12,4},... | collective-permute-start | bytes 1966088 | tf_op jit(solution)/shard_map/ppermute | solution.py:378
  203.2 6.7 %collective-permute-start.31 = (bf16[4,2,320,128]{3,2,1,0:T(8,128)(2,1)S(1)}, bf16[4,2,320,128]{3,2,1,0:T(8,128)(2,1)S(1)}, u32[]{:S(2)}, u32[]{:S(2)}) collective-permute-start(bf16[4,2,320,128]{3,2,1,0:T(8,128)(2,1)S(1)} %collective-permute-done.22.refs_1_), channel_id=1, source_target_pairs={{0,8},{8,0},{1,9},{9,1},{2,10},{10,2},{3,11},{11,3},{4,12},{12,4},... | collective-permute-start | bytes 1966088 | tf_op jit(solution)/shard_map/ppermute | solution.py:378
  203.7 9.5 %collective-permute-start.26 = (bf16[2,2,320,128]{3,2,1,0:T(8,128)(2,1)S(1)}, bf16[2,2,320,128]{3,2,1,0:T(8,128)(2,1)S(1)}, u32[]{:S(2)}, u32[]{:S(2)}) collective-permute-start(bf16[2,2,320,128]{3,2,1,0:T(8,128)(2,1)S(1)} %pad_maximum_fusion.2.refs_0_), channel_id=1, source_target_pairs={{0,8},{8,0},{1,9},{9,1},{2,10},{10,2},{3,11},{11,3},{4,12},{12,4},... | collective-permute-start | bytes 983048 | tf_op jit(solution)/shard_map/ppermute | solution.py:378
  203.8 9.4 %collective-permute-start.27 = (bf16[2,2,320,128]{3,2,1,0:T(8,128)(2,1)S(1)}, bf16[2,2,320,128]{3,2,1,0:T(8,128)(2,1)S(1)}, u32[]{:S(2)}, u32[]{:S(2)}) collective-permute-start(bf16[2,2,320,128]{3,2,1,0:T(8,128)(2,1)S(1)} %collective-permute-done.23.refs_1_), channel_id=1, source_target_pairs={{0,8},{8,0},{1,9},{9,1},{2,10},{10,2},{3,11},{11,3},{4,12},{12,4},... | collective-permute-start | bytes 983048 | tf_op jit(solution)/shard_map/ppermute | solution.py:378
  204.9 8.3 %collective-permute-start.28 = (bf16[2,2,320,128]{3,2,1,0:T(8,128)(2,1)S(1)}, bf16[2,2,320,128]{3,2,1,0:T(8,128)(2,1)S(1)}, u32[]{:S(2)}, u32[]{:S(2)}) collective-permute-start(bf16[2,2,320,128]{3,2,1,0:T(8,128)(2,1)S(1)} %collective-permute-done.24.refs_2_), channel_id=1, source_target_pairs={{0,8},{8,0},{1,9},{9,1},{2,10},{10,2},{3,11},{11,3},{4,12},{12,4},... | collective-permute-start | bytes 983048 | tf_op jit(solution)/shard_map/ppermute | solution.py:378
  205.9 7.3 %collective-permute-start.29 = (bf16[2,2,320,128]{3,2,1,0:T(8,128)(2,1)S(1)}, bf16[2,2,320,128]{3,2,1,0:T(8,128)(2,1)S(1)}, u32[]{:S(2)}, u32[]{:S(2)}) collective-permute-start(bf16[2,2,320,128]{3,2,1,0:T(8,128)(2,1)S(1)} %collective-permute-done.25.refs_3_), channel_id=1, source_target_pairs={{0,8},{8,0},{1,9},{9,1},{2,10},{10,2},{3,11},{11,3},{4,12},{12,4},... | collective-permute-start | bytes 983048 | tf_op jit(solution)/shard_map/ppermute | solution.py:378
  (10 other events, 301.4 us)

commit v3 on v2

--- a/solution.py
+++ b/solution.py
@@ -55,7 +55,7 @@
         other = np.arange((dev ^ 1) * 16, (dev ^ 1) * 16 + 16)
         freqs = [frequency(z + dz, xh + e, core) for dz in range(4) for e in range(2)]
         part = table[freqs].reshape(16, NT)
-        blocks.append(np.stack([spread(part[:, own], 16), spread(part[:, other], 16)]))
+        blocks.append(spread(part[:, np.concatenate([own, other])], 16))
     return np.stack(blocks)
 
 
@@ -84,7 +84,7 @@
     return jnp.dot(a, b, preferred_element_type=jnp.float32)
 
 
-def params(mib=24):
+def params(mib=16):
     return pltpu.CompilerParams(vmem_limit_bytes=mib * MIB)
 
 
@@ -95,34 +95,58 @@
 HALF = 320
 
 
-def first_kernel(by_z, dev_ref, x_ref, xo_ref, w_ref, *out_refs):
+def of_device(table, dev):
+    return lax.dynamic_index_in_dim(jnp.asarray(table), dev[0], 0, keepdims=False)
+
+
+def first_kernel(by_z, x_ref, xo_ref, w_ref, *out_refs):
     rows = x_ref.shape[1]
-    for at in range(0, rows, 16):
-        own = x_ref[:, at : at + 16, :].reshape(256, 128)
-        other = xo_ref[:, at : at + 16, :].reshape(256, 128)
-        part = dot(w_ref[0, 0], own) + dot(w_ref[0, 1], other)
-        part = part.astype(jnp.bfloat16).reshape(4, 2, 2, 16, 128)
-        for i, out_ref in enumerate(out_refs):
-            out_ref[:, :, at : at + 16, :] = part[i] if by_z else part[:, i]
-
-
-def first_transform(dev, x, xo, by_z):
+    for at in range(0, rows, 32):
+        sides = []
+        for here in (slice(at, at + 16), slice(at + 16, at + 32)):
+            both = [x_ref[:, here, :].reshape(256, 128), xo_ref[:, here, :].reshape(256, 128)]
+            sides.append(jnp.concatenate(both, axis=0))
+        both = dot(w_ref[...], jnp.concatenate(sides, axis=1)).astype(jnp.bfloat16)
+        for side in range(2):
+            part = both[:, side * 128 : side * 128 + 128].reshape(4, 2, 2, 16, 128)
+            here = slice(at + side * 16, at + side * 16 + 16)
+            for i, out_ref in enumerate(out_refs):
+                out_ref[:, :, here, :] = part[i] if by_z else part[:, i]
+
+
+def copy_kernel(x_ref, out_ref):
+    out_ref[...] = x_ref[...]
+
+
+def copied(x):
+    spec = pl.BlockSpec((x.shape[0] // 4,) + x.shape[1:], lambda i: (i, 0, 0))
+    return pl.pallas_call(
+        copy_kernel,
+        out_shape=jax.ShapeDtypeStruct(x.shape, x.dtype),
+        grid=(4,),
+        in_specs=[spec],
+        out_specs=spec,
+        compiler_params=params(),
+        cost_estimate=cost(0, 6 << 20),
+        name="copied",
+    )(x)
+
+
+def first_transform(weights, x, xo, half, by_z):
     step = 160
-    spec = pl.BlockSpec((16, step, 128), lambda i, d: (0, i, 0))
+    start = half * HALF // step
+    spec = pl.BlockSpec((16, step, 128), lambda i: (0, i + start, 0))
     count, lead = (4, 2) if by_z else (2, 4)
     return pl.pallas_call(
         functools.partial(first_kernel, by_z),
         out_shape=[jax.ShapeDtypeStruct((lead, 2, HALF, 128), jnp.bfloat16)] * count,
-        grid_spec=pltpu.PrefetchScalarGridSpec(
-            num_scalar_prefetch=1,
-            grid=(HALF // step,),
-            in_specs=[spec, spec, pl.BlockSpec((1, 2, 256, 256), lambda i, d: (d[0], 0, 0, 0))],
-            out_specs=[pl.BlockSpec((lead, 2, step, 128), lambda i, d: (0, 0, i, 0))] * count,
-        ),
+        grid=(HALF // step,),
+        in_specs=[spec, spec, pl.BlockSpec((256, 512), lambda i: (0, 0))],
+        out_specs=[pl.BlockSpec((lead, 2, step, 128), lambda i: (0, 0, i, 0))] * count,
         compiler_params=params(),
         cost_estimate=cost(700 << 20, 6 << 20),
         name="first_transform",
-    )(dev, x, xo, jnp.asarray(first_weights()))
+    )(x, xo, weights)
 
 
 def total_of(refs):
@@ -193,7 +217,7 @@
     rows = 1280
     return pl.pallas_call(
         minus_product_kernel,
-        out_shape=jax.ShapeDtypeStruct((8, 2, 640, 128), jnp.bfloat16),
+        out_shape=pltpu.HBM((8, 2, 640, 128), jnp.bfloat16),
         grid=(5120 // rows,),
         in_specs=[
             pl.BlockSpec(spectra.shape, lambda i: (0, 0, 0, 0)),
@@ -205,6 +229,28 @@
         cost_estimate=cost(4 << 30, 18 << 20),
         name="minus_product",
     )(spectra, reflection)
+
+
+def sum_kernel(p_ref, a_ref, b_ref):
+    total = p_ref[0].astype(jnp.float32)
+    for i in range(1, 8):
+        total = total + p_ref[i].astype(jnp.float32)
+    total = total.astype(jnp.bfloat16)
+    a_ref[...] = total[:, :HALF]
+    b_ref[...] = total[:, HALF:]
+
+
+def summed_halves(parts):
+    return pl.pallas_call(
+        sum_kernel,
+        out_shape=[jax.ShapeDtypeStruct((2, HALF, 128), jnp.bfloat16)] * 2,
+        grid=(2,),
+        in_specs=[pl.BlockSpec((8, 1, 640, 128), lambda i: (0, i, 0, 0))],
+        out_specs=[pl.BlockSpec((1, HALF, 128), lambda i: (i, 0, 0))] * 2,
+        compiler_params=params(),
+        cost_estimate=cost(1 << 20, 3 << 20),
+        name="summed_halves",
+    )(parts)
 
 
 def lanes(rows):
@@ -243,11 +289,11 @@
 
     def body(i, carry):
         field = dot(wi_ref[i], flat)
-        minus = kept(field, i * 32, onsets).astype(jnp.bfloat16)
+        minus = kept(field, i * 64, onsets).astype(jnp.bfloat16)
         acc[...] += dot(wf_ref[i], minus)
         return carry
 
-    lax.fori_loop(0, 8, body, 0)
+    lax.fori_loop(0, 4, body, 0)
     out_ref[...] = unlanes(acc[...]).astype(jnp.bfloat16).reshape(NF, 2, 40, 128)
 
 
@@ -261,8 +307,8 @@
 
 
 def middle(dev, parts, onsets):
-    wi = jnp.asarray(inverse_weights(32))
-    wf = jnp.asarray(forward_weights(32))
+    wi = jnp.asarray(inverse_weights(64))
+    wf = jnp.asarray(forward_weights(64))
     return pl.pallas_call(
         lambda d, *refs: middle_kernel(*refs),
         out_shape=(
@@ -283,24 +329,23 @@
 
 
 def minus_kernel(dev_ref, *refs):
-    mine, others, onset_ref, w_ref, out_ref = refs[:4], refs[4:8], refs[8], refs[9], refs[10]
+    p_refs, onset_ref, w_ref, out_ref = refs[:8], refs[8], refs[9], refs[10]
     dev = dev_ref[0]
     z, xh, core = lax.div(dev, 4), lax.rem(lax.div(dev, 2), 2), lax.rem(dev, 2)
     for k in range(4):
         for e in range(2):
             chip = lax.rem(z + 4 - k, 4) * 2 + lax.rem(xh + e, 2)
             pieces = []
-            for ref, at in ((mine[k], core), (others[k], 1 - core)):
-                flat = lanes(ref[e].astype(jnp.float32)).astype(jnp.bfloat16)
-                pieces.append(unlanes(kept(dot(w_ref[0], flat), dev * 16, onset_ref[chip * 2 + at])))
+            for c, at in ((0, core), (1, 1 - core)):
+                flat = lanes(p_refs[c * 4 + k][e].astype(jnp.float32)).astype(jnp.bfloat16)
+                pieces.append(unlanes(kept(dot(w_ref[...], flat), dev * 16, onset_ref[chip * 2 + at])))
             swap = core == 1
             both = [jnp.where(swap, pieces[1], pieces[0]), jnp.where(swap, pieces[0], pieces[1])]
             rows = pl.ds(pl.multiple_of(chip * 80, 16), 80)
             out_ref[:, rows, :] = jnp.concatenate(both, axis=1).astype(jnp.bfloat16)
 
 
-def minus_output(dev, mine, others, onsets):
-    weights = jnp.asarray(inverse_weights(16))
+def minus_output(dev, parts, onsets, weights):
     return pl.pallas_call(
         minus_kernel,
         out_shape=jax.ShapeDtypeStruct((16, 640, 128), jnp.bfloat16),
@@ -308,13 +353,13 @@
             num_scalar_prefetch=1,
             grid=(1,),
             in_specs=[whole((2, 2 * NF, 40, 128))] * 8
-            + [whole((16, 40, 128)), pl.BlockSpec((1, 128, 256), lambda i, d: (d[0], 0, 0))],
+            + [whole((16, 40, 128)), whole((128, 256))],
             out_specs=whole((16, 640, 128)),
         ),
         compiler_params=params(),
         cost_estimate=cost(700 << 20, 8 << 20),
         name="minus_output",
-    )(dev, *mine, *others, onsets, weights)
+    )(dev, *parts, onsets, weights)
 
 
 def plus_kernel(half, dev_ref, *refs):
@@ -332,7 +377,7 @@
             else:
                 flat = [p_refs[c * 2 + e][k, :, here, :] for c in range(2) for e in range(2) for k in range(4)]
             sides.append(jnp.concatenate([piece.reshape(32, 128) for piece in flat], axis=0))
-        field = dot(w_ref[0], jnp.concatenate(sides, axis=1))
+        field = dot(w_ref[...], jnp.concatenate(sides, axis=1))
         for i in range(2):
             here = slice(at + i * 16, at + i * 16 + 16)
             side = field[:, i * 128 : i * 128 + 128].reshape(16, 16, 128)
@@ -340,10 +385,9 @@
             out_ref[:, here, :] = (x_ref[:, here, :].astype(jnp.float32) + update).astype(jnp.bfloat16)
 
 
-def plus_output(dev, half, parts, onsets, x, held):
-    step = 64
+def plus_output(dev, half, parts, onsets, x, weights, held):
+    step = 160
     start = half * HALF // step
-    weights = jnp.asarray(last_weights())
     lead = 2 if half else 4
     time_spec = pl.BlockSpec((16, step, 128), lambda i, d: (0, i + start, 0))
     operands = [dev, *parts, onsets, x, weights] + ([held] if half else [])
@@ -357,7 +401,7 @@
             + [
                 pl.BlockSpec((step, 128), lambda i, d: (i + start, 0)),
                 time_spec,
-                pl.BlockSpec((1, 256, 512), lambda i, d: (d[0], 0, 0)),
+                whole((256, 512)),
             ]
             + ([pl.BlockSpec(memory_space=pl.ANY)] if half else []),
             out_specs=time_spec,
@@ -389,10 +433,13 @@
 
 
 def start_spectra(dev, x):
-    xa, xb = x[:, :HALF], x[:, HALF:]
-    xoa, xob = along(xa, "core", 1), along(xb, "core", 1)
-    a_got = around(first_transform(dev, xa, xoa, True), "z")
-    b_own, b_send = first_transform(dev, xb, xob, False)
+    weights = of_device(first_weights(), dev)
+    xo = along(x, "core", 1)
+    x = copied(x)
+    a_send = first_transform(weights, x, xo, 0, True)
+    a_send, xo = together(a_send, xo)
+    a_got = around(a_send, "z")
+    b_own, b_send = first_transform(weights, x, xo, 1, False)
     b_got = along(b_send, "xh", 1)
     a_got, b_got = together(a_got, b_got)
     a_keep, a_pass = [add(*[got[e] for got in a_got]) for e in range(2)]
@@ -403,6 +450,11 @@
 def around(parts, axis):
     got = {k: along(parts[k], axis, k) for k in STEPS}
     return [parts[0], got[1], got[2], got[3]]
+
+
+def rest_of(near):
+    mine = around([near] * 4, "z")
+    return mine, [along(v, "core", 1) for v in mine[:3]]
 
 
 def together(*groups):
@@ -417,21 +469,22 @@
     summed, spectra = middle(dev, start_parts.reshape(8, NF, 2, 40, 128), blocks)
     spectra, far = together(exchange(spectra, FREQ), along(summed, "xh", 1))
     parts, near = together(minus_product(spectra, reflection), jnp.stack([summed, far]))
-    parts, mine = together(exchange(parts, SRC), around([near] * 4, "z"))
-
-    total = parts.astype(jnp.float32).sum(0).astype(jnp.bfloat16)
-    a, b = total[:, :HALF], total[:, HALF:]
-    b_far, a_near = along(b, "xh", 1), around([a] * 4, "z")
-    others = [along(v, "core", 1) for v in mine]
-    b_far, a_near = together(b_far, a_near)
+    parts, mine, others = together(exchange(parts, SRC), *rest_of(near))
+
+    a, b = summed_halves(parts)
+    weights = of_device(inverse_weights(16), dev), of_device(last_weights(), dev)
+    last = along(mine[3], "core", 1)
+    b_far, a_near, last, weights = together(along(b, "xh", 1), around([a] * 4, "z"), last, weights)
     a_near, b_near = jnp.stack(a_near), jnp.stack([b, b_far])
-    a_far, b_all = together(along(a_near, "xh", 1), around([b_near] * 4, "z"))
-    minus_field = minus_output(dev, mine, others, blocks)
+    gathered = [pltpu.with_memory_space_constraint(v, pltpu.HBM) for v in (*mine, *others, last)]
+    minus_field = minus_output(dev, gathered, blocks, weights[0])
+    a_far, b_all = along(a_near, "xh", 1), around([b_near] * 4, "z")
+    a_far, b_all, minus_field = together(a_far, b_all, minus_field)
     a_all, b_all = [a_near, a_far], list(b_all)
     a_all = a_all + [along(v, "core", 1) for v in a_all]
     b_all = b_all + [along(v, "core", 1) for v in b_all]
-    plus_field = plus_output(dev, 0, a_all, onsets, focus_start, None)
-    plus_field = plus_output(dev, 1, b_all, onsets, focus_start, plus_field)
+    plus_field = plus_output(dev, 0, a_all, onsets, focus_start, weights[1], None)
+    plus_field = plus_output(dev, 1, b_all, onsets, focus_start, weights[1], plus_field)
     return minus_field, plus_field
 
 

time: 217 us -> 199 us (0.917)
  waiting for transfers between devices: 81.1 us -> 65.9 us
  starting transfers between devices: 36.1 us -> 38.5 us
    ppermute x32 -> x31, waiting for transfers between devices: 81.1 us -> 65.9 us  [along(): return lax.ppermute(x, axis, [(i, (i + step) % size) for i in range(size)])]
    ppermute x32 -> x31, starting transfers between devices: 31.7 us -> 34.9 us  [along(): return lax.ppermute(x, axis, [(i, (i + step) % size) for i in range(size)])]
    reduce_sum x1 -> x0, other arithmetic: 2.91 us -> none  [local(): total = parts.astype(jnp.float32).sum(0).astype(jnp.bfloat16)]
    squeeze x0 -> x3, local copies, waits for them, and re-layouts: none -> 2.79 us  [of_device(): lax.dynamic_index_in_dim(jnp.asarray(table), dev[0], 0, keepdims=False)]
    unnamed x18 -> x24, local copies, waits for them, and re-layouts: 4.42 us -> 3.63 us
    pallas_call x1 -> x3, Pallas kernels: 6.22 us -> 7 us  [the longest x1 6.22 us: minus_product(): pl.pallas_call(minus_product_kernel, out_shape=pltpu.HBM((8, 2, 640, 128)...]
  transfers between devices with their start and end apart: 33 -> 32, of which waited for: 16 -> 12; matrix products, arithmetic and copies ran while one was open for 0% -> 2% of each run, Pallas kernels for 6% -> 4%
where the time goes in v3:
time: 199 us; the launch traced here: 198 us
  waiting for transfers between devices  65.9 us (33%)
  blocking collectives  55.2 us (28%)
  starting transfers between devices  38.5 us (19%)
  Pallas kernels  30.2 us (15%)
  local copies, waits for them, and re-layouts  6.41 us (3%)
    ppermute x31, waiting for transfers between devices, along(): return lax.ppermute(x, axis, [(i, (i + step) % size) for i in range(size)])  65.9 us
    all_to_all x2, blocking collectives, exchange(): return lax.all_to_all(x, axes, 0, 0, tiled=True)  55.2 us
    ppermute x31, starting transfers between devices, along(): return lax.ppermute(x, axis, [(i, (i + step) % size) for i in range(size)])  34.9 us
    pallas_call x1, Pallas kernels, minus_product(): pl.pallas_call(minus_product_kernel, out_shape=pltpu.HBM((8, 2, 640, 128)...  6.22 us
    pallas_call x1, Pallas kernels, start_product(): pl.pallas_call(functools.partial(start_product_kernel, counts), out_shape...  5.43 us
    pallas_call x2, Pallas kernels, first_transform(): pl.pallas_call(functools.partial(first_kernel, by_z), out_shape=[jax.Shap...  5.32 us
    pallas_call x1, Pallas kernels, minus_output(): pl.pallas_call(minus_kernel, out_shape=jax.ShapeDtypeStruct((16, 640, 128...  5.06 us
    pallas_call x2, Pallas kernels, plus_output(): pl.pallas_call(functools.partial(plus_kernel, half), out_shape=jax.ShapeD...  4.44 us
  transfers between devices with their start and end apart: 32, of which 12 were waited for; matrix products, arithmetic and copies ran while one was open for 2% of the time, Pallas kernels for 4%

profile of v3, /device:TPU:1, one launch (start us, length us, event | category | flops | bytes accessed | tf_op | source)
XLA Modules:
  0.0 198.4 jit_solution(17366944473315636065)
XLA Ops:
  0.6 1.5 collective-permute-start
  2.1 1.7 copy-done.1
  5.1 1.9 collective-permute-done.xo_ref
  7.0 2.4 %first_transform.2 = (bf16[2,2,320,128]{3,2,1,0:T(8,128)(2,1)S(1)}, bf16[2,2,320,128]{3,2,1,0:T(8,128)(2,1)S(1)}, bf16[2,2,320,128]{3,2,1,0:T(8,128)(2,1)S(1)}, bf16[2,2,320,128]{3,2,1,0:T(8,128)(2,1)S(1)}) custom-call(bf16[16,640,128]{2,1,0:T(8,128)(2,1)S(1)} %copied.1.x_ref, bf16[16,640,128]{2,1,0:T(8,128)(2,1)} %collective-permute-done.xo_ref, ...), custom_call_target="tpu_custom_call" | custom-call | flops 734003200 | bytes 6291456 | tf_op jit(solution)/shard_map/first_transform/pallas_call | solution.py:140
  9.4 2.9 %first_transform.3 = (bf16[4,2,320,128]{3,2,1,0:T(8,128)(2,1)S(1)}, bf16[4,2,320,128]{3,2,1,0:T(8,128)(2,1)S(1)}) custom-call(bf16[16,640,128]{2,1,0:T(8,128)(2,1)S(1)} %copied.1.x_ref, bf16[16,640,128]{2,1,0:T(8,128)(2,1)} %collective-permute-done.xo_ref, bf16[256,512]{1,0:T(8,128)(2,1)S(1)} %dynamic-slice_bitcast_fusion.1.w_ref), custom_call_target="tpu_custom_call" | custom-call | flops 734003200 | bytes 6291456 | tf_op jit(solution)/shard_map/first_transform/pallas_call | solution.py:140
  12.4 2.9 %collective-permute-start.4 = (bf16[4,2,320,128]{3,2,1,0:T(8,128)(2,1)S(1)}, bf16[4,2,320,128]{3,2,1,0:T(8,128)(2,1)S(1)}, u32[]{:S(2)}, u32[]{:S(2)}) collective-permute-start(bf16[4,2,320,128]{3,2,1,0:T(8,128)(2,1)S(1)} %get-tuple-element.57), channel_id=1, source_target_pairs={{0,16},{16,0},{1,17},{17,1},{2,18},{18,2},{3,19},{19,3},{4,20},{20... | collective-permute-start | bytes 1966088 | tf_op jit(solution)/shard_map/ppermute | solution.py:422
  15.3 1.6 collective-permute-start.1
  16.9 3.3 %collective-permute-start.2 = (bf16[2,2,320,128]{3,2,1,0:T(8,128)(2,1)S(1)}, bf16[2,2,320,128]{3,2,1,0:T(8,128)(2,1)S(1)}, u32[]{:S(2)}, u32[]{:S(2)}) collective-permute-start(bf16[2,2,320,128]{3,2,1,0:T(8,128)(2,1)S(1)} %get-tuple-element.54), channel_id=1, source_target_pairs={{0,64},{32,96},{64,0},{96,32},{1,65},{33,97},{65,1},{97,33},{2,66}... | collective-permute-start | bytes 983048 | tf_op jit(solution)/shard_map/ppermute | solution.py:422
  20.9 5.5 %collective-permute-done.1 = bf16[2,2,320,128]{3,2,1,0:T(8,128)(2,1)S(1)} collective-permute-done((bf16[2,2,320,128]{3,2,1,0:T(8,128)(2,1)S(1)}, bf16[2,2,320,128]{3,2,1,0:T(8,128)(2,1)S(1)}, u32[]{:S(2)}, u32[]{:S(2)}) %collective-permute-start.1) | collective-permute-done | bytes 327712 | tf_op jit(solution)/shard_map/ppermute | solution.py:422
  26.5 7.9 %collective-permute-done.2 = bf16[2,2,320,128]{3,2,1,0:T(8,128)(2,1)S(1)} collective-permute-done((bf16[2,2,320,128]{3,2,1,0:T(8,128)(2,1)S(1)}, bf16[2,2,320,128]{3,2,1,0:T(8,128)(2,1)S(1)}, u32[]{:S(2)}, u32[]{:S(2)}) %collective-permute-start.2) | collective-permute-done | bytes 327712 | tf_op jit(solution)/shard_map/ppermute | solution.py:422
  34.5 2.9 %collective-permute-start.8 = (bf16[2,320,128]{2,1,0:T(8,128)(2,1)S(1)}, bf16[2,320,128]{2,1,0:T(8,128)(2,1)S(1)}, u32[]{:S(2)}, u32[]{:S(2)}) collective-permute-start(bf16[2,320,128]{2,1,0:T(8,128)(2,1)S(1)} %get-tuple-element.94), channel_id=1, source_target_pairs={{0,96},{32,0},{64,32},{96,64},{1,97},{33,1},{65,33},{97,65},{2,98}... | collective-permute-start | bytes 491528 | tf_op jit(solution)/shard_map/ppermute | solution.py:422
  38.6 5.6 %collective-permute-done.8.refs_5_ = bf16[2,320,128]{2,1,0:T(8,128)(2,1)S(1)} collective-permute-done((bf16[2,320,128]{2,1,0:T(8,128)(2,1)S(1)}, bf16[2,320,128]{2,1,0:T(8,128)(2,1)S(1)}, u32[]{:S(2)}, u32[]{:S(2)}) %collective-permute-start.8) | collective-permute-done | bytes 163872 | tf_op jit(solution)/shard_map/ppermute | solution.py:422
  44.2 4.4 %collective-permute-done.6.refs_3_ = bf16[2,320,128]{2,1,0:T(8,128)(2,1)S(1)} collective-permute-done((bf16[2,320,128]{2,1,0:T(8,128)(2,1)S(1)}, bf16[2,320,128]{2,1,0:T(8,128)(2,1)S(1)}, u32[]{:S(2)}, u32[]{:S(2)}) %collective-permute-start.6) | collective-permute-done | bytes 163872 | tf_op jit(solution)/shard_map/ppermute | solution.py:422
  48.6 5.4 %start_product.1 = bf16[128,2,40,128]{3,2,1,0:T(8,128)(2,1)S(1)} custom-call(bf16[2,320,128]{2,1,0:T(8,128)(2,1)S(1)} %get-tuple-element.99.refs_0_, bf16[2,320,128]{2,1,0:T(8,128)(2,1)S(1)} %collective-permute-done.5.refs_1_, bf16[2,320,128]{2,1,0:T(8,128)(2,1)S(1)} %get-tuple-element.97.refs_2_, bf16[2,320,128]{2,1,0:T(8,128)(2,1)S(1)} %collective-permute-done.6.refs_3_, ...), custom_call_target="tpu_custom_call" | custom-call | flops 4294967296 | bytes 18874368 | tf_op jit(solution)/shard_map/start_product/pallas_call | solution.py:186
  54.0 40.6 %all_to_all.15 = bf16[128,2,40,128]{3,2,1,0:T(8,128)(2,1)S(1)} all-to-all(bf16[128,2,40,128]{3,2,1,0:T(8,128)(2,1)S(1)} %start_product.1), channel_id=1, replica_groups=mesh['z'=4,'xh'=2,'core'=2,'y'=4,'xl'=2] {'y','xl','z','xh','core'}, dimensions={0} | all-to-all | bytes 5242880 | tf_op jit(solution)/shard_map/all_to_all | solution.py:417
  94.6 2.9 %middle.1 = (bf16[32,40,128]{2,1,0:T(8,128)(2,1)S(1)}, bf16[16,2,40,128]{3,2,1,0:T(8,128)(2,1)S(1)}) custom-call(s32[1]{0:T(128)} %bitcast.d.dev_ref, bf16[8,16,2,40,128]{4,3,2,1,0:T(8,128)(2,1)S(1)} %bitcast.31, s32[16,40,128]{2,1,0:T(8,128)S(1)} %bitcast.29, bf16[4,512,256]{2,1,0:T(8,128)(2,1)S(1)} %copy-done.5, bf16[4,256,512]{2,1,0:T(8,128)(2,1)S(1)} %copy-done.4), custom_call_target="tpu_custom_call" | custom-call | flops 2147483648 | bytes 8388608 | tf_op jit(solution)/shard_map/middle/pallas_call | solution.py:312
  97.5 1.6 collective-permute-start.9
  99.2 14.6 %all_to_all.16.s_ref = bf16[16,2,40,128]{3,2,1,0:T(8,128)(2,1)S(1)} all-to-all(bf16[16,2,40,128]{3,2,1,0:T(8,128)(2,1)S(1)} %get-tuple-element.64), channel_id=1, replica_groups=mesh['z'=4,'xh'=2,'core'=2,'y'=4,'xl'=2] {'z','xh','core'}, dimensions={0} | all-to-all | bytes 655360 | tf_op jit(solution)/shard_map/all_to_all | solution.py:417
  113.8 6.2 %minus_product.1 = bf16[8,2,640,128]{3,2,1,0:T(8,128)(2,1)} custom-call(bf16[16,2,40,128]{3,2,1,0:T(8,128)(2,1)S(1)} %all_to_all.16.s_ref, bf16[2,1,5120,640]{3,2,1,0:T(8,128)(2,1)S(1)} %copy-done), custom_call_target="tpu_custom_call" | custom-call | flops 4294967296 | bytes 18874368 | tf_op jit(solution)/shard_map/minus_product/pallas_call | solution.py:218
  120.9 3.6 %all-to-all-start.2 = ((bf16[8,2,640,128]{3,2,1,0:T(8,128)(2,1)}), bf16[8,2,640,128]{3,2,1,0:T(8,128)(2,1)S(1)}, u32[]{:S(2)}, u32[]{:S(2)}) async-start(bf16[8,2,640,128]{3,2,1,0:T(8,128)(2,1)} %minus_product.1), calls=%async_computation.2 | async-start | bytes 5242880 | tf_op jit(solution)/shard_map/all_to_all | solution.py:417
  126.0 1.5 collective-permute-start.13
  127.5 2.1 %collective-permute-start.12 = (bf16[2,32,40,128]{3,2,1,0:T(8,128)(2,1)}, bf16[2,32,40,128]{3,2,1,0:T(8,128)(2,1)S(1)}, u32[]{:S(2)}, u32[]{:S(2)}) collective-permute-start(bf16[2,32,40,128]{3,2,1,0:T(8,128)(2,1)} %pad_maximum_fusion.refs_0_), channel_id=1, source_target_pairs={{0,96},{32,0},{64,32},{96,64},{1,97},{33,1},{65,33},{97,65},{2,98}... | collective-permute-start | bytes 1966088 | tf_op jit(solution)/shard_map/ppermute | solution.py:422
  129.6 11.8 %collective-permute-done.11.refs_2_ = bf16[2,32,40,128]{3,2,1,0:T(8,128)(2,1)S(1)} collective-permute-done((bf16[2,32,40,128]{3,2,1,0:T(8,128)(2,1)}, bf16[2,32,40,128]{3,2,1,0:T(8,128)(2,1)S(1)}, u32[]{:S(2)}, u32[]{:S(2)}) %collective-permute-start.11) | collective-permute-done | bytes 655392 | tf_op jit(solution)/shard_map/ppermute | solution.py:422
  141.5 3.8 %collective-permute-start.15 = (bf16[2,32,40,128]{3,2,1,0:T(8,128)(2,1)S(1)}, bf16[2,32,40,128]{3,2,1,0:T(8,128)(2,1)S(1)}, u32[]{:S(2)}, u32[]{:S(2)}) collective-permute-start(bf16[2,32,40,128]{3,2,1,0:T(8,128)(2,1)S(1)} %collective-permute-done.11.refs_2_), channel_id=1, source_target_pairs={{0,8},{8,0},{1,9},{9,1},{2,10},{10,2},{3,11},{11,3},{4,12},{12,4},... | collective-permute-start | bytes 1966088 | tf_op jit(solution)/shard_map/ppermute | solution.py:422
  145.2 11.8 %collective-permute-done.10.refs_1_ = bf16[2,32,40,128]{3,2,1,0:T(8,128)(2,1)S(1)} collective-permute-done((bf16[2,32,40,128]{3,2,1,0:T(8,128)(2,1)}, bf16[2,32,40,128]{3,2,1,0:T(8,128)(2,1)S(1)}, u32[]{:S(2)}, u32[]{:S(2)}) %collective-permute-start.10) | collective-permute-done | bytes 655392 | tf_op jit(solution)/shard_map/ppermute | solution.py:422
  165.2 3.6 %collective-permute-done.16 = bf16[2,320,128]{2,1,0:T(8,128)(2,1)S(1)} collective-permute-done((bf16[2,320,128]{2,1,0:T(8,128)(2,1)S(1)}, bf16[2,320,128]{2,1,0:T(8,128)(2,1)S(1)}, u32[]{:S(2)}, u32[]{:S(2)}) %collective-permute-start.16) | collective-permute-done | bytes 163872 | tf_op jit(solution)/shard_map/ppermute | solution.py:422
  168.8 3.1 %collective-permute-done.17 = bf16[2,320,128]{2,1,0:T(8,128)(2,1)S(1)} collective-permute-done((bf16[2,320,128]{2,1,0:T(8,128)(2,1)S(1)}, bf16[2,320,128]{2,1,0:T(8,128)(2,1)S(1)}, u32[]{:S(2)}, u32[]{:S(2)}) %collective-permute-start.17) | collective-permute-done | bytes 163872 | tf_op jit(solution)/shard_map/ppermute | solution.py:422
  175.1 2.0 %collective-permute-start.29 = (bf16[4,2,320,128]{3,2,1,0:T(8,128)(2,1)S(1)}, bf16[4,2,320,128]{3,2,1,0:T(8,128)(2,1)S(1)}, u32[]{:S(2)}, u32[]{:S(2)}) collective-permute-start(bf16[4,2,320,128]{3,2,1,0:T(8,128)(2,1)S(1)} %pad_maximum_fusion.1.refs_0_), channel_id=1, source_target_pairs={{0,8},{8,0},{1,9},{9,1},{2,10},{10,2},{3,11},{11,3},{4,12},{12,4},... | collective-permute-start | bytes 1966088 | tf_op jit(solution)/shard_map/ppermute | solution.py:422
  177.1 5.1 %minus_output.1 = bf16[16,640,128]{2,1,0:T(8,128)(2,1)} custom-call(s32[1]{0:T(128)} %bitcast.d.dev_ref, bf16[2,32,40,128]{3,2,1,0:T(8,128)(2,1)} %pad_maximum_fusion.refs_0_, bf16[2,32,40,128]{3,2,1,0:T(8,128)(2,1)} %copy-done.7, bf16[2,32,40,128]{3,2,1,0:T(8,128)(2,1)} %copy-done.6, bf16[2,32,40,128]{3,2,1,0:T(8,128)(2,1)} %copy-done.9, ...), custom_call_target="tpu_custom_call" | custom-call | flops 734003200 | bytes 8388608 | tf_op jit(solution)/shard_map/minus_output/pallas_call | solution.py:349
  182.7 8.9 %collective-permute-done.22.refs_1_ = bf16[2,2,320,128]{3,2,1,0:T(8,128)(2,1)S(1)} collective-permute-done((bf16[2,2,320,128]{3,2,1,0:T(8,128)(2,1)S(1)}, bf16[2,2,320,128]{3,2,1,0:T(8,128)(2,1)S(1)}, u32[]{:S(2)}, u32[]{:S(2)}) %collective-permute-start.22) | collective-permute-done | bytes 327712 | tf_op jit(solution)/shard_map/ppermute | solution.py:422
  193.9 2.2 %plus_output.2.refs_11_ = bf16[16,640,128]{2,1,0:T(8,128)(2,1)} custom-call(s32[1]{0:T(128)} %bitcast.d.dev_ref, bf16[4,2,320,128]{3,2,1,0:T(8,128)(2,1)S(1)} %pad_maximum_fusion.1.refs_0_, bf16[4,2,320,128]{3,2,1,0:T(8,128)(2,1)S(1)} %collective-permute-done.21.refs_1_, bf16[4,2,320,128]{3,2,1,0:T(8,128)(2,1)S(1)} %collective-permute-done.29.refs_2_, ...), custom_call_target="tpu_custom_call" | custom-call | flops 734003200 | bytes 6291456 | tf_op jit(solution)/shard_map/plus_output/pallas_call | solution.py:394
  196.1 2.3 %plus_output.3 = bf16[16,640,128]{2,1,0:T(8,128)(2,1)} custom-call(s32[1]{0:T(128)} %bitcast.d.dev_ref, bf16[2,2,320,128]{3,2,1,0:T(8,128)(2,1)S(1)} %pad_maximum_fusion.2.refs_0_, bf16[2,2,320,128]{3,2,1,0:T(8,128)(2,1)S(1)} %collective-permute-done.22.refs_1_, ...), custom_call_target="tpu_custom_call", output_to_operand_aliasing={{}: (12, {})} | custom-call | flops 734003200 | bytes 6291456 | tf_op jit(solution)/shard_map/plus_output/pallas_call | solution.py:394
  (76 shorter events, 19.7 us)
Async XLA Ops:
  0.6 6.4 %collective-permute-start = (bf16[16,640,128]{2,1,0:T(8,128)(2,1)}, bf16[16,640,128]{2,1,0:T(8,128)(2,1)}, u32[]{:S(2)}, u32[]{:S(2)}) collective-permute-start(bf16[16,640,128]{2,1,0:T(8,128)(2,1)} %refs_9_.1), channel_id=1, source_target_pairs={{0,8},{8,0},{1,9},{9,1},{2,10},{10,2},{3,11},{11,3},{4,12},{12,4},... | collective-permute-start | bytes 7864328 | tf_op jit(solution)/shard_map/ppermute | solution.py:422
  12.4 22.0 %collective-permute-start.4 = (bf16[4,2,320,128]{3,2,1,0:T(8,128)(2,1)S(1)}, bf16[4,2,320,128]{3,2,1,0:T(8,128)(2,1)S(1)}, u32[]{:S(2)}, u32[]{:S(2)}) collective-permute-start(bf16[4,2,320,128]{3,2,1,0:T(8,128)(2,1)S(1)} %get-tuple-element.57), channel_id=1, source_target_pairs={{0,16},{16,0},{1,17},{17,1},{2,18},{18,2},{3,19},{19,3},{4,20},{20... | collective-permute-start | bytes 1966088 | tf_op jit(solution)/shard_map/ppermute | solution.py:422
  15.3 11.2 %collective-permute-start.1 = (bf16[2,2,320,128]{3,2,1,0:T(8,128)(2,1)S(1)}, bf16[2,2,320,128]{3,2,1,0:T(8,128)(2,1)S(1)}, u32[]{:S(2)}, u32[]{:S(2)}) collective-permute-start(bf16[2,2,320,128]{3,2,1,0:T(8,128)(2,1)S(1)} %get-tuple-element.53), channel_id=1, source_target_pairs={{0,32},{32,64},{64,96},{96,0},{1,33},{33,65},{65,97},{97,1},{2,34}... | collective-permute-start | bytes 983048 | tf_op jit(solution)/shard_map/ppermute | solution.py:422
  16.9 17.5 %collective-permute-start.2 = (bf16[2,2,320,128]{3,2,1,0:T(8,128)(2,1)S(1)}, bf16[2,2,320,128]{3,2,1,0:T(8,128)(2,1)S(1)}, u32[]{:S(2)}, u32[]{:S(2)}) collective-permute-start(bf16[2,2,320,128]{3,2,1,0:T(8,128)(2,1)S(1)} %get-tuple-element.54), channel_id=1, source_target_pairs={{0,64},{32,96},{64,0},{96,32},{1,65},{33,97},{65,1},{97,33},{2,66}... | collective-permute-start | bytes 983048 | tf_op jit(solution)/shard_map/ppermute | solution.py:422
  20.2 14.2 %collective-permute-start.3 = (bf16[2,2,320,128]{3,2,1,0:T(8,128)(2,1)S(1)}, bf16[2,2,320,128]{3,2,1,0:T(8,128)(2,1)S(1)}, u32[]{:S(2)}, u32[]{:S(2)}) collective-permute-start(bf16[2,2,320,128]{3,2,1,0:T(8,128)(2,1)S(1)} %get-tuple-element.55), channel_id=1, source_target_pairs={{0,96},{32,0},{64,32},{96,64},{1,97},{33,1},{65,33},{97,65},{2,98}... | collective-permute-start | bytes 983048 | tf_op jit(solution)/shard_map/ppermute | solution.py:422
  34.5 9.6 %collective-permute-start.8 = (bf16[2,320,128]{2,1,0:T(8,128)(2,1)S(1)}, bf16[2,320,128]{2,1,0:T(8,128)(2,1)S(1)}, u32[]{:S(2)}, u32[]{:S(2)}) collective-permute-start(bf16[2,320,128]{2,1,0:T(8,128)(2,1)S(1)} %get-tuple-element.94), channel_id=1, source_target_pairs={{0,96},{32,0},{64,32},{96,64},{1,97},{33,1},{65,33},{97,65},{2,98}... | collective-permute-start | bytes 491528 | tf_op jit(solution)/shard_map/ppermute | solution.py:422
  37.4 6.7 %collective-permute-start.7 = (bf16[2,320,128]{2,1,0:T(8,128)(2,1)S(1)}, bf16[2,320,128]{2,1,0:T(8,128)(2,1)S(1)}, u32[]{:S(2)}, u32[]{:S(2)}) collective-permute-start(bf16[2,320,128]{2,1,0:T(8,128)(2,1)S(1)} %get-tuple-element.95), channel_id=1, source_target_pairs={{0,64},{32,96},{64,0},{96,32},{1,65},{33,97},{65,1},{97,33},{2,66}... | collective-permute-start | bytes 491528 | tf_op jit(solution)/shard_map/ppermute | solution.py:422
  37.8 10.8 %collective-permute-start.6 = (bf16[2,320,128]{2,1,0:T(8,128)(2,1)S(1)}, bf16[2,320,128]{2,1,0:T(8,128)(2,1)S(1)}, u32[]{:S(2)}, u32[]{:S(2)}) collective-permute-start(bf16[2,320,128]{2,1,0:T(8,128)(2,1)S(1)} %get-tuple-element.96), channel_id=1, source_target_pairs={{0,32},{32,64},{64,96},{96,0},{1,33},{33,65},{65,97},{97,1},{2,34}... | collective-permute-start | bytes 491528 | tf_op jit(solution)/shard_map/ppermute | solution.py:422
  38.3 10.3 %collective-permute-start.5 = (bf16[2,320,128]{2,1,0:T(8,128)(2,1)S(1)}, bf16[2,320,128]{2,1,0:T(8,128)(2,1)S(1)}, u32[]{:S(2)}, u32[]{:S(2)}) collective-permute-start(bf16[2,320,128]{2,1,0:T(8,128)(2,1)S(1)} %get-tuple-element.98), channel_id=1, source_target_pairs={{0,16},{16,0},{1,17},{17,1},{2,18},{18,2},{3,19},{19,3},{4,20},{20... | collective-permute-start | bytes 491528 | tf_op jit(solution)/shard_map/ppermute | solution.py:422
  97.5 16.2 %collective-permute-start.9 = (bf16[32,40,128]{2,1,0:T(8,128)(2,1)S(1)}, bf16[32,40,128]{2,1,0:T(8,128)(2,1)S(1)}, u32[]{:S(2)}, u32[]{:S(2)}) collective-permute-start(bf16[32,40,128]{2,1,0:T(8,128)(2,1)S(1)} %get-tuple-element.65), channel_id=1, source_target_pairs={{0,16},{16,0},{1,17},{17,1},{2,18},{18,2},{3,19},{19,3},{4,20},{20... | collective-permute-start | bytes 983048 | tf_op jit(solution)/shard_map/ppermute | solution.py:422
  120.9 38.5 %all-to-all-start.2 = ((bf16[8,2,640,128]{3,2,1,0:T(8,128)(2,1)}), bf16[8,2,640,128]{3,2,1,0:T(8,128)(2,1)S(1)}, u32[]{:S(2)}, u32[]{:S(2)}) async-start(bf16[8,2,640,128]{3,2,1,0:T(8,128)(2,1)} %minus_product.1), calls=%async_computation.2 | async-start | bytes 5242880 | tf_op jit(solution)/shard_map/all_to_all | solution.py:417
  124.6 16.9 %collective-permute-start.11 = (bf16[2,32,40,128]{3,2,1,0:T(8,128)(2,1)}, bf16[2,32,40,128]{3,2,1,0:T(8,128)(2,1)S(1)}, u32[]{:S(2)}, u32[]{:S(2)}) collective-permute-start(bf16[2,32,40,128]{3,2,1,0:T(8,128)(2,1)} %pad_maximum_fusion.refs_0_), channel_id=1, source_target_pairs={{0,64},{32,96},{64,0},{96,32},{1,65},{33,97},{65,1},{97,33},{2,66}... | collective-permute-start | bytes 1966088 | tf_op jit(solution)/shard_map/ppermute | solution.py:422
  126.0 31.1 %collective-permute-start.10 = (bf16[2,32,40,128]{3,2,1,0:T(8,128)(2,1)}, bf16[2,32,40,128]{3,2,1,0:T(8,128)(2,1)S(1)}, u32[]{:S(2)}, u32[]{:S(2)}) collective-permute-start(bf16[2,32,40,128]{3,2,1,0:T(8,128)(2,1)} %pad_maximum_fusion.refs_0_), channel_id=1, source_target_pairs={{0,32},{32,64},{64,96},{96,0},{1,33},{33,65},{65,97},{97,1},{2,34}... | collective-permute-start | bytes 1966088 | tf_op jit(solution)/shard_map/ppermute | solution.py:422
  126.0 31.5 %collective-permute-start.13 = (bf16[2,32,40,128]{3,2,1,0:T(8,128)(2,1)}, bf16[2,32,40,128]{3,2,1,0:T(8,128)(2,1)S(1)}, u32[]{:S(2)}, u32[]{:S(2)}) collective-permute-start(bf16[2,32,40,128]{3,2,1,0:T(8,128)(2,1)} %pad_maximum_fusion.refs_0_), channel_id=1, source_target_pairs={{0,8},{8,0},{1,9},{9,1},{2,10},{10,2},{3,11},{11,3},{4,12},{12,4},... | collective-permute-start | bytes 1966088 | tf_op jit(solution)/shard_map/ppermute | solution.py:422
  127.5 30.0 %collective-permute-start.12 = (bf16[2,32,40,128]{3,2,1,0:T(8,128)(2,1)}, bf16[2,32,40,128]{3,2,1,0:T(8,128)(2,1)S(1)}, u32[]{:S(2)}, u32[]{:S(2)}) collective-permute-start(bf16[2,32,40,128]{3,2,1,0:T(8,128)(2,1)} %pad_maximum_fusion.refs_0_), channel_id=1, source_target_pairs={{0,96},{32,0},{64,32},{96,64},{1,97},{33,1},{65,33},{97,65},{2,98}... | collective-permute-start | bytes 1966088 | tf_op jit(solution)/shard_map/ppermute | solution.py:422
  141.5 16.1 %collective-permute-start.15 = (bf16[2,32,40,128]{3,2,1,0:T(8,128)(2,1)S(1)}, bf16[2,32,40,128]{3,2,1,0:T(8,128)(2,1)S(1)}, u32[]{:S(2)}, u32[]{:S(2)}) collective-permute-start(bf16[2,32,40,128]{3,2,1,0:T(8,128)(2,1)S(1)} %collective-permute-done.11.refs_2_), channel_id=1, source_target_pairs={{0,8},{8,0},{1,9},{9,1},{2,10},{10,2},{3,11},{11,3},{4,12},{12,4},... | collective-permute-start | bytes 1966088 | tf_op jit(solution)/shard_map/ppermute | solution.py:422
  157.1 2.4 %collective-permute-start.14 = (bf16[2,32,40,128]{3,2,1,0:T(8,128)(2,1)S(1)}, bf16[2,32,40,128]{3,2,1,0:T(8,128)(2,1)}, u32[]{:S(2)}, u32[]{:S(2)}) collective-permute-start(bf16[2,32,40,128]{3,2,1,0:T(8,128)(2,1)S(1)} %collective-permute-done.10.refs_1_), channel_id=1, source_target_pairs={{0,8},{8,0},{1,9},{9,1},{2,10},{10,2},{3,11},{11,3},{4,12},{12,4},... | collective-permute-start | bytes 1966088 | tf_op jit(solution)/shard_map/ppermute | solution.py:422
  159.4 12.4 %collective-permute-start.20 = (bf16[2,32,40,128]{3,2,1,0:T(8,128)(2,1)}, bf16[2,32,40,128]{3,2,1,0:T(8,128)(2,1)S(1)}, u32[]{:S(2)}, u32[]{:S(2)}) collective-permute-start(bf16[2,32,40,128]{3,2,1,0:T(8,128)(2,1)} %copy-done.9), channel_id=1, source_target_pairs={{0,8},{8,0},{1,9},{9,1},{2,10},{10,2},{3,11},{11,3},{4,12},{12,4},... | collective-permute-start | bytes 1966088 | tf_op jit(solution)/shard_map/ppermute | solution.py:422
  160.3 8.5 %collective-permute-start.19 = (bf16[2,320,128]{2,1,0:T(8,128)(2,1)S(1)}, bf16[2,320,128]{2,1,0:T(8,128)(2,1)S(1)}, u32[]{:S(2)}, u32[]{:S(2)}) collective-permute-start(bf16[2,320,128]{2,1,0:T(8,128)(2,1)S(1)} %get-tuple-element.74), channel_id=1, source_target_pairs={{0,96},{32,0},{64,32},{96,64},{1,97},{33,1},{65,33},{97,65},{2,98}... | collective-permute-start | bytes 491528 | tf_op jit(solution)/shard_map/ppermute | solution.py:422
  160.7 8.1 %collective-permute-start.18 = (bf16[2,320,128]{2,1,0:T(8,128)(2,1)S(1)}, bf16[2,320,128]{2,1,0:T(8,128)(2,1)S(1)}, u32[]{:S(2)}, u32[]{:S(2)}) collective-permute-start(bf16[2,320,128]{2,1,0:T(8,128)(2,1)S(1)} %get-tuple-element.74), channel_id=1, source_target_pairs={{0,64},{32,96},{64,0},{96,32},{1,65},{33,97},{65,1},{97,33},{2,66}... | collective-permute-start | bytes 491528 | tf_op jit(solution)/shard_map/ppermute | solution.py:422
  162.1 9.8 %collective-permute-start.17 = (bf16[2,320,128]{2,1,0:T(8,128)(2,1)S(1)}, bf16[2,320,128]{2,1,0:T(8,128)(2,1)S(1)}, u32[]{:S(2)}, u32[]{:S(2)}) collective-permute-start(bf16[2,320,128]{2,1,0:T(8,128)(2,1)S(1)} %get-tuple-element.74), channel_id=1, source_target_pairs={{0,32},{32,64},{64,96},{96,0},{1,33},{33,65},{65,97},{97,1},{2,34}... | collective-permute-start | bytes 491528 | tf_op jit(solution)/shard_map/ppermute | solution.py:422
  162.6 6.2 %collective-permute-start.16 = (bf16[2,320,128]{2,1,0:T(8,128)(2,1)S(1)}, bf16[2,320,128]{2,1,0:T(8,128)(2,1)S(1)}, u32[]{:S(2)}, u32[]{:S(2)}) collective-permute-start(bf16[2,320,128]{2,1,0:T(8,128)(2,1)S(1)} %get-tuple-element.71), channel_id=1, source_target_pairs={{0,16},{16,0},{1,17},{17,1},{2,18},{18,2},{3,19},{19,3},{4,20},{20... | collective-permute-start | bytes 491528 | tf_op jit(solution)/shard_map/ppermute | solution.py:422
  172.0 19.7 %collective-permute-start.21 = (bf16[4,2,320,128]{3,2,1,0:T(8,128)(2,1)S(1)}, bf16[4,2,320,128]{3,2,1,0:T(8,128)(2,1)S(1)}, u32[]{:S(2)}, u32[]{:S(2)}) collective-permute-start(bf16[4,2,320,128]{3,2,1,0:T(8,128)(2,1)S(1)} %pad_maximum_fusion.1.refs_0_), channel_id=1, source_target_pairs={{0,16},{16,0},{1,17},{17,1},{2,18},{18,2},{3,19},{19,3},{4,20},{20... | collective-permute-start | bytes 1966088 | tf_op jit(solution)/shard_map/ppermute | solution.py:422
  173.3 8.9 %collective-permute-start.24 = (bf16[2,2,320,128]{3,2,1,0:T(8,128)(2,1)S(1)}, bf16[2,2,320,128]{3,2,1,0:T(8,128)(2,1)S(1)}, u32[]{:S(2)}, u32[]{:S(2)}) collective-permute-start(bf16[2,2,320,128]{3,2,1,0:T(8,128)(2,1)S(1)} %pad_maximum_fusion.2.refs_0_), channel_id=1, source_target_pairs={{0,96},{32,0},{64,32},{96,64},{1,97},{33,1},{65,33},{97,65},{2,98}... | collective-permute-start | bytes 983048 | tf_op jit(solution)/shard_map/ppermute | solution.py:422
  173.5 9.2 %collective-permute-start.23 = (bf16[2,2,320,128]{3,2,1,0:T(8,128)(2,1)S(1)}, bf16[2,2,320,128]{3,2,1,0:T(8,128)(2,1)S(1)}, u32[]{:S(2)}, u32[]{:S(2)}) collective-permute-start(bf16[2,2,320,128]{3,2,1,0:T(8,128)(2,1)S(1)} %pad_maximum_fusion.2.refs_0_), channel_id=1, source_target_pairs={{0,64},{32,96},{64,0},{96,32},{1,65},{33,97},{65,1},{97,33},{2,66}... | collective-permute-start | bytes 983048 | tf_op jit(solution)/shard_map/ppermute | solution.py:422
  174.4 17.3 %collective-permute-start.22 = (bf16[2,2,320,128]{3,2,1,0:T(8,128)(2,1)S(1)}, bf16[2,2,320,128]{3,2,1,0:T(8,128)(2,1)S(1)}, u32[]{:S(2)}, u32[]{:S(2)}) collective-permute-start(bf16[2,2,320,128]{3,2,1,0:T(8,128)(2,1)S(1)} %pad_maximum_fusion.2.refs_0_), channel_id=1, source_target_pairs={{0,32},{32,64},{64,96},{96,0},{1,33},{33,65},{65,97},{97,1},{2,34}... | collective-permute-start | bytes 983048 | tf_op jit(solution)/shard_map/ppermute | solution.py:422
  175.1 17.6 %collective-permute-start.29 = (bf16[4,2,320,128]{3,2,1,0:T(8,128)(2,1)S(1)}, bf16[4,2,320,128]{3,2,1,0:T(8,128)(2,1)S(1)}, u32[]{:S(2)}, u32[]{:S(2)}) collective-permute-start(bf16[4,2,320,128]{3,2,1,0:T(8,128)(2,1)S(1)} %pad_maximum_fusion.1.refs_0_), channel_id=1, source_target_pairs={{0,8},{8,0},{1,9},{9,1},{2,10},{10,2},{3,11},{11,3},{4,12},{12,4},... | collective-permute-start | bytes 1966088 | tf_op jit(solution)/shard_map/ppermute | solution.py:422
  191.7 2.2 %collective-permute-start.30 = (bf16[4,2,320,128]{3,2,1,0:T(8,128)(2,1)S(1)}, bf16[4,2,320,128]{3,2,1,0:T(8,128)(2,1)S(1)}, u32[]{:S(2)}, u32[]{:S(2)}) collective-permute-start(bf16[4,2,320,128]{3,2,1,0:T(8,128)(2,1)S(1)} %collective-permute-done.21.refs_1_), channel_id=1, source_target_pairs={{0,8},{8,0},{1,9},{9,1},{2,10},{10,2},{3,11},{11,3},{4,12},{12,4},... | collective-permute-start | bytes 1966088 | tf_op jit(solution)/shard_map/ppermute | solution.py:422
  192.2 3.9 %collective-permute-start.25 = (bf16[2,2,320,128]{3,2,1,0:T(8,128)(2,1)S(1)}, bf16[2,2,320,128]{3,2,1,0:T(8,128)(2,1)S(1)}, u32[]{:S(2)}, u32[]{:S(2)}) collective-permute-start(bf16[2,2,320,128]{3,2,1,0:T(8,128)(2,1)S(1)} %pad_maximum_fusion.2.refs_0_), channel_id=1, source_target_pairs={{0,8},{8,0},{1,9},{9,1},{2,10},{10,2},{3,11},{11,3},{4,12},{12,4},... | collective-permute-start | bytes 983048 | tf_op jit(solution)/shard_map/ppermute | solution.py:422
  192.2 3.9 %collective-permute-start.26 = (bf16[2,2,320,128]{3,2,1,0:T(8,128)(2,1)S(1)}, bf16[2,2,320,128]{3,2,1,0:T(8,128)(2,1)S(1)}, u32[]{:S(2)}, u32[]{:S(2)}) collective-permute-start(bf16[2,2,320,128]{3,2,1,0:T(8,128)(2,1)S(1)} %collective-permute-done.22.refs_1_), channel_id=1, source_target_pairs={{0,8},{8,0},{1,9},{9,1},{2,10},{10,2},{3,11},{11,3},{4,12},{12,4},... | collective-permute-start | bytes 983048 | tf_op jit(solution)/shard_map/ppermute | solution.py:422
  192.7 3.4 %collective-permute-start.27 = (bf16[2,2,320,128]{3,2,1,0:T(8,128)(2,1)S(1)}, bf16[2,2,320,128]{3,2,1,0:T(8,128)(2,1)S(1)}, u32[]{:S(2)}, u32[]{:S(2)}) collective-permute-start(bf16[2,2,320,128]{3,2,1,0:T(8,128)(2,1)S(1)} %collective-permute-done.23.refs_2_), channel_id=1, source_target_pairs={{0,8},{8,0},{1,9},{9,1},{2,10},{10,2},{3,11},{11,3},{4,12},{12,4},... | collective-permute-start | bytes 983048 | tf_op jit(solution)/shard_map/ppermute | solution.py:422
  192.7 3.4 %collective-permute-start.28 = (bf16[2,2,320,128]{3,2,1,0:T(8,128)(2,1)S(1)}, bf16[2,2,320,128]{3,2,1,0:T(8,128)(2,1)S(1)}, u32[]{:S(2)}, u32[]{:S(2)}) collective-permute-start(bf16[2,2,320,128]{3,2,1,0:T(8,128)(2,1)S(1)} %collective-permute-done.24.refs_3_), channel_id=1, source_target_pairs={{0,8},{8,0},{1,9},{9,1},{2,10},{10,2},{3,11},{11,3},{4,12},{12,4},... | collective-permute-start | bytes 983048 | tf_op jit(solution)/shard_map/ppermute | solution.py:422
  (12 other events, 210.6 us)

commit v4 on v3

--- a/solution.py
+++ b/solution.py
@@ -80,6 +80,13 @@
     return np.stack([spread(table[:, i : i + chunk], 8) for i in range(0, NT, chunk)])
 
 
+RESIDENT = pl.BlockSpec(memory_space=pltpu.VMEM)
+
+
+def resident(*arrays):
+    return [pltpu.with_memory_space_constraint(array, pltpu.VMEM) for array in arrays]
+
+
 def dot(a, b):
     return jnp.dot(a, b, preferred_element_type=jnp.float32)
 
@@ -99,11 +106,11 @@
     return lax.dynamic_index_in_dim(jnp.asarray(table), dev[0], 0, keepdims=False)
 
 
-def first_kernel(by_z, x_ref, xo_ref, w_ref, *out_refs):
-    rows = x_ref.shape[1]
-    for at in range(0, rows, 32):
+def first_kernel(half, by_z, x_ref, xo_ref, w_ref, *out_refs):
+    for at in range(0, HALF, 32):
         sides = []
-        for here in (slice(at, at + 16), slice(at + 16, at + 32)):
+        for first in (half * HALF + at, half * HALF + at + 16):
+            here = slice(first, first + 16)
             both = [x_ref[:, here, :].reshape(256, 128), xo_ref[:, here, :].reshape(256, 128)]
             sides.append(jnp.concatenate(both, axis=0))
         both = dot(w_ref[...], jnp.concatenate(sides, axis=1)).astype(jnp.bfloat16)
@@ -114,39 +121,17 @@
                 out_ref[:, :, here, :] = part[i] if by_z else part[:, i]
 
 
-def copy_kernel(x_ref, out_ref):
-    out_ref[...] = x_ref[...]
-
-
-def copied(x):
-    spec = pl.BlockSpec((x.shape[0] // 4,) + x.shape[1:], lambda i: (i, 0, 0))
-    return pl.pallas_call(
-        copy_kernel,
-        out_shape=jax.ShapeDtypeStruct(x.shape, x.dtype),
-        grid=(4,),
-        in_specs=[spec],
-        out_specs=spec,
-        compiler_params=params(),
-        cost_estimate=cost(0, 6 << 20),
-        name="copied",
-    )(x)
-
-
 def first_transform(weights, x, xo, half, by_z):
-    step = 160
-    start = half * HALF // step
-    spec = pl.BlockSpec((16, step, 128), lambda i: (0, i + start, 0))
     count, lead = (4, 2) if by_z else (2, 4)
     return pl.pallas_call(
-        functools.partial(first_kernel, by_z),
-        out_shape=[jax.ShapeDtypeStruct((lead, 2, HALF, 128), jnp.bfloat16)] * count,
-        grid=(HALF // step,),
-        in_specs=[spec, spec, pl.BlockSpec((256, 512), lambda i: (0, 0))],
-        out_specs=[pl.BlockSpec((lead, 2, step, 128), lambda i: (0, 0, i, 0))] * count,
+        functools.partial(first_kernel, half, by_z),
+        out_shape=[pltpu.VMEM((lead, 2, HALF, 128), jnp.bfloat16)] * count,
+        in_specs=[RESIDENT] * 3,
+        out_specs=[RESIDENT] * count,
         compiler_params=params(),
         cost_estimate=cost(700 << 20, 6 << 20),
         name="first_transform",
-    )(x, xo, weights)
+    )(*resident(x, xo, weights))
 
 
 def total_of(refs):
@@ -167,68 +152,76 @@
 def start_product_kernel(counts, *refs):
     s_refs, (r_ref, out_ref, held) = refs[: sum(counts)], refs[sum(counts) :]
 
+    halves = [total_of(s_refs[: counts[0]]), total_of(s_refs[counts[0] :])]
+    real, imag = [jnp.concatenate([h[i] for h in halves], axis=0) for i in range(2)]
+    hold(held, real, imag, 1.0)
+
+    def body(i, carry):
+        rows = pl.ds(pl.multiple_of(i * 1280, 1280), 1280)
+        both = jnp.concatenate([r_ref[0, 0, rows, :], r_ref[1, 0, rows, :]], axis=1)
+        part = dot(both, held[...])
+        for g in range(32):
+            here = slice(g * 40, g * 40 + 40)
+            out_ref[i * 32 + g, 0] = part[here, :128].astype(jnp.bfloat16)
+            out_ref[i * 32 + g, 1] = part[here, 128:].astype(jnp.bfloat16)
+        return carry
+
+    lax.fori_loop(0, 4, body, 0)
+
+
+def start_product(spectra, counts, reflection):
+    depth = reflection.shape[3]
+    return pl.pallas_call(
+        functools.partial(start_product_kernel, counts),
+        out_shape=pltpu.VMEM((128, 2, 40, 128), jnp.bfloat16),
+        in_specs=[RESIDENT] * (len(spectra) + 1),
+        out_specs=RESIDENT,
+        scratch_shapes=[pltpu.VMEM((2 * depth, 256), jnp.bfloat16)],
+        compiler_params=params(),
+        cost_estimate=cost(4 << 30, 18 << 20),
+        name="start_product",
+    )(*resident(*spectra, reflection))
+
+
+def minus_product_kernel(s_ref, r_ref, here_ref, far_ref, out_ref, near_ref, held):
     @pl.when(pl.program_id(0) == 0)
     def _():
-        halves = [total_of(s_refs[: counts[0]]), total_of(s_refs[counts[0] :])]
-        real, imag = [jnp.concatenate([h[i] for h in halves], axis=0) for i in range(2)]
-        hold(held, real, imag, 1.0)
-
-    both = jnp.concatenate([r_ref[0, 0], r_ref[1, 0]], axis=1)
-    part = dot(both, held[...])
-    for g in range(out_ref.shape[0]):
-        out_ref[g, 0] = part[g * 40 : g * 40 + 40, :128].astype(jnp.bfloat16)
-        out_ref[g, 1] = part[g * 40 : g * 40 + 40, 128:].astype(jnp.bfloat16)
-
-
-def start_product(spectra, counts, reflection):
-    depth = reflection.shape[3]
-    rows = 1280
-    return pl.pallas_call(
-        functools.partial(start_product_kernel, counts),
-        out_shape=jax.ShapeDtypeStruct((128, 2, 40, 128), jnp.bfloat16),
-        grid=(5120 // rows,),
-        in_specs=[pl.BlockSpec(s.shape, lambda i, n=s.ndim: (0,) * n) for s in spectra]
-        + [pl.BlockSpec((2, 1, rows, depth), lambda i: (0, 0, i, 0))],
-        out_specs=pl.BlockSpec((rows // 40, 2, 40, 128), lambda i: (i, 0, 0, 0)),
-        scratch_shapes=[pltpu.VMEM((2 * depth, 256), jnp.bfloat16)],
-        compiler_params=params(),
-        cost_estimate=cost(4 << 30, 18 << 20),
-        name="start_product",
-    )(*spectra, reflection)
-
-
-def minus_product_kernel(s_ref, r_ref, out_ref, held):
-    @pl.when(pl.program_id(0) == 0)
-    def _():
+        near_ref[0] = here_ref[...]
+        near_ref[1] = far_ref[...]
         real, imag = [
             jnp.concatenate([s_ref[i, part].astype(jnp.float32) for i in range(16)], axis=0) for part in range(2)
         ]
         hold(held, real, imag, -1.0)
 
-    both = jnp.concatenate([r_ref[0, 0], r_ref[1, 0]], axis=1)
+    rows = pl.ds(pl.multiple_of(pl.program_id(0) * 1280, 1280), 1280)
+    both = jnp.concatenate([r_ref[0, 0, rows, :], r_ref[1, 0, rows, :]], axis=1)
     part = dot(both, held[...]).astype(jnp.bfloat16)
     for g in range(out_ref.shape[0]):
         for i in range(2):
             out_ref[g, i] = part[g * 640 : g * 640 + 640, i * 128 : i * 128 + 128]
 
 
-def minus_product(spectra, reflection):
+def minus_product(spectra, reflection, here, far):
     depth = reflection.shape[3]
     rows = 1280
     return pl.pallas_call(
         minus_product_kernel,
-        out_shape=pltpu.HBM((8, 2, 640, 128), jnp.bfloat16),
+        out_shape=[pltpu.HBM((8, 2, 640, 128), jnp.bfloat16), pltpu.HBM((2,) + here.shape, jnp.bfloat16)],
         grid=(5120 // rows,),
         in_specs=[
-            pl.BlockSpec(spectra.shape, lambda i: (0, 0, 0, 0)),
-            pl.BlockSpec((2, 1, rows, depth), lambda i: (0, 0, i, 0)),
+            RESIDENT,
+            RESIDENT,
+            RESIDENT,
+            RESIDENT,
         ],
-        out_specs=pl.BlockSpec((rows // 640, 2, 640, 128), lambda i: (i, 0, 0, 0)),
+        out_specs=[pl.BlockSpec((rows // 640, 2, 640, 128), lambda i: (i, 0, 0, 0)),
+            pl.BlockSpec((2,) + here.shape, lambda i: (0, 0, 0, 0)),
+        ],
         scratch_shapes=[pltpu.VMEM((2 * depth, 256), jnp.bfloat16)],
         compiler_params=params(),
         cost_estimate=cost(4 << 30, 18 << 20),
         name="minus_product",
-    )(spectra, reflection)
+    )(*resident(spectra, reflection, here, far))
 
 
 def sum_kernel(p_ref, a_ref, b_ref):
@@ -312,20 +305,20 @@
     return pl.pallas_call(
         lambda d, *refs: middle_kernel(*refs),
         out_shape=(
-            jax.ShapeDtypeStruct((2 * NF, 40, 128), jnp.bfloat16),
-            jax.ShapeDtypeStruct((NF, 2, 40, 128), jnp.bfloat16),
+            pltpu.VMEM((2 * NF, 40, 128), jnp.bfloat16),
+            pltpu.VMEM((NF, 2, 40, 128), jnp.bfloat16),
         ),
         grid_spec=pltpu.PrefetchScalarGridSpec(
             num_scalar_prefetch=1,
             grid=(1,),
-            in_specs=[whole(parts.shape), onset_spec(), whole(wi.shape), whole(wf.shape)],
-            out_specs=(whole((2 * NF, 40, 128)), whole((NF, 2, 40, 128))),
+            in_specs=[RESIDENT, onset_spec(), RESIDENT, RESIDENT],
+            out_specs=(RESIDENT, RESIDENT),
             scratch_shapes=[pltpu.VMEM((256, 640), jnp.float32)],
         ),
         compiler_params=params(),
         cost_estimate=cost(2 << 30, 8 << 20),
         name="middle",
-    )(dev, parts, onsets, wi, wf)
+    )(dev, *resident(parts), onsets, *resident(wi, wf))
 
 
 def minus_kernel(dev_ref, *refs):
@@ -359,7 +352,7 @@
         compiler_params=params(),
         cost_estimate=cost(700 << 20, 8 << 20),
         name="minus_output",
-    )(dev, *parts, onsets, weights)
+    )(dev, *[pltpu.with_memory_space_constraint(v, pltpu.HBM) for v in parts], onsets, weights)
 
 
 def plus_kernel(half, dev_ref, *refs):
@@ -369,9 +362,11 @@
     rows = x_ref.shape[1]
     times = first + lax.broadcasted_iota(jnp.int32, (16, 16, 128), 0)
     distance = jnp.minimum(times, NT - times)
+    done = pl.program_id(0) * rows
     for at in range(0, rows, 32):
         sides = []
-        for here in (slice(at, at + 16), slice(at + 16, at + 32)):
+        for from_row in (at, at + 16):
+            here = pl.ds(pl.multiple_of(done + from_row, 16), 16)
             if half:
                 flat = [p_refs[c * 4 + k][e, :, here, :] for c in range(2) for e in range(2) for k in range(4)]
             else:
@@ -388,16 +383,15 @@
 def plus_output(dev, half, parts, onsets, x, weights, held):
     step = 160
     start = half * HALF // step
-    lead = 2 if half else 4
     time_spec = pl.BlockSpec((16, step, 128), lambda i, d: (0, i + start, 0))
-    operands = [dev, *parts, onsets, x, weights] + ([held] if half else [])
+    operands = [dev, *resident(*parts), onsets, x, weights] + ([held] if half else [])
     return pl.pallas_call(
         functools.partial(plus_kernel, half),
         out_shape=jax.ShapeDtypeStruct(x.shape, jnp.bfloat16),
         grid_spec=pltpu.PrefetchScalarGridSpec(
             num_scalar_prefetch=1,
             grid=(HALF // step,),
-            in_specs=[pl.BlockSpec((lead, 2, step, 128), lambda i, d: (0, 0, i, 0))] * len(parts)
+            in_specs=[RESIDENT] * len(parts)
             + [
                 pl.BlockSpec((step, 128), lambda i, d: (i + start, 0)),
                 time_spec,
@@ -435,7 +429,6 @@
 def start_spectra(dev, x):
     weights = of_device(first_weights(), dev)
     xo = along(x, "core", 1)
-    x = copied(x)
     a_send = first_transform(weights, x, xo, 0, True)
     a_send, xo = together(a_send, xo)
     a_got = around(a_send, "z")
@@ -468,7 +461,7 @@
     start_parts = exchange(start_product(spectra, (2, 4), reflection), SRC + FREQ)
     summed, spectra = middle(dev, start_parts.reshape(8, NF, 2, 40, 128), blocks)
     spectra, far = together(exchange(spectra, FREQ), along(summed, "xh", 1))
-    parts, near = together(minus_product(spectra, reflection), jnp.stack([summed, far]))
+    parts, near = minus_product(spectra, reflection, summed, far)
     parts, mine, others = together(exchange(parts, SRC), *rest_of(near))
 
     a, b = summed_halves(parts)
@@ -476,8 +469,7 @@
     last = along(mine[3], "core", 1)
     b_far, a_near, last, weights = together(along(b, "xh", 1), around([a] * 4, "z"), last, weights)
     a_near, b_near = jnp.stack(a_near), jnp.stack([b, b_far])
-    gathered = [pltpu.with_memory_space_constraint(v, pltpu.HBM) for v in (*mine, *others, last)]
-    minus_field = minus_output(dev, gathered, blocks, weights[0])
+    minus_field = minus_output(dev, [*mine, *others, last], blocks, weights[0])
     a_far, b_all = along(a_near, "xh", 1), around([b_near] * 4, "z")
     a_far, b_all, minus_field = together(a_far, b_all, minus_field)
     a_all, b_all = [a_near, a_far], list(b_all)

time: 199 us -> 193 us (0.970)
  Pallas kernels: 30.2 us -> 23.7 us
    pallas_call x5 -> x4, Pallas kernels: 14.7 us -> 9.71 us  [the longest x1 5.11 us: minus_product(): pl.pallas_call(minus_product_kernel, out_shape=[pltpu.HBM((8, 2, 640, 128...]
where the time goes in v4:
time: 193 us
  waiting for transfers between devices  67.7 us (35%)
  blocking collectives  55.2 us (29%)
  starting transfers between devices  38.5 us (20%)
  Pallas kernels  23.7 us (12%)
  local copies, waits for them, and re-layouts  6.41 us (3%)
    ppermute x31, waiting for transfers between devices, along(): return lax.ppermute(x, axis, [(i, (i + step) % size) for i in range(size)])  67.7 us
    all_to_all x2, blocking collectives, exchange(): return lax.all_to_all(x, axes, 0, 0, tiled=True)  55.2 us
    ppermute x31, starting transfers between devices, along(): return lax.ppermute(x, axis, [(i, (i + step) % size) for i in range(size)])  34.9 us
    pallas_call x1, Pallas kernels, minus_product(): pl.pallas_call(minus_product_kernel, out_shape=[pltpu.HBM((8, 2, 640, 128...  5.11 us
    pallas_call x1, Pallas kernels, minus_output(): pl.pallas_call(minus_kernel, out_shape=jax.ShapeDtypeStruct((16, 640, 128...  5.07 us
    pallas_call x1, Pallas kernels, start_product(): pl.pallas_call(functools.partial(start_product_kernel, counts), out_shape...  4.22 us
    pallas_call x2, Pallas kernels, plus_output(): pl.pallas_call(functools.partial(plus_kernel, half), out_shape=jax.ShapeD...  4.12 us
  transfers between devices with their start and end apart: 32, of which 12 were waited for; matrix products, arithmetic and copies ran while one was open for 2% of the time, Pallas kernels for 4%

profile of v4, /device:TPU:1, one launch (start us, length us, event | category | flops | bytes accessed | tf_op | source)
XLA Modules:
  0.0 192.8 jit_solution(8057033683494832464)
XLA Ops:
  0.6 1.5 collective-permute-start
  3.1 3.8 %collective-permute-done.xo_ref = bf16[16,640,128]{2,1,0:T(8,128)(2,1)S(1)} collective-permute-done((bf16[16,640,128]{2,1,0:T(8,128)(2,1)}, bf16[16,640,128]{2,1,0:T(8,128)(2,1)S(1)}, u32[]{:S(2)}, u32[]{:S(2)}) %collective-permute-start) | collective-permute-done | bytes 2621472 | tf_op jit(solution)/shard_map/ppermute | solution.py:416
  6.9 1.7 copy-done
  10.3 2.9 %collective-permute-start.4 = (bf16[4,2,320,128]{3,2,1,0:T(8,128)(2,1)S(1)}, bf16[4,2,320,128]{3,2,1,0:T(8,128)(2,1)S(1)}, u32[]{:S(2)}, u32[]{:S(2)}) collective-permute-start(bf16[4,2,320,128]{3,2,1,0:T(8,128)(2,1)S(1)} %get-tuple-element.57), channel_id=1, source_target_pairs={{0,16},{16,0},{1,17},{17,1},{2,18},{18,2},{3,19},{19,3},{4,20},{20... | collective-permute-start | bytes 1966088 | tf_op jit(solution)/shard_map/ppermute | solution.py:416
  13.2 1.6 collective-permute-start.1
  14.9 3.3 %collective-permute-start.2 = (bf16[2,2,320,128]{3,2,1,0:T(8,128)(2,1)S(1)}, bf16[2,2,320,128]{3,2,1,0:T(8,128)(2,1)S(1)}, u32[]{:S(2)}, u32[]{:S(2)}) collective-permute-start(bf16[2,2,320,128]{3,2,1,0:T(8,128)(2,1)S(1)} %get-tuple-element.54), channel_id=1, source_target_pairs={{0,64},{32,96},{64,0},{96,32},{1,65},{33,97},{65,1},{97,33},{2,66}... | collective-permute-start | bytes 983048 | tf_op jit(solution)/shard_map/ppermute | solution.py:416
  18.9 5.5 %collective-permute-done.1 = bf16[2,2,320,128]{3,2,1,0:T(8,128)(2,1)S(1)} collective-permute-done((bf16[2,2,320,128]{3,2,1,0:T(8,128)(2,1)S(1)}, bf16[2,2,320,128]{3,2,1,0:T(8,128)(2,1)S(1)}, u32[]{:S(2)}, u32[]{:S(2)}) %collective-permute-start.1) | collective-permute-done | bytes 327712 | tf_op jit(solution)/shard_map/ppermute | solution.py:416
  24.4 7.9 %collective-permute-done.2 = bf16[2,2,320,128]{3,2,1,0:T(8,128)(2,1)S(1)} collective-permute-done((bf16[2,2,320,128]{3,2,1,0:T(8,128)(2,1)S(1)}, bf16[2,2,320,128]{3,2,1,0:T(8,128)(2,1)S(1)}, u32[]{:S(2)}, u32[]{:S(2)}) %collective-permute-start.2) | collective-permute-done | bytes 327712 | tf_op jit(solution)/shard_map/ppermute | solution.py:416
  32.5 2.9 %collective-permute-start.8 = (bf16[2,320,128]{2,1,0:T(8,128)(2,1)S(1)}, bf16[2,320,128]{2,1,0:T(8,128)(2,1)S(1)}, u32[]{:S(2)}, u32[]{:S(2)}) collective-permute-start(bf16[2,320,128]{2,1,0:T(8,128)(2,1)S(1)} %get-tuple-element.94), channel_id=1, source_target_pairs={{0,96},{32,0},{64,32},{96,64},{1,97},{33,1},{65,33},{97,65},{2,98}... | collective-permute-start | bytes 491528 | tf_op jit(solution)/shard_map/ppermute | solution.py:416
  36.6 5.6 %collective-permute-done.8.refs_5_ = bf16[2,320,128]{2,1,0:T(8,128)(2,1)S(1)} collective-permute-done((bf16[2,320,128]{2,1,0:T(8,128)(2,1)S(1)}, bf16[2,320,128]{2,1,0:T(8,128)(2,1)S(1)}, u32[]{:S(2)}, u32[]{:S(2)}) %collective-permute-start.8) | collective-permute-done | bytes 163872 | tf_op jit(solution)/shard_map/ppermute | solution.py:416
  42.1 4.4 %collective-permute-done.6.refs_3_ = bf16[2,320,128]{2,1,0:T(8,128)(2,1)S(1)} collective-permute-done((bf16[2,320,128]{2,1,0:T(8,128)(2,1)S(1)}, bf16[2,320,128]{2,1,0:T(8,128)(2,1)S(1)}, u32[]{:S(2)}, u32[]{:S(2)}) %collective-permute-start.6) | collective-permute-done | bytes 163872 | tf_op jit(solution)/shard_map/ppermute | solution.py:416
  46.5 4.2 %start_product.1 = bf16[128,2,40,128]{3,2,1,0:T(8,128)(2,1)S(1)} custom-call(bf16[2,320,128]{2,1,0:T(8,128)(2,1)S(1)} %get-tuple-element.99.refs_0_, bf16[2,320,128]{2,1,0:T(8,128)(2,1)S(1)} %collective-permute-done.5.refs_1_, bf16[2,320,128]{2,1,0:T(8,128)(2,1)S(1)} %get-tuple-element.97.refs_2_, bf16[2,320,128]{2,1,0:T(8,128)(2,1)S(1)} %collective-permute-done.6.refs_3_, ...), custom_call_target="tpu_custom_call" | custom-call | flops 4294967296 | bytes 18874368 | tf_op jit(solution)/shard_map/start_product/pallas_call | solution.py:174
  50.8 40.6 %all_to_all.15 = bf16[128,2,40,128]{3,2,1,0:T(8,128)(2,1)S(1)} all-to-all(bf16[128,2,40,128]{3,2,1,0:T(8,128)(2,1)S(1)} %start_product.1), channel_id=1, replica_groups=mesh['z'=4,'xh'=2,'core'=2,'y'=4,'xl'=2] {'y','xl','z','xh','core'}, dimensions={0} | all-to-all | bytes 5242880 | tf_op jit(solution)/shard_map/all_to_all | solution.py:411
  91.4 2.9 %middle.1 = (bf16[32,40,128]{2,1,0:T(8,128)(2,1)S(1)}, bf16[16,2,40,128]{3,2,1,0:T(8,128)(2,1)S(1)}) custom-call(s32[1]{0:T(128)} %bitcast.d.dev_ref, bf16[8,16,2,40,128]{4,3,2,1,0:T(8,128)(2,1)S(1)} %bitcast.29, s32[16,40,128]{2,1,0:T(8,128)S(1)} %bitcast.27, bf16[4,512,256]{2,1,0:T(8,128)(2,1)S(1)} %copy-done.5, bf16[4,256,512]{2,1,0:T(8,128)(2,1)S(1)} %copy-done.4), custom_call_target="tpu_custom_call" | custom-call | flops 2147483648 | bytes 8388608 | tf_op jit(solution)/shard_map/middle/pallas_call | solution.py:305
  94.3 1.6 collective-permute-start.9
  95.9 14.6 %all_to_all.16.s_ref = bf16[16,2,40,128]{3,2,1,0:T(8,128)(2,1)S(1)} all-to-all(bf16[16,2,40,128]{3,2,1,0:T(8,128)(2,1)S(1)} %get-tuple-element.64), channel_id=1, replica_groups=mesh['z'=4,'xh'=2,'core'=2,'y'=4,'xl'=2] {'z','xh','core'}, dimensions={0} | all-to-all | bytes 655360 | tf_op jit(solution)/shard_map/all_to_all | solution.py:411
  110.5 5.1 %minus_product.1 = (bf16[8,2,640,128]{3,2,1,0:T(8,128)(2,1)}, bf16[2,32,40,128]{3,2,1,0:T(8,128)(2,1)}) custom-call(bf16[16,2,40,128]{3,2,1,0:T(8,128)(2,1)S(1)} %all_to_all.16.s_ref, bf16[2,1,5120,640]{3,2,1,0:T(8,128)(2,1)S(1)} %copy-done.2, bf16[32,40,128]{2,1,0:T(8,128)(2,1)S(1)} %get-tuple-element.65.here_ref, ...), custom_call_target="tpu_custom_call" | custom-call | flops 4294967296 | bytes 18874368 | tf_op jit(solution)/shard_map/minus_product/pallas_call | solution.py:207
  115.7 3.6 %all-to-all-start.2 = ((bf16[8,2,640,128]{3,2,1,0:T(8,128)(2,1)}), bf16[8,2,640,128]{3,2,1,0:T(8,128)(2,1)S(1)}, u32[]{:S(2)}, u32[]{:S(2)}) async-start(bf16[8,2,640,128]{3,2,1,0:T(8,128)(2,1)} %get-tuple-element.68), calls=%async_computation.2 | async-start | bytes 5242880 | tf_op jit(solution)/shard_map/all_to_all | solution.py:411
  119.3 1.4 collective-permute-start.11
  120.8 1.5 collective-permute-start.13
  122.2 2.1 %collective-permute-start.12 = (bf16[2,32,40,128]{3,2,1,0:T(8,128)(2,1)}, bf16[2,32,40,128]{3,2,1,0:T(8,128)(2,1)S(1)}, u32[]{:S(2)}, u32[]{:S(2)}) collective-permute-start(bf16[2,32,40,128]{3,2,1,0:T(8,128)(2,1)} %get-tuple-element.79.refs_0_), channel_id=1, source_target_pairs={{0,96},{32,0},{64,32},{96,64},{1,97},{33,1},{65,33},{97,65},{2,98}... | collective-permute-start | bytes 1966088 | tf_op jit(solution)/shard_map/ppermute | solution.py:416
  124.3 11.8 %collective-permute-done.11.refs_2_ = bf16[2,32,40,128]{3,2,1,0:T(8,128)(2,1)S(1)} collective-permute-done((bf16[2,32,40,128]{3,2,1,0:T(8,128)(2,1)}, bf16[2,32,40,128]{3,2,1,0:T(8,128)(2,1)S(1)}, u32[]{:S(2)}, u32[]{:S(2)}) %collective-permute-start.11) | collective-permute-done | bytes 655392 | tf_op jit(solution)/shard_map/ppermute | solution.py:416
  136.2 3.8 %collective-permute-start.15 = (bf16[2,32,40,128]{3,2,1,0:T(8,128)(2,1)S(1)}, bf16[2,32,40,128]{3,2,1,0:T(8,128)(2,1)S(1)}, u32[]{:S(2)}, u32[]{:S(2)}) collective-permute-start(bf16[2,32,40,128]{3,2,1,0:T(8,128)(2,1)S(1)} %collective-permute-done.11.refs_2_), channel_id=1, source_target_pairs={{0,8},{8,0},{1,9},{9,1},{2,10},{10,2},{3,11},{11,3},{4,12},{12,4},... | collective-permute-start | bytes 1966088 | tf_op jit(solution)/shard_map/ppermute | solution.py:416
  140.0 11.8 %collective-permute-done.10.refs_1_ = bf16[2,32,40,128]{3,2,1,0:T(8,128)(2,1)S(1)} collective-permute-done((bf16[2,32,40,128]{3,2,1,0:T(8,128)(2,1)}, bf16[2,32,40,128]{3,2,1,0:T(8,128)(2,1)S(1)}, u32[]{:S(2)}, u32[]{:S(2)}) %collective-permute-start.10) | collective-permute-done | bytes 655392 | tf_op jit(solution)/shard_map/ppermute | solution.py:416
  155.5 1.3 collective-permute-start.18
  159.9 3.6 %collective-permute-done.16 = bf16[2,320,128]{2,1,0:T(8,128)(2,1)S(1)} collective-permute-done((bf16[2,320,128]{2,1,0:T(8,128)(2,1)S(1)}, bf16[2,320,128]{2,1,0:T(8,128)(2,1)S(1)}, u32[]{:S(2)}, u32[]{:S(2)}) %collective-permute-start.16) | collective-permute-done | bytes 163872 | tf_op jit(solution)/shard_map/ppermute | solution.py:416
  163.5 3.1 %collective-permute-done.17 = bf16[2,320,128]{2,1,0:T(8,128)(2,1)S(1)} collective-permute-done((bf16[2,320,128]{2,1,0:T(8,128)(2,1)S(1)}, bf16[2,320,128]{2,1,0:T(8,128)(2,1)S(1)}, u32[]{:S(2)}, u32[]{:S(2)}) %collective-permute-start.17) | collective-permute-done | bytes 163872 | tf_op jit(solution)/shard_map/ppermute | solution.py:416
  169.9 2.0 %collective-permute-start.29 = (bf16[4,2,320,128]{3,2,1,0:T(8,128)(2,1)S(1)}, bf16[4,2,320,128]{3,2,1,0:T(8,128)(2,1)S(1)}, u32[]{:S(2)}, u32[]{:S(2)}) collective-permute-start(bf16[4,2,320,128]{3,2,1,0:T(8,128)(2,1)S(1)} %pad_maximum_fusion.refs_0_), channel_id=1, source_target_pairs={{0,8},{8,0},{1,9},{9,1},{2,10},{10,2},{3,11},{11,3},{4,12},{12,4},... | collective-permute-start | bytes 1966088 | tf_op jit(solution)/shard_map/ppermute | solution.py:416
  171.9 5.1 %minus_output.1 = bf16[16,640,128]{2,1,0:T(8,128)(2,1)} custom-call(s32[1]{0:T(128)} %bitcast.d.dev_ref, bf16[2,32,40,128]{3,2,1,0:T(8,128)(2,1)} %get-tuple-element.79.refs_0_, bf16[2,32,40,128]{3,2,1,0:T(8,128)(2,1)} %copy-done.7, bf16[2,32,40,128]{3,2,1,0:T(8,128)(2,1)} %copy-done.6, bf16[2,32,40,128]{3,2,1,0:T(8,128)(2,1)} %copy-done.9, ...), custom_call_target="tpu_custom_call" | custom-call | flops 734003200 | bytes 8388608 | tf_op jit(solution)/shard_map/minus_output/pallas_call | solution.py:342
  177.5 8.9 %collective-permute-done.22.refs_1_ = bf16[2,2,320,128]{3,2,1,0:T(8,128)(2,1)S(1)} collective-permute-done((bf16[2,2,320,128]{3,2,1,0:T(8,128)(2,1)S(1)}, bf16[2,2,320,128]{3,2,1,0:T(8,128)(2,1)S(1)}, u32[]{:S(2)}, u32[]{:S(2)}) %collective-permute-start.22) | collective-permute-done | bytes 327712 | tf_op jit(solution)/shard_map/ppermute | solution.py:416
  188.6 2.0 %plus_output.2.refs_11_ = bf16[16,640,128]{2,1,0:T(8,128)(2,1)} custom-call(s32[1]{0:T(128)} %bitcast.d.dev_ref, bf16[4,2,320,128]{3,2,1,0:T(8,128)(2,1)S(1)} %pad_maximum_fusion.refs_0_, bf16[4,2,320,128]{3,2,1,0:T(8,128)(2,1)S(1)} %collective-permute-done.21.refs_1_, bf16[4,2,320,128]{3,2,1,0:T(8,128)(2,1)S(1)} %collective-permute-done.29.refs_2_, ...), custom_call_target="tpu_custom_call" | custom-call | flops 734003200 | bytes 6291456 | tf_op jit(solution)/shard_map/plus_output/pallas_call | solution.py:388
  190.7 2.1 %plus_output.3 = bf16[16,640,128]{2,1,0:T(8,128)(2,1)} custom-call(s32[1]{0:T(128)} %bitcast.d.dev_ref, bf16[2,2,320,128]{3,2,1,0:T(8,128)(2,1)S(1)} %pad_maximum_fusion.1.refs_0_, bf16[2,2,320,128]{3,2,1,0:T(8,128)(2,1)S(1)} %collective-permute-done.22.refs_1_, ...), custom_call_target="tpu_custom_call", output_to_operand_aliasing={{}: (12, {})} | custom-call | flops 734003200 | bytes 6291456 | tf_op jit(solution)/shard_map/plus_output/pallas_call | solution.py:388
  (74 shorter events, 17.5 us)
Async XLA Ops:
  0.6 6.2 %collective-permute-start = (bf16[16,640,128]{2,1,0:T(8,128)(2,1)}, bf16[16,640,128]{2,1,0:T(8,128)(2,1)S(1)}, u32[]{:S(2)}, u32[]{:S(2)}) collective-permute-start(bf16[16,640,128]{2,1,0:T(8,128)(2,1)} %refs_9_.1), channel_id=1, source_target_pairs={{0,8},{8,0},{1,9},{9,1},{2,10},{10,2},{3,11},{11,3},{4,12},{12,4},... | collective-permute-start | bytes 7864328 | tf_op jit(solution)/shard_map/ppermute | solution.py:416
  10.3 22.0 %collective-permute-start.4 = (bf16[4,2,320,128]{3,2,1,0:T(8,128)(2,1)S(1)}, bf16[4,2,320,128]{3,2,1,0:T(8,128)(2,1)S(1)}, u32[]{:S(2)}, u32[]{:S(2)}) collective-permute-start(bf16[4,2,320,128]{3,2,1,0:T(8,128)(2,1)S(1)} %get-tuple-element.57), channel_id=1, source_target_pairs={{0,16},{16,0},{1,17},{17,1},{2,18},{18,2},{3,19},{19,3},{4,20},{20... | collective-permute-start | bytes 1966088 | tf_op jit(solution)/shard_map/ppermute | solution.py:416
  13.2 11.2 %collective-permute-start.1 = (bf16[2,2,320,128]{3,2,1,0:T(8,128)(2,1)S(1)}, bf16[2,2,320,128]{3,2,1,0:T(8,128)(2,1)S(1)}, u32[]{:S(2)}, u32[]{:S(2)}) collective-permute-start(bf16[2,2,320,128]{3,2,1,0:T(8,128)(2,1)S(1)} %get-tuple-element.53), channel_id=1, source_target_pairs={{0,32},{32,64},{64,96},{96,0},{1,33},{33,65},{65,97},{97,1},{2,34}... | collective-permute-start | bytes 983048 | tf_op jit(solution)/shard_map/ppermute | solution.py:416
  14.9 17.5 %collective-permute-start.2 = (bf16[2,2,320,128]{3,2,1,0:T(8,128)(2,1)S(1)}, bf16[2,2,320,128]{3,2,1,0:T(8,128)(2,1)S(1)}, u32[]{:S(2)}, u32[]{:S(2)}) collective-permute-start(bf16[2,2,320,128]{3,2,1,0:T(8,128)(2,1)S(1)} %get-tuple-element.54), channel_id=1, source_target_pairs={{0,64},{32,96},{64,0},{96,32},{1,65},{33,97},{65,1},{97,33},{2,66}... | collective-permute-start | bytes 983048 | tf_op jit(solution)/shard_map/ppermute | solution.py:416
  18.2 14.2 %collective-permute-start.3 = (bf16[2,2,320,128]{3,2,1,0:T(8,128)(2,1)S(1)}, bf16[2,2,320,128]{3,2,1,0:T(8,128)(2,1)S(1)}, u32[]{:S(2)}, u32[]{:S(2)}) collective-permute-start(bf16[2,2,320,128]{3,2,1,0:T(8,128)(2,1)S(1)} %get-tuple-element.55), channel_id=1, source_target_pairs={{0,96},{32,0},{64,32},{96,64},{1,97},{33,1},{65,33},{97,65},{2,98}... | collective-permute-start | bytes 983048 | tf_op jit(solution)/shard_map/ppermute | solution.py:416
  32.5 9.6 %collective-permute-start.8 = (bf16[2,320,128]{2,1,0:T(8,128)(2,1)S(1)}, bf16[2,320,128]{2,1,0:T(8,128)(2,1)S(1)}, u32[]{:S(2)}, u32[]{:S(2)}) collective-permute-start(bf16[2,320,128]{2,1,0:T(8,128)(2,1)S(1)} %get-tuple-element.94), channel_id=1, source_target_pairs={{0,96},{32,0},{64,32},{96,64},{1,97},{33,1},{65,33},{97,65},{2,98}... | collective-permute-start | bytes 491528 | tf_op jit(solution)/shard_map/ppermute | solution.py:416
  35.4 6.7 %collective-permute-start.7 = (bf16[2,320,128]{2,1,0:T(8,128)(2,1)S(1)}, bf16[2,320,128]{2,1,0:T(8,128)(2,1)S(1)}, u32[]{:S(2)}, u32[]{:S(2)}) collective-permute-start(bf16[2,320,128]{2,1,0:T(8,128)(2,1)S(1)} %get-tuple-element.95), channel_id=1, source_target_pairs={{0,64},{32,96},{64,0},{96,32},{1,65},{33,97},{65,1},{97,33},{2,66}... | collective-permute-start | bytes 491528 | tf_op jit(solution)/shard_map/ppermute | solution.py:416
  35.8 10.8 %collective-permute-start.6 = (bf16[2,320,128]{2,1,0:T(8,128)(2,1)S(1)}, bf16[2,320,128]{2,1,0:T(8,128)(2,1)S(1)}, u32[]{:S(2)}, u32[]{:S(2)}) collective-permute-start(bf16[2,320,128]{2,1,0:T(8,128)(2,1)S(1)} %get-tuple-element.96), channel_id=1, source_target_pairs={{0,32},{32,64},{64,96},{96,0},{1,33},{33,65},{65,97},{97,1},{2,34}... | collective-permute-start | bytes 491528 | tf_op jit(solution)/shard_map/ppermute | solution.py:416
  36.2 10.3 %collective-permute-start.5 = (bf16[2,320,128]{2,1,0:T(8,128)(2,1)S(1)}, bf16[2,320,128]{2,1,0:T(8,128)(2,1)S(1)}, u32[]{:S(2)}, u32[]{:S(2)}) collective-permute-start(bf16[2,320,128]{2,1,0:T(8,128)(2,1)S(1)} %get-tuple-element.98), channel_id=1, source_target_pairs={{0,16},{16,0},{1,17},{17,1},{2,18},{18,2},{3,19},{19,3},{4,20},{20... | collective-permute-start | bytes 491528 | tf_op jit(solution)/shard_map/ppermute | solution.py:416
  94.3 16.2 %collective-permute-start.9 = (bf16[32,40,128]{2,1,0:T(8,128)(2,1)S(1)}, bf16[32,40,128]{2,1,0:T(8,128)(2,1)S(1)}, u32[]{:S(2)}, u32[]{:S(2)}) collective-permute-start(bf16[32,40,128]{2,1,0:T(8,128)(2,1)S(1)} %get-tuple-element.65.here_ref), channel_id=1, source_target_pairs={{0,16},{16,0},{1,17},{17,1},{2,18},{18,2},{3,19},{19,3},{4,20},{20... | collective-permute-start | bytes 983048 | tf_op jit(solution)/shard_map/ppermute | solution.py:416
  115.7 38.5 %all-to-all-start.2 = ((bf16[8,2,640,128]{3,2,1,0:T(8,128)(2,1)}), bf16[8,2,640,128]{3,2,1,0:T(8,128)(2,1)S(1)}, u32[]{:S(2)}, u32[]{:S(2)}) async-start(bf16[8,2,640,128]{3,2,1,0:T(8,128)(2,1)} %get-tuple-element.68), calls=%async_computation.2 | async-start | bytes 5242880 | tf_op jit(solution)/shard_map/all_to_all | solution.py:411
  119.3 16.9 %collective-permute-start.11 = (bf16[2,32,40,128]{3,2,1,0:T(8,128)(2,1)}, bf16[2,32,40,128]{3,2,1,0:T(8,128)(2,1)S(1)}, u32[]{:S(2)}, u32[]{:S(2)}) collective-permute-start(bf16[2,32,40,128]{3,2,1,0:T(8,128)(2,1)} %get-tuple-element.79.refs_0_), channel_id=1, source_target_pairs={{0,64},{32,96},{64,0},{96,32},{1,65},{33,97},{65,1},{97,33},{2,66}... | collective-permute-start | bytes 1966088 | tf_op jit(solution)/shard_map/ppermute | solution.py:416
  120.7 31.1 %collective-permute-start.10 = (bf16[2,32,40,128]{3,2,1,0:T(8,128)(2,1)}, bf16[2,32,40,128]{3,2,1,0:T(8,128)(2,1)S(1)}, u32[]{:S(2)}, u32[]{:S(2)}) collective-permute-start(bf16[2,32,40,128]{3,2,1,0:T(8,128)(2,1)} %get-tuple-element.79.refs_0_), channel_id=1, source_target_pairs={{0,32},{32,64},{64,96},{96,0},{1,33},{33,65},{65,97},{97,1},{2,34}... | collective-permute-start | bytes 1966088 | tf_op jit(solution)/shard_map/ppermute | solution.py:416
  120.8 31.5 %collective-permute-start.13 = (bf16[2,32,40,128]{3,2,1,0:T(8,128)(2,1)}, bf16[2,32,40,128]{3,2,1,0:T(8,128)(2,1)S(1)}, u32[]{:S(2)}, u32[]{:S(2)}) collective-permute-start(bf16[2,32,40,128]{3,2,1,0:T(8,128)(2,1)} %get-tuple-element.79.refs_0_), channel_id=1, source_target_pairs={{0,8},{8,0},{1,9},{9,1},{2,10},{10,2},{3,11},{11,3},{4,12},{12,4},... | collective-permute-start | bytes 1966088 | tf_op jit(solution)/shard_map/ppermute | solution.py:416
  122.2 30.0 %collective-permute-start.12 = (bf16[2,32,40,128]{3,2,1,0:T(8,128)(2,1)}, bf16[2,32,40,128]{3,2,1,0:T(8,128)(2,1)S(1)}, u32[]{:S(2)}, u32[]{:S(2)}) collective-permute-start(bf16[2,32,40,128]{3,2,1,0:T(8,128)(2,1)} %get-tuple-element.79.refs_0_), channel_id=1, source_target_pairs={{0,96},{32,0},{64,32},{96,64},{1,97},{33,1},{65,33},{97,65},{2,98}... | collective-permute-start | bytes 1966088 | tf_op jit(solution)/shard_map/ppermute | solution.py:416
  136.2 16.1 %collective-permute-start.15 = (bf16[2,32,40,128]{3,2,1,0:T(8,128)(2,1)S(1)}, bf16[2,32,40,128]{3,2,1,0:T(8,128)(2,1)S(1)}, u32[]{:S(2)}, u32[]{:S(2)}) collective-permute-start(bf16[2,32,40,128]{3,2,1,0:T(8,128)(2,1)S(1)} %collective-permute-done.11.refs_2_), channel_id=1, source_target_pairs={{0,8},{8,0},{1,9},{9,1},{2,10},{10,2},{3,11},{11,3},{4,12},{12,4},... | collective-permute-start | bytes 1966088 | tf_op jit(solution)/shard_map/ppermute | solution.py:416
  151.8 2.4 %collective-permute-start.14 = (bf16[2,32,40,128]{3,2,1,0:T(8,128)(2,1)S(1)}, bf16[2,32,40,128]{3,2,1,0:T(8,128)(2,1)}, u32[]{:S(2)}, u32[]{:S(2)}) collective-permute-start(bf16[2,32,40,128]{3,2,1,0:T(8,128)(2,1)S(1)} %collective-permute-done.10.refs_1_), channel_id=1, source_target_pairs={{0,8},{8,0},{1,9},{9,1},{2,10},{10,2},{3,11},{11,3},{4,12},{12,4},... | collective-permute-start | bytes 1966088 | tf_op jit(solution)/shard_map/ppermute | solution.py:416
  154.2 12.4 %collective-permute-start.20 = (bf16[2,32,40,128]{3,2,1,0:T(8,128)(2,1)}, bf16[2,32,40,128]{3,2,1,0:T(8,128)(2,1)S(1)}, u32[]{:S(2)}, u32[]{:S(2)}) collective-permute-start(bf16[2,32,40,128]{3,2,1,0:T(8,128)(2,1)} %copy-done.9), channel_id=1, source_target_pairs={{0,8},{8,0},{1,9},{9,1},{2,10},{10,2},{3,11},{11,3},{4,12},{12,4},... | collective-permute-start | bytes 1966088 | tf_op jit(solution)/shard_map/ppermute | solution.py:416
  155.1 8.5 %collective-permute-start.19 = (bf16[2,320,128]{2,1,0:T(8,128)(2,1)S(1)}, bf16[2,320,128]{2,1,0:T(8,128)(2,1)S(1)}, u32[]{:S(2)}, u32[]{:S(2)}) collective-permute-start(bf16[2,320,128]{2,1,0:T(8,128)(2,1)S(1)} %get-tuple-element.74), channel_id=1, source_target_pairs={{0,96},{32,0},{64,32},{96,64},{1,97},{33,1},{65,33},{97,65},{2,98}... | collective-permute-start | bytes 491528 | tf_op jit(solution)/shard_map/ppermute | solution.py:416
  155.5 8.1 %collective-permute-start.18 = (bf16[2,320,128]{2,1,0:T(8,128)(2,1)S(1)}, bf16[2,320,128]{2,1,0:T(8,128)(2,1)S(1)}, u32[]{:S(2)}, u32[]{:S(2)}) collective-permute-start(bf16[2,320,128]{2,1,0:T(8,128)(2,1)S(1)} %get-tuple-element.74), channel_id=1, source_target_pairs={{0,64},{32,96},{64,0},{96,32},{1,65},{33,97},{65,1},{97,33},{2,66}... | collective-permute-start | bytes 491528 | tf_op jit(solution)/shard_map/ppermute | solution.py:416
  156.8 9.8 %collective-permute-start.17 = (bf16[2,320,128]{2,1,0:T(8,128)(2,1)S(1)}, bf16[2,320,128]{2,1,0:T(8,128)(2,1)S(1)}, u32[]{:S(2)}, u32[]{:S(2)}) collective-permute-start(bf16[2,320,128]{2,1,0:T(8,128)(2,1)S(1)} %get-tuple-element.74), channel_id=1, source_target_pairs={{0,32},{32,64},{64,96},{96,0},{1,33},{33,65},{65,97},{97,1},{2,34}... | collective-permute-start | bytes 491528 | tf_op jit(solution)/shard_map/ppermute | solution.py:416
  157.4 6.2 %collective-permute-start.16 = (bf16[2,320,128]{2,1,0:T(8,128)(2,1)S(1)}, bf16[2,320,128]{2,1,0:T(8,128)(2,1)S(1)}, u32[]{:S(2)}, u32[]{:S(2)}) collective-permute-start(bf16[2,320,128]{2,1,0:T(8,128)(2,1)S(1)} %get-tuple-element.71), channel_id=1, source_target_pairs={{0,16},{16,0},{1,17},{17,1},{2,18},{18,2},{3,19},{19,3},{4,20},{20... | collective-permute-start | bytes 491528 | tf_op jit(solution)/shard_map/ppermute | solution.py:416
  166.7 19.7 %collective-permute-start.21 = (bf16[4,2,320,128]{3,2,1,0:T(8,128)(2,1)S(1)}, bf16[4,2,320,128]{3,2,1,0:T(8,128)(2,1)S(1)}, u32[]{:S(2)}, u32[]{:S(2)}) collective-permute-start(bf16[4,2,320,128]{3,2,1,0:T(8,128)(2,1)S(1)} %pad_maximum_fusion.refs_0_), channel_id=1, source_target_pairs={{0,16},{16,0},{1,17},{17,1},{2,18},{18,2},{3,19},{19,3},{4,20},{20... | collective-permute-start | bytes 1966088 | tf_op jit(solution)/shard_map/ppermute | solution.py:416
  168.1 8.9 %collective-permute-start.24 = (bf16[2,2,320,128]{3,2,1,0:T(8,128)(2,1)S(1)}, bf16[2,2,320,128]{3,2,1,0:T(8,128)(2,1)S(1)}, u32[]{:S(2)}, u32[]{:S(2)}) collective-permute-start(bf16[2,2,320,128]{3,2,1,0:T(8,128)(2,1)S(1)} %pad_maximum_fusion.1.refs_0_), channel_id=1, source_target_pairs={{0,96},{32,0},{64,32},{96,64},{1,97},{33,1},{65,33},{97,65},{2,98}... | collective-permute-start | bytes 983048 | tf_op jit(solution)/shard_map/ppermute | solution.py:416
  168.2 9.2 %collective-permute-start.23 = (bf16[2,2,320,128]{3,2,1,0:T(8,128)(2,1)S(1)}, bf16[2,2,320,128]{3,2,1,0:T(8,128)(2,1)S(1)}, u32[]{:S(2)}, u32[]{:S(2)}) collective-permute-start(bf16[2,2,320,128]{3,2,1,0:T(8,128)(2,1)S(1)} %pad_maximum_fusion.1.refs_0_), channel_id=1, source_target_pairs={{0,64},{32,96},{64,0},{96,32},{1,65},{33,97},{65,1},{97,33},{2,66}... | collective-permute-start | bytes 983048 | tf_op jit(solution)/shard_map/ppermute | solution.py:416
  169.1 17.3 %collective-permute-start.22 = (bf16[2,2,320,128]{3,2,1,0:T(8,128)(2,1)S(1)}, bf16[2,2,320,128]{3,2,1,0:T(8,128)(2,1)S(1)}, u32[]{:S(2)}, u32[]{:S(2)}) collective-permute-start(bf16[2,2,320,128]{3,2,1,0:T(8,128)(2,1)S(1)} %pad_maximum_fusion.1.refs_0_), channel_id=1, source_target_pairs={{0,32},{32,64},{64,96},{96,0},{1,33},{33,65},{65,97},{97,1},{2,34}... | collective-permute-start | bytes 983048 | tf_op jit(solution)/shard_map/ppermute | solution.py:416
  169.9 17.6 %collective-permute-start.29 = (bf16[4,2,320,128]{3,2,1,0:T(8,128)(2,1)S(1)}, bf16[4,2,320,128]{3,2,1,0:T(8,128)(2,1)S(1)}, u32[]{:S(2)}, u32[]{:S(2)}) collective-permute-start(bf16[4,2,320,128]{3,2,1,0:T(8,128)(2,1)S(1)} %pad_maximum_fusion.refs_0_), channel_id=1, source_target_pairs={{0,8},{8,0},{1,9},{9,1},{2,10},{10,2},{3,11},{11,3},{4,12},{12,4},... | collective-permute-start | bytes 1966088 | tf_op jit(solution)/shard_map/ppermute | solution.py:416
  186.4 2.2 %collective-permute-start.30 = (bf16[4,2,320,128]{3,2,1,0:T(8,128)(2,1)S(1)}, bf16[4,2,320,128]{3,2,1,0:T(8,128)(2,1)S(1)}, u32[]{:S(2)}, u32[]{:S(2)}) collective-permute-start(bf16[4,2,320,128]{3,2,1,0:T(8,128)(2,1)S(1)} %collective-permute-done.21.refs_1_), channel_id=1, source_target_pairs={{0,8},{8,0},{1,9},{9,1},{2,10},{10,2},{3,11},{11,3},{4,12},{12,4},... | collective-permute-start | bytes 1966088 | tf_op jit(solution)/shard_map/ppermute | solution.py:416
  186.9 3.8 %collective-permute-start.25 = (bf16[2,2,320,128]{3,2,1,0:T(8,128)(2,1)S(1)}, bf16[2,2,320,128]{3,2,1,0:T(8,128)(2,1)S(1)}, u32[]{:S(2)}, u32[]{:S(2)}) collective-permute-start(bf16[2,2,320,128]{3,2,1,0:T(8,128)(2,1)S(1)} %pad_maximum_fusion.1.refs_0_), channel_id=1, source_target_pairs={{0,8},{8,0},{1,9},{9,1},{2,10},{10,2},{3,11},{11,3},{4,12},{12,4},... | collective-permute-start | bytes 983048 | tf_op jit(solution)/shard_map/ppermute | solution.py:416
  186.9 3.8 %collective-permute-start.26 = (bf16[2,2,320,128]{3,2,1,0:T(8,128)(2,1)S(1)}, bf16[2,2,320,128]{3,2,1,0:T(8,128)(2,1)S(1)}, u32[]{:S(2)}, u32[]{:S(2)}) collective-permute-start(bf16[2,2,320,128]{3,2,1,0:T(8,128)(2,1)S(1)} %collective-permute-done.22.refs_1_), channel_id=1, source_target_pairs={{0,8},{8,0},{1,9},{9,1},{2,10},{10,2},{3,11},{11,3},{4,12},{12,4},... | collective-permute-start | bytes 983048 | tf_op jit(solution)/shard_map/ppermute | solution.py:416
  187.4 3.3 %collective-permute-start.27 = (bf16[2,2,320,128]{3,2,1,0:T(8,128)(2,1)S(1)}, bf16[2,2,320,128]{3,2,1,0:T(8,128)(2,1)S(1)}, u32[]{:S(2)}, u32[]{:S(2)}) collective-permute-start(bf16[2,2,320,128]{3,2,1,0:T(8,128)(2,1)S(1)} %collective-permute-done.23.refs_2_), channel_id=1, source_target_pairs={{0,8},{8,0},{1,9},{9,1},{2,10},{10,2},{3,11},{11,3},{4,12},{12,4},... | collective-permute-start | bytes 983048 | tf_op jit(solution)/shard_map/ppermute | solution.py:416
  187.4 3.2 %collective-permute-start.28 = (bf16[2,2,320,128]{3,2,1,0:T(8,128)(2,1)S(1)}, bf16[2,2,320,128]{3,2,1,0:T(8,128)(2,1)S(1)}, u32[]{:S(2)}, u32[]{:S(2)}) collective-permute-start(bf16[2,2,320,128]{3,2,1,0:T(8,128)(2,1)S(1)} %collective-permute-done.24.refs_3_), channel_id=1, source_target_pairs={{0,8},{8,0},{1,9},{9,1},{2,10},{10,2},{3,11},{11,3},{4,12},{12,4},... | collective-permute-start | bytes 983048 | tf_op jit(solution)/shard_map/ppermute | solution.py:416
  (12 other events, 207.0 us)

commit v5 on v4

--- a/solution.py
+++ b/solution.py
@@ -224,7 +224,8 @@
     )(*resident(spectra, reflection, here, far))
 
 
-def sum_kernel(p_ref, a_ref, b_ref):
+def sum_kernel(p_ref, *refs):
+    a_ref, b_ref = refs[-2:]
     total = p_ref[0].astype(jnp.float32)
     for i in range(1, 8):
         total = total + p_ref[i].astype(jnp.float32)
@@ -233,17 +234,22 @@
     b_ref[...] = total[:, HALF:]
 
 
-def summed_halves(parts):
+def in_hbm(arrays):
+    return [pltpu.with_memory_space_constraint(array, pltpu.HBM) for array in arrays]
+
+
+def summed_halves(parts, after):
     return pl.pallas_call(
         sum_kernel,
         out_shape=[jax.ShapeDtypeStruct((2, HALF, 128), jnp.bfloat16)] * 2,
         grid=(2,),
-        in_specs=[pl.BlockSpec((8, 1, 640, 128), lambda i: (0, i, 0, 0))],
+        in_specs=[pl.BlockSpec((8, 1, 640, 128), lambda i: (0, i, 0, 0))]
+        + [pl.BlockSpec(memory_space=pl.ANY)] * len(after),
         out_specs=[pl.BlockSpec((1, HALF, 128), lambda i: (i, 0, 0))] * 2,
         compiler_params=params(),
         cost_estimate=cost(1 << 20, 3 << 20),
         name="summed_halves",
-    )(parts)
+    )(parts, *in_hbm(after))
 
 
 def lanes(rows):
@@ -282,11 +288,11 @@
 
     def body(i, carry):
         field = dot(wi_ref[i], flat)
-        minus = kept(field, i * 64, onsets).astype(jnp.bfloat16)
+        minus = kept(field, i * 128, onsets).astype(jnp.bfloat16)
         acc[...] += dot(wf_ref[i], minus)
         return carry
 
-    lax.fori_loop(0, 4, body, 0)
+    lax.fori_loop(0, 2, body, 0)
     out_ref[...] = unlanes(acc[...]).astype(jnp.bfloat16).reshape(NF, 2, 40, 128)
 
 
@@ -300,8 +306,8 @@
 
 
 def middle(dev, parts, onsets):
-    wi = jnp.asarray(inverse_weights(64))
-    wf = jnp.asarray(forward_weights(64))
+    wi = jnp.asarray(inverse_weights(128))
+    wf = jnp.asarray(forward_weights(128))
     return pl.pallas_call(
         lambda d, *refs: middle_kernel(*refs),
         out_shape=(
@@ -352,7 +358,7 @@
         compiler_params=params(),
         cost_estimate=cost(700 << 20, 8 << 20),
         name="minus_output",
-    )(dev, *[pltpu.with_memory_space_constraint(v, pltpu.HBM) for v in parts], onsets, weights)
+    )(dev, *in_hbm(parts), onsets, weights)
 
 
 def plus_kernel(half, dev_ref, *refs):
@@ -423,7 +429,7 @@
     return total.astype(jnp.bfloat16)
 
 
-STEPS = (2, 1, 3)
+STEPS = (1, 3, 2)
 
 
 def start_spectra(dev, x):
@@ -462,9 +468,9 @@
     summed, spectra = middle(dev, start_parts.reshape(8, NF, 2, 40, 128), blocks)
     spectra, far = together(exchange(spectra, FREQ), along(summed, "xh", 1))
     parts, near = minus_product(spectra, reflection, summed, far)
-    parts, mine, others = together(exchange(parts, SRC), *rest_of(near))
-
-    a, b = summed_halves(parts)
+    parts, (mine, others) = exchange(parts, SRC), rest_of(near)
+
+    a, b = summed_halves(parts, [*mine[1:], *others])
     weights = of_device(inverse_weights(16), dev), of_device(last_weights(), dev)
     last = along(mine[3], "core", 1)
     b_far, a_near, last, weights = together(along(b, "xh", 1), around([a] * 4, "z"), last, weights)

time: 193 us -> 193 us (level)
  transfers between devices with their start and end apart: 32 -> 32, of which waited for: 12 -> 13; matrix products, arithmetic and copies ran while one was open for 2% -> 2% of each run, Pallas kernels for 4% -> 4%
where the time goes in v5:
time: 193 us; the launch traced here: 192 us
  waiting for transfers between devices  68.3 us (35%)
  blocking collectives  55.2 us (29%)
  starting transfers between devices  38.3 us (20%)
  Pallas kernels  23.2 us (12%)
  local copies, waits for them, and re-layouts  6.23 us (3%)
    ppermute x31, waiting for transfers between devices, along(): return lax.ppermute(x, axis, [(i, (i + step) % size) for i in range(size)])  68.3 us
    all_to_all x2, blocking collectives, exchange(): return lax.all_to_all(x, axes, 0, 0, tiled=True)  55.2 us
    ppermute x31, starting transfers between devices, along(): return lax.ppermute(x, axis, [(i, (i + step) % size) for i in range(size)])  34.7 us
    pallas_call x1, Pallas kernels, minus_product(): pl.pallas_call(minus_product_kernel, out_shape=[pltpu.HBM((8, 2, 640, 128...  5.11 us
    pallas_call x1, Pallas kernels, minus_output(): pl.pallas_call(minus_kernel, out_shape=jax.ShapeDtypeStruct((16, 640, 128...  5.07 us
    pallas_call x1, Pallas kernels, start_product(): pl.pallas_call(functools.partial(start_product_kernel, counts), out_shape...  4.22 us
    pallas_call x2, Pallas kernels, plus_output(): pl.pallas_call(functools.partial(plus_kernel, half), out_shape=jax.ShapeD...  4.12 us
  transfers between devices with their start and end apart: 32, of which 13 were waited for; matrix products, arithmetic and copies ran while one was open for 2% of the time, Pallas kernels for 4%

profile of v5, /device:TPU:1, one launch (start us, length us, event | category | flops | bytes accessed | tf_op | source)
XLA Modules:
  0.0 192.5 jit_solution(905380856734985421)
XLA Ops:
  0.6 1.5 collective-permute-start
  3.1 3.8 %collective-permute-done.xo_ref = bf16[16,640,128]{2,1,0:T(8,128)(2,1)S(1)} collective-permute-done((bf16[16,640,128]{2,1,0:T(8,128)(2,1)}, bf16[16,640,128]{2,1,0:T(8,128)(2,1)S(1)}, u32[]{:S(2)}, u32[]{:S(2)}) %collective-permute-start) | collective-permute-done | bytes 2621472 | tf_op jit(solution)/shard_map/ppermute | solution.py:422
  6.9 1.7 copy-done
  10.3 2.9 %collective-permute-start.4 = (bf16[4,2,320,128]{3,2,1,0:T(8,128)(2,1)S(1)}, bf16[4,2,320,128]{3,2,1,0:T(8,128)(2,1)S(1)}, u32[]{:S(2)}, u32[]{:S(2)}) collective-permute-start(bf16[4,2,320,128]{3,2,1,0:T(8,128)(2,1)S(1)} %get-tuple-element.49), channel_id=1, source_target_pairs={{0,16},{16,0},{1,17},{17,1},{2,18},{18,2},{3,19},{19,3},{4,20},{20... | collective-permute-start | bytes 1966088 | tf_op jit(solution)/shard_map/ppermute | solution.py:422
  13.2 1.6 collective-permute-start.1
  14.9 3.3 %collective-permute-start.2 = (bf16[2,2,320,128]{3,2,1,0:T(8,128)(2,1)S(1)}, bf16[2,2,320,128]{3,2,1,0:T(8,128)(2,1)S(1)}, u32[]{:S(2)}, u32[]{:S(2)}) collective-permute-start(bf16[2,2,320,128]{3,2,1,0:T(8,128)(2,1)S(1)} %get-tuple-element.46), channel_id=1, source_target_pairs={{0,64},{32,96},{64,0},{96,32},{1,65},{33,97},{65,1},{97,33},{2,66}... | collective-permute-start | bytes 983048 | tf_op jit(solution)/shard_map/ppermute | solution.py:422
  18.9 5.5 %collective-permute-done.1 = bf16[2,2,320,128]{3,2,1,0:T(8,128)(2,1)S(1)} collective-permute-done((bf16[2,2,320,128]{3,2,1,0:T(8,128)(2,1)S(1)}, bf16[2,2,320,128]{3,2,1,0:T(8,128)(2,1)S(1)}, u32[]{:S(2)}, u32[]{:S(2)}) %collective-permute-start.1) | collective-permute-done | bytes 327712 | tf_op jit(solution)/shard_map/ppermute | solution.py:422
  24.4 7.9 %collective-permute-done.2 = bf16[2,2,320,128]{3,2,1,0:T(8,128)(2,1)S(1)} collective-permute-done((bf16[2,2,320,128]{3,2,1,0:T(8,128)(2,1)S(1)}, bf16[2,2,320,128]{3,2,1,0:T(8,128)(2,1)S(1)}, u32[]{:S(2)}, u32[]{:S(2)}) %collective-permute-start.2) | collective-permute-done | bytes 327712 | tf_op jit(solution)/shard_map/ppermute | solution.py:422
  32.5 2.9 %collective-permute-start.8 = (bf16[2,320,128]{2,1,0:T(8,128)(2,1)S(1)}, bf16[2,320,128]{2,1,0:T(8,128)(2,1)S(1)}, u32[]{:S(2)}, u32[]{:S(2)}) collective-permute-start(bf16[2,320,128]{2,1,0:T(8,128)(2,1)S(1)} %get-tuple-element.78), channel_id=1, source_target_pairs={{0,96},{32,0},{64,32},{96,64},{1,97},{33,1},{65,33},{97,65},{2,98}... | collective-permute-start | bytes 491528 | tf_op jit(solution)/shard_map/ppermute | solution.py:422
  36.6 5.6 %collective-permute-done.8.refs_5_ = bf16[2,320,128]{2,1,0:T(8,128)(2,1)S(1)} collective-permute-done((bf16[2,320,128]{2,1,0:T(8,128)(2,1)S(1)}, bf16[2,320,128]{2,1,0:T(8,128)(2,1)S(1)}, u32[]{:S(2)}, u32[]{:S(2)}) %collective-permute-start.8) | collective-permute-done | bytes 163872 | tf_op jit(solution)/shard_map/ppermute | solution.py:422
  42.1 4.4 %collective-permute-done.6.refs_3_ = bf16[2,320,128]{2,1,0:T(8,128)(2,1)S(1)} collective-permute-done((bf16[2,320,128]{2,1,0:T(8,128)(2,1)S(1)}, bf16[2,320,128]{2,1,0:T(8,128)(2,1)S(1)}, u32[]{:S(2)}, u32[]{:S(2)}) %collective-permute-start.6) | collective-permute-done | bytes 163872 | tf_op jit(solution)/shard_map/ppermute | solution.py:422
  46.5 4.2 %start_product.1 = bf16[128,2,40,128]{3,2,1,0:T(8,128)(2,1)S(1)} custom-call(bf16[2,320,128]{2,1,0:T(8,128)(2,1)S(1)} %get-tuple-element.83.refs_0_, bf16[2,320,128]{2,1,0:T(8,128)(2,1)S(1)} %collective-permute-done.5.refs_1_, bf16[2,320,128]{2,1,0:T(8,128)(2,1)S(1)} %get-tuple-element.81.refs_2_, bf16[2,320,128]{2,1,0:T(8,128)(2,1)S(1)} %collective-permute-done.6.refs_3_, ...), custom_call_target="tpu_custom_call" | custom-call | flops 4294967296 | bytes 18874368 | tf_op jit(solution)/shard_map/start_product/pallas_call | solution.py:174
  50.8 40.6 %all_to_all.15 = bf16[128,2,40,128]{3,2,1,0:T(8,128)(2,1)S(1)} all-to-all(bf16[128,2,40,128]{3,2,1,0:T(8,128)(2,1)S(1)} %start_product.1), channel_id=1, replica_groups=mesh['z'=4,'xh'=2,'core'=2,'y'=4,'xl'=2] {'y','xl','z','xh','core'}, dimensions={0} | all-to-all | bytes 5242880 | tf_op jit(solution)/shard_map/all_to_all | solution.py:417
  91.4 2.4 %middle.1 = (bf16[32,40,128]{2,1,0:T(8,128)(2,1)S(1)}, bf16[16,2,40,128]{3,2,1,0:T(8,128)(2,1)S(1)}) custom-call(s32[1]{0:T(128)} %bitcast.d.dev_ref, bf16[8,16,2,40,128]{4,3,2,1,0:T(8,128)(2,1)S(1)} %bitcast.29, s32[16,40,128]{2,1,0:T(8,128)S(1)} %bitcast.27, bf16[2,1024,256]{2,1,0:T(8,128)(2,1)S(1)} %copy-done.5, bf16[2,256,1024]{2,1,0:T(8,128)(2,1)S(1)} %copy-done.4), custom_call_target="tpu_custom_call" | custom-call | flops 2147483648 | bytes 8388608 | tf_op jit(solution)/shard_map/middle/pallas_call | solution.py:311
  93.8 1.6 collective-permute-start.9
  95.4 14.6 %all_to_all.16.s_ref = bf16[16,2,40,128]{3,2,1,0:T(8,128)(2,1)S(1)} all-to-all(bf16[16,2,40,128]{3,2,1,0:T(8,128)(2,1)S(1)} %get-tuple-element.56), channel_id=1, replica_groups=mesh['z'=4,'xh'=2,'core'=2,'y'=4,'xl'=2] {'z','xh','core'}, dimensions={0} | all-to-all | bytes 655360 | tf_op jit(solution)/shard_map/all_to_all | solution.py:417
  110.0 5.1 %minus_product.1 = (bf16[8,2,640,128]{3,2,1,0:T(8,128)(2,1)}, bf16[2,32,40,128]{3,2,1,0:T(8,128)(2,1)}) custom-call(bf16[16,2,40,128]{3,2,1,0:T(8,128)(2,1)S(1)} %all_to_all.16.s_ref, bf16[2,1,5120,640]{3,2,1,0:T(8,128)(2,1)S(1)} %copy-done.2, bf16[32,40,128]{2,1,0:T(8,128)(2,1)S(1)} %get-tuple-element.57.here_ref, ...), custom_call_target="tpu_custom_call" | custom-call | flops 4294967296 | bytes 18874368 | tf_op jit(solution)/shard_map/minus_product/pallas_call | solution.py:207
  115.2 3.6 %all-to-all-start.2 = ((bf16[8,2,640,128]{3,2,1,0:T(8,128)(2,1)}), bf16[8,2,640,128]{3,2,1,0:T(8,128)(2,1)S(1)}, u32[]{:S(2)}, u32[]{:S(2)}) async-start(bf16[8,2,640,128]{3,2,1,0:T(8,128)(2,1)} %get-tuple-element.60), calls=%async_computation.2 | async-start | bytes 5242880 | tf_op jit(solution)/shard_map/all_to_all | solution.py:417
  118.8 1.4 collective-permute-start.11
  120.3 2.6 %collective-permute-start.12 = (bf16[2,32,40,128]{3,2,1,0:T(8,128)(2,1)}, bf16[2,32,40,128]{3,2,1,0:T(8,128)(2,1)}, u32[]{:S(2)}, u32[]{:S(2)}) collective-permute-start(bf16[2,32,40,128]{3,2,1,0:T(8,128)(2,1)} %get-tuple-element.61.refs_0_), channel_id=1, source_target_pairs={{0,96},{32,0},{64,32},{96,64},{1,97},{33,1},{65,33},{97,65},{2,98}... | collective-permute-start | bytes 1966088 | tf_op jit(solution)/shard_map/ppermute | solution.py:422
  122.9 1.2 collective-permute-start.13
  124.1 11.6 %collective-permute-done.11.refs_1_.refs_2_ = bf16[2,32,40,128]{3,2,1,0:T(8,128)(2,1)S(1)} collective-permute-done((bf16[2,32,40,128]{3,2,1,0:T(8,128)(2,1)}, bf16[2,32,40,128]{3,2,1,0:T(8,128)(2,1)S(1)}, u32[]{:S(2)}, u32[]{:S(2)}) %collective-permute-start.11) | collective-permute-done | bytes 655392 | tf_op jit(solution)/shard_map/ppermute | solution.py:422
  135.7 3.8 %collective-permute-start.15 = (bf16[2,32,40,128]{3,2,1,0:T(8,128)(2,1)S(1)}, bf16[2,32,40,128]{3,2,1,0:T(8,128)(2,1)S(1)}, u32[]{:S(2)}, u32[]{:S(2)}) collective-permute-start(bf16[2,32,40,128]{3,2,1,0:T(8,128)(2,1)S(1)} %collective-permute-done.11.refs_1_.refs_2_), channel_id=1, source_target_pairs={{0,8},{8,0},{1,9},{9,1},{2,10},{10,2},{3,11},{11,3},{4,12},{12,4},... | collective-permute-start | bytes 1966088 | tf_op jit(solution)/shard_map/ppermute | solution.py:422
  139.5 11.8 %collective-permute-done.10.refs_0_.refs_1_ = bf16[2,32,40,128]{3,2,1,0:T(8,128)(2,1)S(1)} collective-permute-done((bf16[2,32,40,128]{3,2,1,0:T(8,128)(2,1)}, bf16[2,32,40,128]{3,2,1,0:T(8,128)(2,1)S(1)}, u32[]{:S(2)}, u32[]{:S(2)}) %collective-permute-start.10) | collective-permute-done | bytes 655392 | tf_op jit(solution)/shard_map/ppermute | solution.py:422
  159.3 3.4 %collective-permute-done.16 = bf16[2,320,128]{2,1,0:T(8,128)(2,1)S(1)} collective-permute-done((bf16[2,320,128]{2,1,0:T(8,128)(2,1)S(1)}, bf16[2,320,128]{2,1,0:T(8,128)(2,1)S(1)}, u32[]{:S(2)}, u32[]{:S(2)}) %collective-permute-start.16) | collective-permute-done | bytes 163872 | tf_op jit(solution)/shard_map/ppermute | solution.py:422
  162.7 3.7 %collective-permute-done.17 = bf16[2,320,128]{2,1,0:T(8,128)(2,1)S(1)} collective-permute-done((bf16[2,320,128]{2,1,0:T(8,128)(2,1)S(1)}, bf16[2,320,128]{2,1,0:T(8,128)(2,1)S(1)}, u32[]{:S(2)}, u32[]{:S(2)}) %collective-permute-start.17) | collective-permute-done | bytes 163872 | tf_op jit(solution)/shard_map/ppermute | solution.py:422
  166.4 1.3 collective-permute-start.21
  169.4 1.8 collective-permute-start.29
  171.2 5.1 %minus_output.1 = bf16[16,640,128]{2,1,0:T(8,128)(2,1)} custom-call(s32[1]{0:T(128)} %bitcast.d.dev_ref, bf16[2,32,40,128]{3,2,1,0:T(8,128)(2,1)} %get-tuple-element.61.refs_0_, bf16[2,32,40,128]{3,2,1,0:T(8,128)(2,1)} %copy-done.7, bf16[2,32,40,128]{3,2,1,0:T(8,128)(2,1)} %copy-done.6, bf16[2,32,40,128]{3,2,1,0:T(8,128)(2,1)} %collective-permute-done.12.refs_2_.refs_3_, ...), custom_call_target="tpu_custom_call" | custom-call | flops 734003200 | bytes 8388608 | tf_op jit(solution)/shard_map/minus_output/pallas_call | solution.py:348
  177.4 8.7 %collective-permute-done.22.refs_1_ = bf16[2,2,320,128]{3,2,1,0:T(8,128)(2,1)S(1)} collective-permute-done((bf16[2,2,320,128]{3,2,1,0:T(8,128)(2,1)S(1)}, bf16[2,2,320,128]{3,2,1,0:T(8,128)(2,1)S(1)}, u32[]{:S(2)}, u32[]{:S(2)}) %collective-permute-start.22) | collective-permute-done | bytes 327712 | tf_op jit(solution)/shard_map/ppermute | solution.py:422
  188.3 2.0 %plus_output.2.refs_11_ = bf16[16,640,128]{2,1,0:T(8,128)(2,1)} custom-call(s32[1]{0:T(128)} %bitcast.d.dev_ref, bf16[4,2,320,128]{3,2,1,0:T(8,128)(2,1)S(1)} %pad_maximum_fusion.refs_0_, bf16[4,2,320,128]{3,2,1,0:T(8,128)(2,1)S(1)} %collective-permute-done.21.refs_1_, bf16[4,2,320,128]{3,2,1,0:T(8,128)(2,1)S(1)} %collective-permute-done.29.refs_2_, ...), custom_call_target="tpu_custom_call" | custom-call | flops 734003200 | bytes 6291456 | tf_op jit(solution)/shard_map/plus_output/pallas_call | solution.py:394
  190.4 2.1 %plus_output.3 = bf16[16,640,128]{2,1,0:T(8,128)(2,1)} custom-call(s32[1]{0:T(128)} %bitcast.d.dev_ref, bf16[2,2,320,128]{3,2,1,0:T(8,128)(2,1)S(1)} %pad_maximum_fusion.1.refs_0_, bf16[2,2,320,128]{3,2,1,0:T(8,128)(2,1)S(1)} %collective-permute-done.22.refs_1_, ...), custom_call_target="tpu_custom_call", output_to_operand_aliasing={{}: (12, {})} | custom-call | flops 734003200 | bytes 6291456 | tf_op jit(solution)/shard_map/plus_output/pallas_call | solution.py:394
  (70 shorter events, 17.9 us)
Async XLA Ops:
  0.6 6.2 %collective-permute-start = (bf16[16,640,128]{2,1,0:T(8,128)(2,1)}, bf16[16,640,128]{2,1,0:T(8,128)(2,1)S(1)}, u32[]{:S(2)}, u32[]{:S(2)}) collective-permute-start(bf16[16,640,128]{2,1,0:T(8,128)(2,1)} %refs_9_.1), channel_id=1, source_target_pairs={{0,8},{8,0},{1,9},{9,1},{2,10},{10,2},{3,11},{11,3},{4,12},{12,4},... | collective-permute-start | bytes 7864328 | tf_op jit(solution)/shard_map/ppermute | solution.py:422
  10.3 22.0 %collective-permute-start.4 = (bf16[4,2,320,128]{3,2,1,0:T(8,128)(2,1)S(1)}, bf16[4,2,320,128]{3,2,1,0:T(8,128)(2,1)S(1)}, u32[]{:S(2)}, u32[]{:S(2)}) collective-permute-start(bf16[4,2,320,128]{3,2,1,0:T(8,128)(2,1)S(1)} %get-tuple-element.49), channel_id=1, source_target_pairs={{0,16},{16,0},{1,17},{17,1},{2,18},{18,2},{3,19},{19,3},{4,20},{20... | collective-permute-start | bytes 1966088 | tf_op jit(solution)/shard_map/ppermute | solution.py:422
  13.2 11.2 %collective-permute-start.1 = (bf16[2,2,320,128]{3,2,1,0:T(8,128)(2,1)S(1)}, bf16[2,2,320,128]{3,2,1,0:T(8,128)(2,1)S(1)}, u32[]{:S(2)}, u32[]{:S(2)}) collective-permute-start(bf16[2,2,320,128]{3,2,1,0:T(8,128)(2,1)S(1)} %get-tuple-element.45), channel_id=1, source_target_pairs={{0,32},{32,64},{64,96},{96,0},{1,33},{33,65},{65,97},{97,1},{2,34}... | collective-permute-start | bytes 983048 | tf_op jit(solution)/shard_map/ppermute | solution.py:422
  14.9 17.5 %collective-permute-start.2 = (bf16[2,2,320,128]{3,2,1,0:T(8,128)(2,1)S(1)}, bf16[2,2,320,128]{3,2,1,0:T(8,128)(2,1)S(1)}, u32[]{:S(2)}, u32[]{:S(2)}) collective-permute-start(bf16[2,2,320,128]{3,2,1,0:T(8,128)(2,1)S(1)} %get-tuple-element.46), channel_id=1, source_target_pairs={{0,64},{32,96},{64,0},{96,32},{1,65},{33,97},{65,1},{97,33},{2,66}... | collective-permute-start | bytes 983048 | tf_op jit(solution)/shard_map/ppermute | solution.py:422
  18.2 14.2 %collective-permute-start.3 = (bf16[2,2,320,128]{3,2,1,0:T(8,128)(2,1)S(1)}, bf16[2,2,320,128]{3,2,1,0:T(8,128)(2,1)S(1)}, u32[]{:S(2)}, u32[]{:S(2)}) collective-permute-start(bf16[2,2,320,128]{3,2,1,0:T(8,128)(2,1)S(1)} %get-tuple-element.47), channel_id=1, source_target_pairs={{0,96},{32,0},{64,32},{96,64},{1,97},{33,1},{65,33},{97,65},{2,98}... | collective-permute-start | bytes 983048 | tf_op jit(solution)/shard_map/ppermute | solution.py:422
  32.5 9.6 %collective-permute-start.8 = (bf16[2,320,128]{2,1,0:T(8,128)(2,1)S(1)}, bf16[2,320,128]{2,1,0:T(8,128)(2,1)S(1)}, u32[]{:S(2)}, u32[]{:S(2)}) collective-permute-start(bf16[2,320,128]{2,1,0:T(8,128)(2,1)S(1)} %get-tuple-element.78), channel_id=1, source_target_pairs={{0,96},{32,0},{64,32},{96,64},{1,97},{33,1},{65,33},{97,65},{2,98}... | collective-permute-start | bytes 491528 | tf_op jit(solution)/shard_map/ppermute | solution.py:422
  35.4 6.7 %collective-permute-start.7 = (bf16[2,320,128]{2,1,0:T(8,128)(2,1)S(1)}, bf16[2,320,128]{2,1,0:T(8,128)(2,1)S(1)}, u32[]{:S(2)}, u32[]{:S(2)}) collective-permute-start(bf16[2,320,128]{2,1,0:T(8,128)(2,1)S(1)} %get-tuple-element.79), channel_id=1, source_target_pairs={{0,64},{32,96},{64,0},{96,32},{1,65},{33,97},{65,1},{97,33},{2,66}... | collective-permute-start | bytes 491528 | tf_op jit(solution)/shard_map/ppermute | solution.py:422
  35.8 10.8 %collective-permute-start.6 = (bf16[2,320,128]{2,1,0:T(8,128)(2,1)S(1)}, bf16[2,320,128]{2,1,0:T(8,128)(2,1)S(1)}, u32[]{:S(2)}, u32[]{:S(2)}) collective-permute-start(bf16[2,320,128]{2,1,0:T(8,128)(2,1)S(1)} %get-tuple-element.80), channel_id=1, source_target_pairs={{0,32},{32,64},{64,96},{96,0},{1,33},{33,65},{65,97},{97,1},{2,34}... | collective-permute-start | bytes 491528 | tf_op jit(solution)/shard_map/ppermute | solution.py:422
  36.2 10.3 %collective-permute-start.5 = (bf16[2,320,128]{2,1,0:T(8,128)(2,1)S(1)}, bf16[2,320,128]{2,1,0:T(8,128)(2,1)S(1)}, u32[]{:S(2)}, u32[]{:S(2)}) collective-permute-start(bf16[2,320,128]{2,1,0:T(8,128)(2,1)S(1)} %get-tuple-element.82), channel_id=1, source_target_pairs={{0,16},{16,0},{1,17},{17,1},{2,18},{18,2},{3,19},{19,3},{4,20},{20... | collective-permute-start | bytes 491528 | tf_op jit(solution)/shard_map/ppermute | solution.py:422
  93.8 16.2 %collective-permute-start.9 = (bf16[32,40,128]{2,1,0:T(8,128)(2,1)S(1)}, bf16[32,40,128]{2,1,0:T(8,128)(2,1)S(1)}, u32[]{:S(2)}, u32[]{:S(2)}) collective-permute-start(bf16[32,40,128]{2,1,0:T(8,128)(2,1)S(1)} %get-tuple-element.57.here_ref), channel_id=1, source_target_pairs={{0,16},{16,0},{1,17},{17,1},{2,18},{18,2},{3,19},{19,3},{4,20},{20... | collective-permute-start | bytes 983048 | tf_op jit(solution)/shard_map/ppermute | solution.py:422
  115.2 38.5 %all-to-all-start.2 = ((bf16[8,2,640,128]{3,2,1,0:T(8,128)(2,1)}), bf16[8,2,640,128]{3,2,1,0:T(8,128)(2,1)S(1)}, u32[]{:S(2)}, u32[]{:S(2)}) async-start(bf16[8,2,640,128]{3,2,1,0:T(8,128)(2,1)} %get-tuple-element.60), calls=%async_computation.2 | async-start | bytes 5242880 | tf_op jit(solution)/shard_map/all_to_all | solution.py:417
  118.8 16.9 %collective-permute-start.11 = (bf16[2,32,40,128]{3,2,1,0:T(8,128)(2,1)}, bf16[2,32,40,128]{3,2,1,0:T(8,128)(2,1)S(1)}, u32[]{:S(2)}, u32[]{:S(2)}) collective-permute-start(bf16[2,32,40,128]{3,2,1,0:T(8,128)(2,1)} %get-tuple-element.61.refs_0_), channel_id=1, source_target_pairs={{0,64},{32,96},{64,0},{96,32},{1,65},{33,97},{65,1},{97,33},{2,66}... | collective-permute-start | bytes 1966088 | tf_op jit(solution)/shard_map/ppermute | solution.py:422
  120.2 31.1 %collective-permute-start.10 = (bf16[2,32,40,128]{3,2,1,0:T(8,128)(2,1)}, bf16[2,32,40,128]{3,2,1,0:T(8,128)(2,1)S(1)}, u32[]{:S(2)}, u32[]{:S(2)}) collective-permute-start(bf16[2,32,40,128]{3,2,1,0:T(8,128)(2,1)} %get-tuple-element.61.refs_0_), channel_id=1, source_target_pairs={{0,32},{32,64},{64,96},{96,0},{1,33},{33,65},{65,97},{97,1},{2,34}... | collective-permute-start | bytes 1966088 | tf_op jit(solution)/shard_map/ppermute | solution.py:422
  120.3 31.5 %collective-permute-start.12 = (bf16[2,32,40,128]{3,2,1,0:T(8,128)(2,1)}, bf16[2,32,40,128]{3,2,1,0:T(8,128)(2,1)}, u32[]{:S(2)}, u32[]{:S(2)}) collective-permute-start(bf16[2,32,40,128]{3,2,1,0:T(8,128)(2,1)} %get-tuple-element.61.refs_0_), channel_id=1, source_target_pairs={{0,96},{32,0},{64,32},{96,64},{1,97},{33,1},{65,33},{97,65},{2,98}... | collective-permute-start | bytes 1966088 | tf_op jit(solution)/shard_map/ppermute | solution.py:422
  122.9 29.0 %collective-permute-start.13 = (bf16[2,32,40,128]{3,2,1,0:T(8,128)(2,1)}, bf16[2,32,40,128]{3,2,1,0:T(8,128)(2,1)S(1)}, u32[]{:S(2)}, u32[]{:S(2)}) collective-permute-start(bf16[2,32,40,128]{3,2,1,0:T(8,128)(2,1)} %get-tuple-element.61.refs_0_), channel_id=1, source_target_pairs={{0,8},{8,0},{1,9},{9,1},{2,10},{10,2},{3,11},{11,3},{4,12},{12,4},... | collective-permute-start | bytes 1966088 | tf_op jit(solution)/shard_map/ppermute | solution.py:422
  135.7 16.2 %collective-permute-start.15 = (bf16[2,32,40,128]{3,2,1,0:T(8,128)(2,1)S(1)}, bf16[2,32,40,128]{3,2,1,0:T(8,128)(2,1)S(1)}, u32[]{:S(2)}, u32[]{:S(2)}) collective-permute-start(bf16[2,32,40,128]{3,2,1,0:T(8,128)(2,1)S(1)} %collective-permute-done.11.refs_1_.refs_2_), channel_id=1, source_target_pairs={{0,8},{8,0},{1,9},{9,1},{2,10},{10,2},{3,11},{11,3},{4,12},{12,4},... | collective-permute-start | bytes 1966088 | tf_op jit(solution)/shard_map/ppermute | solution.py:422
  151.3 2.4 %collective-permute-start.14 = (bf16[2,32,40,128]{3,2,1,0:T(8,128)(2,1)S(1)}, bf16[2,32,40,128]{3,2,1,0:T(8,128)(2,1)}, u32[]{:S(2)}, u32[]{:S(2)}) collective-permute-start(bf16[2,32,40,128]{3,2,1,0:T(8,128)(2,1)S(1)} %collective-permute-done.10.refs_0_.refs_1_), channel_id=1, source_target_pairs={{0,8},{8,0},{1,9},{9,1},{2,10},{10,2},{3,11},{11,3},{4,12},{12,4},... | collective-permute-start | bytes 1966088 | tf_op jit(solution)/shard_map/ppermute | solution.py:422
  151.8 7.5 %collective-permute-start.20 = (bf16[2,32,40,128]{3,2,1,0:T(8,128)(2,1)}, bf16[2,32,40,128]{3,2,1,0:T(8,128)(2,1)}, u32[]{:S(2)}, u32[]{:S(2)}) collective-permute-start(bf16[2,32,40,128]{3,2,1,0:T(8,128)(2,1)} %collective-permute-done.12.refs_2_.refs_3_), channel_id=1, source_target_pairs={{0,8},{8,0},{1,9},{9,1},{2,10},{10,2},{3,11},{11,3},{4,12},{12,4},... | collective-permute-start | bytes 1966088 | tf_op jit(solution)/shard_map/ppermute | solution.py:422
  154.3 8.4 %collective-permute-start.19 = (bf16[2,320,128]{2,1,0:T(8,128)(2,1)S(1)}, bf16[2,320,128]{2,1,0:T(8,128)(2,1)S(1)}, u32[]{:S(2)}, u32[]{:S(2)}) collective-permute-start(bf16[2,320,128]{2,1,0:T(8,128)(2,1)S(1)} %get-tuple-element.64), channel_id=1, source_target_pairs={{0,96},{32,0},{64,32},{96,64},{1,97},{33,1},{65,33},{97,65},{2,98}... | collective-permute-start | bytes 491528 | tf_op jit(solution)/shard_map/ppermute | solution.py:422
  155.2 7.5 %collective-permute-start.18 = (bf16[2,320,128]{2,1,0:T(8,128)(2,1)S(1)}, bf16[2,320,128]{2,1,0:T(8,128)(2,1)S(1)}, u32[]{:S(2)}, u32[]{:S(2)}) collective-permute-start(bf16[2,320,128]{2,1,0:T(8,128)(2,1)S(1)} %get-tuple-element.64), channel_id=1, source_target_pairs={{0,64},{32,96},{64,0},{96,32},{1,65},{33,97},{65,1},{97,33},{2,66}... | collective-permute-start | bytes 491528 | tf_op jit(solution)/shard_map/ppermute | solution.py:422
  156.4 9.9 %collective-permute-start.17 = (bf16[2,320,128]{2,1,0:T(8,128)(2,1)S(1)}, bf16[2,320,128]{2,1,0:T(8,128)(2,1)S(1)}, u32[]{:S(2)}, u32[]{:S(2)}) collective-permute-start(bf16[2,320,128]{2,1,0:T(8,128)(2,1)S(1)} %get-tuple-element.64), channel_id=1, source_target_pairs={{0,32},{32,64},{64,96},{96,0},{1,33},{33,65},{65,97},{97,1},{2,34}... | collective-permute-start | bytes 491528 | tf_op jit(solution)/shard_map/ppermute | solution.py:422
  156.7 6.0 %collective-permute-start.16 = (bf16[2,320,128]{2,1,0:T(8,128)(2,1)S(1)}, bf16[2,320,128]{2,1,0:T(8,128)(2,1)S(1)}, u32[]{:S(2)}, u32[]{:S(2)}) collective-permute-start(bf16[2,320,128]{2,1,0:T(8,128)(2,1)S(1)} %get-tuple-element.62), channel_id=1, source_target_pairs={{0,16},{16,0},{1,17},{17,1},{2,18},{18,2},{3,19},{19,3},{4,20},{20... | collective-permute-start | bytes 491528 | tf_op jit(solution)/shard_map/ppermute | solution.py:422
  166.4 19.7 %collective-permute-start.21 = (bf16[4,2,320,128]{3,2,1,0:T(8,128)(2,1)S(1)}, bf16[4,2,320,128]{3,2,1,0:T(8,128)(2,1)S(1)}, u32[]{:S(2)}, u32[]{:S(2)}) collective-permute-start(bf16[4,2,320,128]{3,2,1,0:T(8,128)(2,1)S(1)} %pad_maximum_fusion.refs_0_), channel_id=1, source_target_pairs={{0,16},{16,0},{1,17},{17,1},{2,18},{18,2},{3,19},{19,3},{4,20},{20... | collective-permute-start | bytes 1966088 | tf_op jit(solution)/shard_map/ppermute | solution.py:422
  167.8 8.5 %collective-permute-start.24 = (bf16[2,2,320,128]{3,2,1,0:T(8,128)(2,1)S(1)}, bf16[2,2,320,128]{3,2,1,0:T(8,128)(2,1)S(1)}, u32[]{:S(2)}, u32[]{:S(2)}) collective-permute-start(bf16[2,2,320,128]{3,2,1,0:T(8,128)(2,1)S(1)} %pad_maximum_fusion.1.refs_0_), channel_id=1, source_target_pairs={{0,96},{32,0},{64,32},{96,64},{1,97},{33,1},{65,33},{97,65},{2,98}... | collective-permute-start | bytes 983048 | tf_op jit(solution)/shard_map/ppermute | solution.py:422
  167.8 9.5 %collective-permute-start.23 = (bf16[2,2,320,128]{3,2,1,0:T(8,128)(2,1)S(1)}, bf16[2,2,320,128]{3,2,1,0:T(8,128)(2,1)S(1)}, u32[]{:S(2)}, u32[]{:S(2)}) collective-permute-start(bf16[2,2,320,128]{3,2,1,0:T(8,128)(2,1)S(1)} %pad_maximum_fusion.1.refs_0_), channel_id=1, source_target_pairs={{0,64},{32,96},{64,0},{96,32},{1,65},{33,97},{65,1},{97,33},{2,66}... | collective-permute-start | bytes 983048 | tf_op jit(solution)/shard_map/ppermute | solution.py:422
  168.6 17.4 %collective-permute-start.22 = (bf16[2,2,320,128]{3,2,1,0:T(8,128)(2,1)S(1)}, bf16[2,2,320,128]{3,2,1,0:T(8,128)(2,1)S(1)}, u32[]{:S(2)}, u32[]{:S(2)}) collective-permute-start(bf16[2,2,320,128]{3,2,1,0:T(8,128)(2,1)S(1)} %pad_maximum_fusion.1.refs_0_), channel_id=1, source_target_pairs={{0,32},{32,64},{64,96},{96,0},{1,33},{33,65},{65,97},{97,1},{2,34}... | collective-permute-start | bytes 983048 | tf_op jit(solution)/shard_map/ppermute | solution.py:422
  169.4 17.7 %collective-permute-start.29 = (bf16[4,2,320,128]{3,2,1,0:T(8,128)(2,1)S(1)}, bf16[4,2,320,128]{3,2,1,0:T(8,128)(2,1)S(1)}, u32[]{:S(2)}, u32[]{:S(2)}) collective-permute-start(bf16[4,2,320,128]{3,2,1,0:T(8,128)(2,1)S(1)} %pad_maximum_fusion.refs_0_), channel_id=1, source_target_pairs={{0,8},{8,0},{1,9},{9,1},{2,10},{10,2},{3,11},{11,3},{4,12},{12,4},... | collective-permute-start | bytes 1966088 | tf_op jit(solution)/shard_map/ppermute | solution.py:422
  186.1 2.2 %collective-permute-start.30 = (bf16[4,2,320,128]{3,2,1,0:T(8,128)(2,1)S(1)}, bf16[4,2,320,128]{3,2,1,0:T(8,128)(2,1)S(1)}, u32[]{:S(2)}, u32[]{:S(2)}) collective-permute-start(bf16[4,2,320,128]{3,2,1,0:T(8,128)(2,1)S(1)} %collective-permute-done.21.refs_1_), channel_id=1, source_target_pairs={{0,8},{8,0},{1,9},{9,1},{2,10},{10,2},{3,11},{11,3},{4,12},{12,4},... | collective-permute-start | bytes 1966088 | tf_op jit(solution)/shard_map/ppermute | solution.py:422
  186.6 3.8 %collective-permute-start.25 = (bf16[2,2,320,128]{3,2,1,0:T(8,128)(2,1)S(1)}, bf16[2,2,320,128]{3,2,1,0:T(8,128)(2,1)S(1)}, u32[]{:S(2)}, u32[]{:S(2)}) collective-permute-start(bf16[2,2,320,128]{3,2,1,0:T(8,128)(2,1)S(1)} %pad_maximum_fusion.1.refs_0_), channel_id=1, source_target_pairs={{0,8},{8,0},{1,9},{9,1},{2,10},{10,2},{3,11},{11,3},{4,12},{12,4},... | collective-permute-start | bytes 983048 | tf_op jit(solution)/shard_map/ppermute | solution.py:422
  186.6 3.7 %collective-permute-start.26 = (bf16[2,2,320,128]{3,2,1,0:T(8,128)(2,1)S(1)}, bf16[2,2,320,128]{3,2,1,0:T(8,128)(2,1)S(1)}, u32[]{:S(2)}, u32[]{:S(2)}) collective-permute-start(bf16[2,2,320,128]{3,2,1,0:T(8,128)(2,1)S(1)} %collective-permute-done.22.refs_1_), channel_id=1, source_target_pairs={{0,8},{8,0},{1,9},{9,1},{2,10},{10,2},{3,11},{11,3},{4,12},{12,4},... | collective-permute-start | bytes 983048 | tf_op jit(solution)/shard_map/ppermute | solution.py:422
  187.1 3.3 %collective-permute-start.27 = (bf16[2,2,320,128]{3,2,1,0:T(8,128)(2,1)S(1)}, bf16[2,2,320,128]{3,2,1,0:T(8,128)(2,1)S(1)}, u32[]{:S(2)}, u32[]{:S(2)}) collective-permute-start(bf16[2,2,320,128]{3,2,1,0:T(8,128)(2,1)S(1)} %collective-permute-done.23.refs_2_), channel_id=1, source_target_pairs={{0,8},{8,0},{1,9},{9,1},{2,10},{10,2},{3,11},{11,3},{4,12},{12,4},... | collective-permute-start | bytes 983048 | tf_op jit(solution)/shard_map/ppermute | solution.py:422
  187.1 3.2 %collective-permute-start.28 = (bf16[2,2,320,128]{3,2,1,0:T(8,128)(2,1)S(1)}, bf16[2,2,320,128]{3,2,1,0:T(8,128)(2,1)S(1)}, u32[]{:S(2)}, u32[]{:S(2)}) collective-permute-start(bf16[2,2,320,128]{3,2,1,0:T(8,128)(2,1)S(1)} %collective-permute-done.24.refs_3_), channel_id=1, source_target_pairs={{0,8},{8,0},{1,9},{9,1},{2,10},{10,2},{3,11},{11,3},{4,12},{12,4},... | collective-permute-start | bytes 983048 | tf_op jit(solution)/shard_map/ppermute | solution.py:422
  (10 other events, 200.8 us)

commit v6 on v4

--- a/solution.py
+++ b/solution.py
@@ -282,11 +282,11 @@
 
     def body(i, carry):
         field = dot(wi_ref[i], flat)
-        minus = kept(field, i * 64, onsets).astype(jnp.bfloat16)
+        minus = kept(field, i * 128, onsets).astype(jnp.bfloat16)
         acc[...] += dot(wf_ref[i], minus)
         return carry
 
-    lax.fori_loop(0, 4, body, 0)
+    lax.fori_loop(0, 2, body, 0)
     out_ref[...] = unlanes(acc[...]).astype(jnp.bfloat16).reshape(NF, 2, 40, 128)
 
 
@@ -300,8 +300,8 @@
 
 
 def middle(dev, parts, onsets):
-    wi = jnp.asarray(inverse_weights(64))
-    wf = jnp.asarray(forward_weights(64))
+    wi = jnp.asarray(inverse_weights(128))
+    wf = jnp.asarray(forward_weights(128))
     return pl.pallas_call(
         lambda d, *refs: middle_kernel(*refs),
         out_shape=(

time: 193 us -> 193 us (level)
  no operation moved by 1% of the time
where the time goes in v6:
time: 193 us; the launch traced here: 192 us
  waiting for transfers between devices  67.7 us (35%)
  blocking collectives  55.2 us (29%)
  starting transfers between devices  38.7 us (20%)
  Pallas kernels  23.2 us (12%)
  local copies, waits for them, and re-layouts  6.41 us (3%)
    ppermute x31, waiting for transfers between devices, along(): return lax.ppermute(x, axis, [(i, (i + step) % size) for i in range(size)])  67.7 us
    all_to_all x2, blocking collectives, exchange(): return lax.all_to_all(x, axes, 0, 0, tiled=True)  55.2 us
    ppermute x31, starting transfers between devices, along(): return lax.ppermute(x, axis, [(i, (i + step) % size) for i in range(size)])  35 us
    pallas_call x1, Pallas kernels, minus_product(): pl.pallas_call(minus_product_kernel, out_shape=[pltpu.HBM((8, 2, 640, 128...  5.11 us
    pallas_call x1, Pallas kernels, minus_output(): pl.pallas_call(minus_kernel, out_shape=jax.ShapeDtypeStruct((16, 640, 128...  5.07 us
    pallas_call x1, Pallas kernels, start_product(): pl.pallas_call(functools.partial(start_product_kernel, counts), out_shape...  4.22 us
    pallas_call x2, Pallas kernels, plus_output(): pl.pallas_call(functools.partial(plus_kernel, half), out_shape=jax.ShapeD...  4.12 us
  transfers between devices with their start and end apart: 32, of which 12 were waited for; matrix products, arithmetic and copies ran while one was open for 2% of the time, Pallas kernels for 4%

profile of v6, /device:TPU:1, one launch (start us, length us, event | category | flops | bytes accessed | tf_op | source)
XLA Modules:
  0.0 192.4 jit_solution(9336422020395102798)
XLA Ops:
  0.6 1.5 collective-permute-start
  3.1 3.8 %collective-permute-done.xo_ref = bf16[16,640,128]{2,1,0:T(8,128)(2,1)S(1)} collective-permute-done((bf16[16,640,128]{2,1,0:T(8,128)(2,1)}, bf16[16,640,128]{2,1,0:T(8,128)(2,1)S(1)}, u32[]{:S(2)}, u32[]{:S(2)}) %collective-permute-start) | collective-permute-done | bytes 2621472 | tf_op jit(solution)/shard_map/ppermute | solution.py:416
  6.9 1.7 copy-done
  10.3 2.9 %collective-permute-start.4 = (bf16[4,2,320,128]{3,2,1,0:T(8,128)(2,1)S(1)}, bf16[4,2,320,128]{3,2,1,0:T(8,128)(2,1)S(1)}, u32[]{:S(2)}, u32[]{:S(2)}) collective-permute-start(bf16[4,2,320,128]{3,2,1,0:T(8,128)(2,1)S(1)} %get-tuple-element.57), channel_id=1, source_target_pairs={{0,16},{16,0},{1,17},{17,1},{2,18},{18,2},{3,19},{19,3},{4,20},{20... | collective-permute-start | bytes 1966088 | tf_op jit(solution)/shard_map/ppermute | solution.py:416
  13.2 1.6 collective-permute-start.1
  14.9 3.3 %collective-permute-start.2 = (bf16[2,2,320,128]{3,2,1,0:T(8,128)(2,1)S(1)}, bf16[2,2,320,128]{3,2,1,0:T(8,128)(2,1)S(1)}, u32[]{:S(2)}, u32[]{:S(2)}) collective-permute-start(bf16[2,2,320,128]{3,2,1,0:T(8,128)(2,1)S(1)} %get-tuple-element.54), channel_id=1, source_target_pairs={{0,64},{32,96},{64,0},{96,32},{1,65},{33,97},{65,1},{97,33},{2,66}... | collective-permute-start | bytes 983048 | tf_op jit(solution)/shard_map/ppermute | solution.py:416
  18.9 5.5 %collective-permute-done.1 = bf16[2,2,320,128]{3,2,1,0:T(8,128)(2,1)S(1)} collective-permute-done((bf16[2,2,320,128]{3,2,1,0:T(8,128)(2,1)S(1)}, bf16[2,2,320,128]{3,2,1,0:T(8,128)(2,1)S(1)}, u32[]{:S(2)}, u32[]{:S(2)}) %collective-permute-start.1) | collective-permute-done | bytes 327712 | tf_op jit(solution)/shard_map/ppermute | solution.py:416
  24.4 7.9 %collective-permute-done.2 = bf16[2,2,320,128]{3,2,1,0:T(8,128)(2,1)S(1)} collective-permute-done((bf16[2,2,320,128]{3,2,1,0:T(8,128)(2,1)S(1)}, bf16[2,2,320,128]{3,2,1,0:T(8,128)(2,1)S(1)}, u32[]{:S(2)}, u32[]{:S(2)}) %collective-permute-start.2) | collective-permute-done | bytes 327712 | tf_op jit(solution)/shard_map/ppermute | solution.py:416
  32.5 2.9 %collective-permute-start.8 = (bf16[2,320,128]{2,1,0:T(8,128)(2,1)S(1)}, bf16[2,320,128]{2,1,0:T(8,128)(2,1)S(1)}, u32[]{:S(2)}, u32[]{:S(2)}) collective-permute-start(bf16[2,320,128]{2,1,0:T(8,128)(2,1)S(1)} %get-tuple-element.94), channel_id=1, source_target_pairs={{0,96},{32,0},{64,32},{96,64},{1,97},{33,1},{65,33},{97,65},{2,98}... | collective-permute-start | bytes 491528 | tf_op jit(solution)/shard_map/ppermute | solution.py:416
  36.6 5.6 %collective-permute-done.8.refs_5_ = bf16[2,320,128]{2,1,0:T(8,128)(2,1)S(1)} collective-permute-done((bf16[2,320,128]{2,1,0:T(8,128)(2,1)S(1)}, bf16[2,320,128]{2,1,0:T(8,128)(2,1)S(1)}, u32[]{:S(2)}, u32[]{:S(2)}) %collective-permute-start.8) | collective-permute-done | bytes 163872 | tf_op jit(solution)/shard_map/ppermute | solution.py:416
  42.1 4.4 %collective-permute-done.6.refs_3_ = bf16[2,320,128]{2,1,0:T(8,128)(2,1)S(1)} collective-permute-done((bf16[2,320,128]{2,1,0:T(8,128)(2,1)S(1)}, bf16[2,320,128]{2,1,0:T(8,128)(2,1)S(1)}, u32[]{:S(2)}, u32[]{:S(2)}) %collective-permute-start.6) | collective-permute-done | bytes 163872 | tf_op jit(solution)/shard_map/ppermute | solution.py:416
  46.5 4.2 %start_product.1 = bf16[128,2,40,128]{3,2,1,0:T(8,128)(2,1)S(1)} custom-call(bf16[2,320,128]{2,1,0:T(8,128)(2,1)S(1)} %get-tuple-element.99.refs_0_, bf16[2,320,128]{2,1,0:T(8,128)(2,1)S(1)} %collective-permute-done.5.refs_1_, bf16[2,320,128]{2,1,0:T(8,128)(2,1)S(1)} %get-tuple-element.97.refs_2_, bf16[2,320,128]{2,1,0:T(8,128)(2,1)S(1)} %collective-permute-done.6.refs_3_, ...), custom_call_target="tpu_custom_call" | custom-call | flops 4294967296 | bytes 18874368 | tf_op jit(solution)/shard_map/start_product/pallas_call | solution.py:174
  50.8 40.6 %all_to_all.15 = bf16[128,2,40,128]{3,2,1,0:T(8,128)(2,1)S(1)} all-to-all(bf16[128,2,40,128]{3,2,1,0:T(8,128)(2,1)S(1)} %start_product.1), channel_id=1, replica_groups=mesh['z'=4,'xh'=2,'core'=2,'y'=4,'xl'=2] {'y','xl','z','xh','core'}, dimensions={0} | all-to-all | bytes 5242880 | tf_op jit(solution)/shard_map/all_to_all | solution.py:411
  91.4 2.4 %middle.1 = (bf16[32,40,128]{2,1,0:T(8,128)(2,1)S(1)}, bf16[16,2,40,128]{3,2,1,0:T(8,128)(2,1)S(1)}) custom-call(s32[1]{0:T(128)} %bitcast.d.dev_ref, bf16[8,16,2,40,128]{4,3,2,1,0:T(8,128)(2,1)S(1)} %bitcast.29, s32[16,40,128]{2,1,0:T(8,128)S(1)} %bitcast.27, bf16[2,1024,256]{2,1,0:T(8,128)(2,1)S(1)} %copy-done.5, bf16[2,256,1024]{2,1,0:T(8,128)(2,1)S(1)} %copy-done.4), custom_call_target="tpu_custom_call" | custom-call | flops 2147483648 | bytes 8388608 | tf_op jit(solution)/shard_map/middle/pallas_call | solution.py:305
  93.8 1.6 collective-permute-start.9
  95.4 14.6 %all_to_all.16.s_ref = bf16[16,2,40,128]{3,2,1,0:T(8,128)(2,1)S(1)} all-to-all(bf16[16,2,40,128]{3,2,1,0:T(8,128)(2,1)S(1)} %get-tuple-element.64), channel_id=1, replica_groups=mesh['z'=4,'xh'=2,'core'=2,'y'=4,'xl'=2] {'z','xh','core'}, dimensions={0} | all-to-all | bytes 655360 | tf_op jit(solution)/shard_map/all_to_all | solution.py:411
  110.0 5.1 %minus_product.1 = (bf16[8,2,640,128]{3,2,1,0:T(8,128)(2,1)}, bf16[2,32,40,128]{3,2,1,0:T(8,128)(2,1)}) custom-call(bf16[16,2,40,128]{3,2,1,0:T(8,128)(2,1)S(1)} %all_to_all.16.s_ref, bf16[2,1,5120,640]{3,2,1,0:T(8,128)(2,1)S(1)} %copy-done.2, bf16[32,40,128]{2,1,0:T(8,128)(2,1)S(1)} %get-tuple-element.65.here_ref, ...), custom_call_target="tpu_custom_call" | custom-call | flops 4294967296 | bytes 18874368 | tf_op jit(solution)/shard_map/minus_product/pallas_call | solution.py:207
  115.2 3.6 %all-to-all-start.2 = ((bf16[8,2,640,128]{3,2,1,0:T(8,128)(2,1)}), bf16[8,2,640,128]{3,2,1,0:T(8,128)(2,1)S(1)}, u32[]{:S(2)}, u32[]{:S(2)}) async-start(bf16[8,2,640,128]{3,2,1,0:T(8,128)(2,1)} %get-tuple-element.68), calls=%async_computation.2 | async-start | bytes 5242880 | tf_op jit(solution)/shard_map/all_to_all | solution.py:411
  118.8 1.4 collective-permute-start.11
  120.3 1.5 collective-permute-start.13
  121.7 2.1 %collective-permute-start.12 = (bf16[2,32,40,128]{3,2,1,0:T(8,128)(2,1)}, bf16[2,32,40,128]{3,2,1,0:T(8,128)(2,1)S(1)}, u32[]{:S(2)}, u32[]{:S(2)}) collective-permute-start(bf16[2,32,40,128]{3,2,1,0:T(8,128)(2,1)} %get-tuple-element.79.refs_0_), channel_id=1, source_target_pairs={{0,96},{32,0},{64,32},{96,64},{1,97},{33,1},{65,33},{97,65},{2,98}... | collective-permute-start | bytes 1966088 | tf_op jit(solution)/shard_map/ppermute | solution.py:416
  123.8 11.8 %collective-permute-done.11.refs_2_ = bf16[2,32,40,128]{3,2,1,0:T(8,128)(2,1)S(1)} collective-permute-done((bf16[2,32,40,128]{3,2,1,0:T(8,128)(2,1)}, bf16[2,32,40,128]{3,2,1,0:T(8,128)(2,1)S(1)}, u32[]{:S(2)}, u32[]{:S(2)}) %collective-permute-start.11) | collective-permute-done | bytes 655392 | tf_op jit(solution)/shard_map/ppermute | solution.py:416
  135.7 3.8 %collective-permute-start.15 = (bf16[2,32,40,128]{3,2,1,0:T(8,128)(2,1)S(1)}, bf16[2,32,40,128]{3,2,1,0:T(8,128)(2,1)S(1)}, u32[]{:S(2)}, u32[]{:S(2)}) collective-permute-start(bf16[2,32,40,128]{3,2,1,0:T(8,128)(2,1)S(1)} %collective-permute-done.11.refs_2_), channel_id=1, source_target_pairs={{0,8},{8,0},{1,9},{9,1},{2,10},{10,2},{3,11},{11,3},{4,12},{12,4},... | collective-permute-start | bytes 1966088 | tf_op jit(solution)/shard_map/ppermute | solution.py:416
  139.5 11.8 %collective-permute-done.10.refs_1_ = bf16[2,32,40,128]{3,2,1,0:T(8,128)(2,1)S(1)} collective-permute-done((bf16[2,32,40,128]{3,2,1,0:T(8,128)(2,1)}, bf16[2,32,40,128]{3,2,1,0:T(8,128)(2,1)S(1)}, u32[]{:S(2)}, u32[]{:S(2)}) %collective-permute-start.10) | collective-permute-done | bytes 655392 | tf_op jit(solution)/shard_map/ppermute | solution.py:416
  155.2 1.3 collective-permute-start.18
  159.6 3.6 %collective-permute-done.16 = bf16[2,320,128]{2,1,0:T(8,128)(2,1)S(1)} collective-permute-done((bf16[2,320,128]{2,1,0:T(8,128)(2,1)S(1)}, bf16[2,320,128]{2,1,0:T(8,128)(2,1)S(1)}, u32[]{:S(2)}, u32[]{:S(2)}) %collective-permute-start.16) | collective-permute-done | bytes 163872 | tf_op jit(solution)/shard_map/ppermute | solution.py:416
  163.2 3.1 %collective-permute-done.17 = bf16[2,320,128]{2,1,0:T(8,128)(2,1)S(1)} collective-permute-done((bf16[2,320,128]{2,1,0:T(8,128)(2,1)S(1)}, bf16[2,320,128]{2,1,0:T(8,128)(2,1)S(1)}, u32[]{:S(2)}, u32[]{:S(2)}) %collective-permute-start.17) | collective-permute-done | bytes 163872 | tf_op jit(solution)/shard_map/ppermute | solution.py:416
  169.5 2.0 %collective-permute-start.29 = (bf16[4,2,320,128]{3,2,1,0:T(8,128)(2,1)S(1)}, bf16[4,2,320,128]{3,2,1,0:T(8,128)(2,1)S(1)}, u32[]{:S(2)}, u32[]{:S(2)}) collective-permute-start(bf16[4,2,320,128]{3,2,1,0:T(8,128)(2,1)S(1)} %pad_maximum_fusion.refs_0_), channel_id=1, source_target_pairs={{0,8},{8,0},{1,9},{9,1},{2,10},{10,2},{3,11},{11,3},{4,12},{12,4},... | collective-permute-start | bytes 1966088 | tf_op jit(solution)/shard_map/ppermute | solution.py:416
  171.5 5.1 %minus_output.1 = bf16[16,640,128]{2,1,0:T(8,128)(2,1)} custom-call(s32[1]{0:T(128)} %bitcast.d.dev_ref, bf16[2,32,40,128]{3,2,1,0:T(8,128)(2,1)} %get-tuple-element.79.refs_0_, bf16[2,32,40,128]{3,2,1,0:T(8,128)(2,1)} %copy-done.7, bf16[2,32,40,128]{3,2,1,0:T(8,128)(2,1)} %copy-done.6, bf16[2,32,40,128]{3,2,1,0:T(8,128)(2,1)} %copy-done.9, ...), custom_call_target="tpu_custom_call" | custom-call | flops 734003200 | bytes 8388608 | tf_op jit(solution)/shard_map/minus_output/pallas_call | solution.py:342
  177.1 8.9 %collective-permute-done.22.refs_1_ = bf16[2,2,320,128]{3,2,1,0:T(8,128)(2,1)S(1)} collective-permute-done((bf16[2,2,320,128]{3,2,1,0:T(8,128)(2,1)S(1)}, bf16[2,2,320,128]{3,2,1,0:T(8,128)(2,1)S(1)}, u32[]{:S(2)}, u32[]{:S(2)}) %collective-permute-start.22) | collective-permute-done | bytes 327712 | tf_op jit(solution)/shard_map/ppermute | solution.py:416
  188.3 2.0 %plus_output.2.refs_11_ = bf16[16,640,128]{2,1,0:T(8,128)(2,1)} custom-call(s32[1]{0:T(128)} %bitcast.d.dev_ref, bf16[4,2,320,128]{3,2,1,0:T(8,128)(2,1)S(1)} %pad_maximum_fusion.refs_0_, bf16[4,2,320,128]{3,2,1,0:T(8,128)(2,1)S(1)} %collective-permute-done.21.refs_1_, bf16[4,2,320,128]{3,2,1,0:T(8,128)(2,1)S(1)} %collective-permute-done.29.refs_2_, ...), custom_call_target="tpu_custom_call" | custom-call | flops 734003200 | bytes 6291456 | tf_op jit(solution)/shard_map/plus_output/pallas_call | solution.py:388
  190.3 2.1 %plus_output.3 = bf16[16,640,128]{2,1,0:T(8,128)(2,1)} custom-call(s32[1]{0:T(128)} %bitcast.d.dev_ref, bf16[2,2,320,128]{3,2,1,0:T(8,128)(2,1)S(1)} %pad_maximum_fusion.1.refs_0_, bf16[2,2,320,128]{3,2,1,0:T(8,128)(2,1)S(1)} %collective-permute-done.22.refs_1_, ...), custom_call_target="tpu_custom_call", output_to_operand_aliasing={{}: (12, {})} | custom-call | flops 734003200 | bytes 6291456 | tf_op jit(solution)/shard_map/plus_output/pallas_call | solution.py:388
  (74 shorter events, 17.7 us)
Async XLA Ops:
  0.6 6.2 %collective-permute-start = (bf16[16,640,128]{2,1,0:T(8,128)(2,1)}, bf16[16,640,128]{2,1,0:T(8,128)(2,1)S(1)}, u32[]{:S(2)}, u32[]{:S(2)}) collective-permute-start(bf16[16,640,128]{2,1,0:T(8,128)(2,1)} %refs_9_.1), channel_id=1, source_target_pairs={{0,8},{8,0},{1,9},{9,1},{2,10},{10,2},{3,11},{11,3},{4,12},{12,4},... | collective-permute-start | bytes 7864328 | tf_op jit(solution)/shard_map/ppermute | solution.py:416
  10.3 22.0 %collective-permute-start.4 = (bf16[4,2,320,128]{3,2,1,0:T(8,128)(2,1)S(1)}, bf16[4,2,320,128]{3,2,1,0:T(8,128)(2,1)S(1)}, u32[]{:S(2)}, u32[]{:S(2)}) collective-permute-start(bf16[4,2,320,128]{3,2,1,0:T(8,128)(2,1)S(1)} %get-tuple-element.57), channel_id=1, source_target_pairs={{0,16},{16,0},{1,17},{17,1},{2,18},{18,2},{3,19},{19,3},{4,20},{20... | collective-permute-start | bytes 1966088 | tf_op jit(solution)/shard_map/ppermute | solution.py:416
  13.2 11.2 %collective-permute-start.1 = (bf16[2,2,320,128]{3,2,1,0:T(8,128)(2,1)S(1)}, bf16[2,2,320,128]{3,2,1,0:T(8,128)(2,1)S(1)}, u32[]{:S(2)}, u32[]{:S(2)}) collective-permute-start(bf16[2,2,320,128]{3,2,1,0:T(8,128)(2,1)S(1)} %get-tuple-element.53), channel_id=1, source_target_pairs={{0,32},{32,64},{64,96},{96,0},{1,33},{33,65},{65,97},{97,1},{2,34}... | collective-permute-start | bytes 983048 | tf_op jit(solution)/shard_map/ppermute | solution.py:416
  14.9 17.5 %collective-permute-start.2 = (bf16[2,2,320,128]{3,2,1,0:T(8,128)(2,1)S(1)}, bf16[2,2,320,128]{3,2,1,0:T(8,128)(2,1)S(1)}, u32[]{:S(2)}, u32[]{:S(2)}) collective-permute-start(bf16[2,2,320,128]{3,2,1,0:T(8,128)(2,1)S(1)} %get-tuple-element.54), channel_id=1, source_target_pairs={{0,64},{32,96},{64,0},{96,32},{1,65},{33,97},{65,1},{97,33},{2,66}... | collective-permute-start | bytes 983048 | tf_op jit(solution)/shard_map/ppermute | solution.py:416
  18.2 14.2 %collective-permute-start.3 = (bf16[2,2,320,128]{3,2,1,0:T(8,128)(2,1)S(1)}, bf16[2,2,320,128]{3,2,1,0:T(8,128)(2,1)S(1)}, u32[]{:S(2)}, u32[]{:S(2)}) collective-permute-start(bf16[2,2,320,128]{3,2,1,0:T(8,128)(2,1)S(1)} %get-tuple-element.55), channel_id=1, source_target_pairs={{0,96},{32,0},{64,32},{96,64},{1,97},{33,1},{65,33},{97,65},{2,98}... | collective-permute-start | bytes 983048 | tf_op jit(solution)/shard_map/ppermute | solution.py:416
  32.5 9.6 %collective-permute-start.8 = (bf16[2,320,128]{2,1,0:T(8,128)(2,1)S(1)}, bf16[2,320,128]{2,1,0:T(8,128)(2,1)S(1)}, u32[]{:S(2)}, u32[]{:S(2)}) collective-permute-start(bf16[2,320,128]{2,1,0:T(8,128)(2,1)S(1)} %get-tuple-element.94), channel_id=1, source_target_pairs={{0,96},{32,0},{64,32},{96,64},{1,97},{33,1},{65,33},{97,65},{2,98}... | collective-permute-start | bytes 491528 | tf_op jit(solution)/shard_map/ppermute | solution.py:416
  35.4 6.7 %collective-permute-start.7 = (bf16[2,320,128]{2,1,0:T(8,128)(2,1)S(1)}, bf16[2,320,128]{2,1,0:T(8,128)(2,1)S(1)}, u32[]{:S(2)}, u32[]{:S(2)}) collective-permute-start(bf16[2,320,128]{2,1,0:T(8,128)(2,1)S(1)} %get-tuple-element.95), channel_id=1, source_target_pairs={{0,64},{32,96},{64,0},{96,32},{1,65},{33,97},{65,1},{97,33},{2,66}... | collective-permute-start | bytes 491528 | tf_op jit(solution)/shard_map/ppermute | solution.py:416
  35.8 10.8 %collective-permute-start.6 = (bf16[2,320,128]{2,1,0:T(8,128)(2,1)S(1)}, bf16[2,320,128]{2,1,0:T(8,128)(2,1)S(1)}, u32[]{:S(2)}, u32[]{:S(2)}) collective-permute-start(bf16[2,320,128]{2,1,0:T(8,128)(2,1)S(1)} %get-tuple-element.96), channel_id=1, source_target_pairs={{0,32},{32,64},{64,96},{96,0},{1,33},{33,65},{65,97},{97,1},{2,34}... | collective-permute-start | bytes 491528 | tf_op jit(solution)/shard_map/ppermute | solution.py:416
  36.2 10.3 %collective-permute-start.5 = (bf16[2,320,128]{2,1,0:T(8,128)(2,1)S(1)}, bf16[2,320,128]{2,1,0:T(8,128)(2,1)S(1)}, u32[]{:S(2)}, u32[]{:S(2)}) collective-permute-start(bf16[2,320,128]{2,1,0:T(8,128)(2,1)S(1)} %get-tuple-element.98), channel_id=1, source_target_pairs={{0,16},{16,0},{1,17},{17,1},{2,18},{18,2},{3,19},{19,3},{4,20},{20... | collective-permute-start | bytes 491528 | tf_op jit(solution)/shard_map/ppermute | solution.py:416
  93.8 16.2 %collective-permute-start.9 = (bf16[32,40,128]{2,1,0:T(8,128)(2,1)S(1)}, bf16[32,40,128]{2,1,0:T(8,128)(2,1)S(1)}, u32[]{:S(2)}, u32[]{:S(2)}) collective-permute-start(bf16[32,40,128]{2,1,0:T(8,128)(2,1)S(1)} %get-tuple-element.65.here_ref), channel_id=1, source_target_pairs={{0,16},{16,0},{1,17},{17,1},{2,18},{18,2},{3,19},{19,3},{4,20},{20... | collective-permute-start | bytes 983048 | tf_op jit(solution)/shard_map/ppermute | solution.py:416
  115.2 38.5 %all-to-all-start.2 = ((bf16[8,2,640,128]{3,2,1,0:T(8,128)(2,1)}), bf16[8,2,640,128]{3,2,1,0:T(8,128)(2,1)S(1)}, u32[]{:S(2)}, u32[]{:S(2)}) async-start(bf16[8,2,640,128]{3,2,1,0:T(8,128)(2,1)} %get-tuple-element.68), calls=%async_computation.2 | async-start | bytes 5242880 | tf_op jit(solution)/shard_map/all_to_all | solution.py:411
  118.8 16.9 %collective-permute-start.11 = (bf16[2,32,40,128]{3,2,1,0:T(8,128)(2,1)}, bf16[2,32,40,128]{3,2,1,0:T(8,128)(2,1)S(1)}, u32[]{:S(2)}, u32[]{:S(2)}) collective-permute-start(bf16[2,32,40,128]{3,2,1,0:T(8,128)(2,1)} %get-tuple-element.79.refs_0_), channel_id=1, source_target_pairs={{0,64},{32,96},{64,0},{96,32},{1,65},{33,97},{65,1},{97,33},{2,66}... | collective-permute-start | bytes 1966088 | tf_op jit(solution)/shard_map/ppermute | solution.py:416
  120.2 31.1 %collective-permute-start.10 = (bf16[2,32,40,128]{3,2,1,0:T(8,128)(2,1)}, bf16[2,32,40,128]{3,2,1,0:T(8,128)(2,1)S(1)}, u32[]{:S(2)}, u32[]{:S(2)}) collective-permute-start(bf16[2,32,40,128]{3,2,1,0:T(8,128)(2,1)} %get-tuple-element.79.refs_0_), channel_id=1, source_target_pairs={{0,32},{32,64},{64,96},{96,0},{1,33},{33,65},{65,97},{97,1},{2,34}... | collective-permute-start | bytes 1966088 | tf_op jit(solution)/shard_map/ppermute | solution.py:416
  120.3 31.5 %collective-permute-start.13 = (bf16[2,32,40,128]{3,2,1,0:T(8,128)(2,1)}, bf16[2,32,40,128]{3,2,1,0:T(8,128)(2,1)S(1)}, u32[]{:S(2)}, u32[]{:S(2)}) collective-permute-start(bf16[2,32,40,128]{3,2,1,0:T(8,128)(2,1)} %get-tuple-element.79.refs_0_), channel_id=1, source_target_pairs={{0,8},{8,0},{1,9},{9,1},{2,10},{10,2},{3,11},{11,3},{4,12},{12,4},... | collective-permute-start | bytes 1966088 | tf_op jit(solution)/shard_map/ppermute | solution.py:416
  121.7 30.0 %collective-permute-start.12 = (bf16[2,32,40,128]{3,2,1,0:T(8,128)(2,1)}, bf16[2,32,40,128]{3,2,1,0:T(8,128)(2,1)S(1)}, u32[]{:S(2)}, u32[]{:S(2)}) collective-permute-start(bf16[2,32,40,128]{3,2,1,0:T(8,128)(2,1)} %get-tuple-element.79.refs_0_), channel_id=1, source_target_pairs={{0,96},{32,0},{64,32},{96,64},{1,97},{33,1},{65,33},{97,65},{2,98}... | collective-permute-start | bytes 1966088 | tf_op jit(solution)/shard_map/ppermute | solution.py:416
  135.7 16.1 %collective-permute-start.15 = (bf16[2,32,40,128]{3,2,1,0:T(8,128)(2,1)S(1)}, bf16[2,32,40,128]{3,2,1,0:T(8,128)(2,1)S(1)}, u32[]{:S(2)}, u32[]{:S(2)}) collective-permute-start(bf16[2,32,40,128]{3,2,1,0:T(8,128)(2,1)S(1)} %collective-permute-done.11.refs_2_), channel_id=1, source_target_pairs={{0,8},{8,0},{1,9},{9,1},{2,10},{10,2},{3,11},{11,3},{4,12},{12,4},... | collective-permute-start | bytes 1966088 | tf_op jit(solution)/shard_map/ppermute | solution.py:416
  151.3 2.4 %collective-permute-start.14 = (bf16[2,32,40,128]{3,2,1,0:T(8,128)(2,1)S(1)}, bf16[2,32,40,128]{3,2,1,0:T(8,128)(2,1)}, u32[]{:S(2)}, u32[]{:S(2)}) collective-permute-start(bf16[2,32,40,128]{3,2,1,0:T(8,128)(2,1)S(1)} %collective-permute-done.10.refs_1_), channel_id=1, source_target_pairs={{0,8},{8,0},{1,9},{9,1},{2,10},{10,2},{3,11},{11,3},{4,12},{12,4},... | collective-permute-start | bytes 1966088 | tf_op jit(solution)/shard_map/ppermute | solution.py:416
  153.7 12.6 %collective-permute-start.20 = (bf16[2,32,40,128]{3,2,1,0:T(8,128)(2,1)}, bf16[2,32,40,128]{3,2,1,0:T(8,128)(2,1)S(1)}, u32[]{:S(2)}, u32[]{:S(2)}) collective-permute-start(bf16[2,32,40,128]{3,2,1,0:T(8,128)(2,1)} %copy-done.9), channel_id=1, source_target_pairs={{0,8},{8,0},{1,9},{9,1},{2,10},{10,2},{3,11},{11,3},{4,12},{12,4},... | collective-permute-start | bytes 1966088 | tf_op jit(solution)/shard_map/ppermute | solution.py:416
  154.6 8.6 %collective-permute-start.19 = (bf16[2,320,128]{2,1,0:T(8,128)(2,1)S(1)}, bf16[2,320,128]{2,1,0:T(8,128)(2,1)S(1)}, u32[]{:S(2)}, u32[]{:S(2)}) collective-permute-start(bf16[2,320,128]{2,1,0:T(8,128)(2,1)S(1)} %get-tuple-element.74), channel_id=1, source_target_pairs={{0,96},{32,0},{64,32},{96,64},{1,97},{33,1},{65,33},{97,65},{2,98}... | collective-permute-start | bytes 491528 | tf_op jit(solution)/shard_map/ppermute | solution.py:416
  155.2 8.1 %collective-permute-start.18 = (bf16[2,320,128]{2,1,0:T(8,128)(2,1)S(1)}, bf16[2,320,128]{2,1,0:T(8,128)(2,1)S(1)}, u32[]{:S(2)}, u32[]{:S(2)}) collective-permute-start(bf16[2,320,128]{2,1,0:T(8,128)(2,1)S(1)} %get-tuple-element.74), channel_id=1, source_target_pairs={{0,64},{32,96},{64,0},{96,32},{1,65},{33,97},{65,1},{97,33},{2,66}... | collective-permute-start | bytes 491528 | tf_op jit(solution)/shard_map/ppermute | solution.py:416
  156.5 9.8 %collective-permute-start.17 = (bf16[2,320,128]{2,1,0:T(8,128)(2,1)S(1)}, bf16[2,320,128]{2,1,0:T(8,128)(2,1)S(1)}, u32[]{:S(2)}, u32[]{:S(2)}) collective-permute-start(bf16[2,320,128]{2,1,0:T(8,128)(2,1)S(1)} %get-tuple-element.74), channel_id=1, source_target_pairs={{0,32},{32,64},{64,96},{96,0},{1,33},{33,65},{65,97},{97,1},{2,34}... | collective-permute-start | bytes 491528 | tf_op jit(solution)/shard_map/ppermute | solution.py:416
  157.0 6.2 %collective-permute-start.16 = (bf16[2,320,128]{2,1,0:T(8,128)(2,1)S(1)}, bf16[2,320,128]{2,1,0:T(8,128)(2,1)S(1)}, u32[]{:S(2)}, u32[]{:S(2)}) collective-permute-start(bf16[2,320,128]{2,1,0:T(8,128)(2,1)S(1)} %get-tuple-element.71), channel_id=1, source_target_pairs={{0,16},{16,0},{1,17},{17,1},{2,18},{18,2},{3,19},{19,3},{4,20},{20... | collective-permute-start | bytes 491528 | tf_op jit(solution)/shard_map/ppermute | solution.py:416
  166.4 19.7 %collective-permute-start.21 = (bf16[4,2,320,128]{3,2,1,0:T(8,128)(2,1)S(1)}, bf16[4,2,320,128]{3,2,1,0:T(8,128)(2,1)S(1)}, u32[]{:S(2)}, u32[]{:S(2)}) collective-permute-start(bf16[4,2,320,128]{3,2,1,0:T(8,128)(2,1)S(1)} %pad_maximum_fusion.refs_0_), channel_id=1, source_target_pairs={{0,16},{16,0},{1,17},{17,1},{2,18},{18,2},{3,19},{19,3},{4,20},{20... | collective-permute-start | bytes 1966088 | tf_op jit(solution)/shard_map/ppermute | solution.py:416
  167.7 8.9 %collective-permute-start.24 = (bf16[2,2,320,128]{3,2,1,0:T(8,128)(2,1)S(1)}, bf16[2,2,320,128]{3,2,1,0:T(8,128)(2,1)S(1)}, u32[]{:S(2)}, u32[]{:S(2)}) collective-permute-start(bf16[2,2,320,128]{3,2,1,0:T(8,128)(2,1)S(1)} %pad_maximum_fusion.1.refs_0_), channel_id=1, source_target_pairs={{0,96},{32,0},{64,32},{96,64},{1,97},{33,1},{65,33},{97,65},{2,98}... | collective-permute-start | bytes 983048 | tf_op jit(solution)/shard_map/ppermute | solution.py:416
  167.9 9.2 %collective-permute-start.23 = (bf16[2,2,320,128]{3,2,1,0:T(8,128)(2,1)S(1)}, bf16[2,2,320,128]{3,2,1,0:T(8,128)(2,1)S(1)}, u32[]{:S(2)}, u32[]{:S(2)}) collective-permute-start(bf16[2,2,320,128]{3,2,1,0:T(8,128)(2,1)S(1)} %pad_maximum_fusion.1.refs_0_), channel_id=1, source_target_pairs={{0,64},{32,96},{64,0},{96,32},{1,65},{33,97},{65,1},{97,33},{2,66}... | collective-permute-start | bytes 983048 | tf_op jit(solution)/shard_map/ppermute | solution.py:416
  168.8 17.3 %collective-permute-start.22 = (bf16[2,2,320,128]{3,2,1,0:T(8,128)(2,1)S(1)}, bf16[2,2,320,128]{3,2,1,0:T(8,128)(2,1)S(1)}, u32[]{:S(2)}, u32[]{:S(2)}) collective-permute-start(bf16[2,2,320,128]{3,2,1,0:T(8,128)(2,1)S(1)} %pad_maximum_fusion.1.refs_0_), channel_id=1, source_target_pairs={{0,32},{32,64},{64,96},{96,0},{1,33},{33,65},{65,97},{97,1},{2,34}... | collective-permute-start | bytes 983048 | tf_op jit(solution)/shard_map/ppermute | solution.py:416
  169.5 17.6 %collective-permute-start.29 = (bf16[4,2,320,128]{3,2,1,0:T(8,128)(2,1)S(1)}, bf16[4,2,320,128]{3,2,1,0:T(8,128)(2,1)S(1)}, u32[]{:S(2)}, u32[]{:S(2)}) collective-permute-start(bf16[4,2,320,128]{3,2,1,0:T(8,128)(2,1)S(1)} %pad_maximum_fusion.refs_0_), channel_id=1, source_target_pairs={{0,8},{8,0},{1,9},{9,1},{2,10},{10,2},{3,11},{11,3},{4,12},{12,4},... | collective-permute-start | bytes 1966088 | tf_op jit(solution)/shard_map/ppermute | solution.py:416
  186.1 2.2 %collective-permute-start.30 = (bf16[4,2,320,128]{3,2,1,0:T(8,128)(2,1)S(1)}, bf16[4,2,320,128]{3,2,1,0:T(8,128)(2,1)S(1)}, u32[]{:S(2)}, u32[]{:S(2)}) collective-permute-start(bf16[4,2,320,128]{3,2,1,0:T(8,128)(2,1)S(1)} %collective-permute-done.21.refs_1_), channel_id=1, source_target_pairs={{0,8},{8,0},{1,9},{9,1},{2,10},{10,2},{3,11},{11,3},{4,12},{12,4},... | collective-permute-start | bytes 1966088 | tf_op jit(solution)/shard_map/ppermute | solution.py:416
  186.6 3.8 %collective-permute-start.25 = (bf16[2,2,320,128]{3,2,1,0:T(8,128)(2,1)S(1)}, bf16[2,2,320,128]{3,2,1,0:T(8,128)(2,1)S(1)}, u32[]{:S(2)}, u32[]{:S(2)}) collective-permute-start(bf16[2,2,320,128]{3,2,1,0:T(8,128)(2,1)S(1)} %pad_maximum_fusion.1.refs_0_), channel_id=1, source_target_pairs={{0,8},{8,0},{1,9},{9,1},{2,10},{10,2},{3,11},{11,3},{4,12},{12,4},... | collective-permute-start | bytes 983048 | tf_op jit(solution)/shard_map/ppermute | solution.py:416
  186.6 3.7 %collective-permute-start.26 = (bf16[2,2,320,128]{3,2,1,0:T(8,128)(2,1)S(1)}, bf16[2,2,320,128]{3,2,1,0:T(8,128)(2,1)S(1)}, u32[]{:S(2)}, u32[]{:S(2)}) collective-permute-start(bf16[2,2,320,128]{3,2,1,0:T(8,128)(2,1)S(1)} %collective-permute-done.22.refs_1_), channel_id=1, source_target_pairs={{0,8},{8,0},{1,9},{9,1},{2,10},{10,2},{3,11},{11,3},{4,12},{12,4},... | collective-permute-start | bytes 983048 | tf_op jit(solution)/shard_map/ppermute | solution.py:416
  187.1 3.3 %collective-permute-start.27 = (bf16[2,2,320,128]{3,2,1,0:T(8,128)(2,1)S(1)}, bf16[2,2,320,128]{3,2,1,0:T(8,128)(2,1)S(1)}, u32[]{:S(2)}, u32[]{:S(2)}) collective-permute-start(bf16[2,2,320,128]{3,2,1,0:T(8,128)(2,1)S(1)} %collective-permute-done.23.refs_2_), channel_id=1, source_target_pairs={{0,8},{8,0},{1,9},{9,1},{2,10},{10,2},{3,11},{11,3},{4,12},{12,4},... | collective-permute-start | bytes 983048 | tf_op jit(solution)/shard_map/ppermute | solution.py:416
  187.1 3.2 %collective-permute-start.28 = (bf16[2,2,320,128]{3,2,1,0:T(8,128)(2,1)S(1)}, bf16[2,2,320,128]{3,2,1,0:T(8,128)(2,1)S(1)}, u32[]{:S(2)}, u32[]{:S(2)}) collective-permute-start(bf16[2,2,320,128]{3,2,1,0:T(8,128)(2,1)S(1)} %collective-permute-done.24.refs_3_), channel_id=1, source_target_pairs={{0,8},{8,0},{1,9},{9,1},{2,10},{10,2},{3,11},{11,3},{4,12},{12,4},... | collective-permute-start | bytes 983048 | tf_op jit(solution)/shard_map/ppermute | solution.py:416
  (12 other events, 207.0 us)
